TPU v7x, 32 devices: a whole 2x2x4 slice. The times are simulated.
32 devices in a mesh: grp: 2 (over x), lat: 8 (over z, y), chan: 2 (over core).
Axes of the slice: x: 2, y: 2, z: 4, core: 2. Of those that a mesh axis runs over, the one named last changes fastest.
Arguments:
- state_in: bfloat16 [32, 1440, 512], P(('grp', 'lat'), None, 'chan'), parts along dimension 0, may hold values from -6 to 6
- basis_blocks: bfloat16 [16, 5, 80, 3, 4, 80], P('lat'), may hold values from -0.1875 to 0.1875
- block_start: int32 [16, 3], P('lat'), may hold values from 0 to 17
- block_count: int32 [16, 3], P('lat'), may hold values from 1 to 4, as said below
- mix_weight: bfloat16 [5, 512, 512], P(None, 'chan'), may hold values from -0.125 to 0.125
- up_weight: bfloat16 [512, 1024], P(None, 'chan'), may hold values from -0.25 to 0.25
- down_weight: bfloat16 [1024, 512], P('chan'), may hold values from -0.1875 to 0.1875
Outputs:
- state_out: bfloat16 [32, 1440, 512], P(('grp', 'lat'), None, 'chan'), parts along dimension 0
There are 2 independent parts, one for each index of `grp`. A program takes and returns all parts, laid end to end along the dimension named above; an argument that names none is the same for every part. Nothing has to cross between parts.
Inputs may be any that keep to these rules, and one draw needn't show every extreme that they name: `block_count`: the count of row i and tap t is min(4, 1 + 3 * (16 - i) * (16 - i) // 256 + e), e being 0 or 1 drawn for each row and tap.
All inputs are finite; a program needn't handle non-finite values.
Results may differ from a plain program's by a relative error of at most 0.0049.
Values may be sent and summed in bfloat16 or wider, within the bound.
No kernel may reach another device: no remote copies, remote signals or barrier semaphores. Data moves between devices by JAX's collectives and lax.ppermute only.
A program may use at most 128 MiB of HBM per device.

v0:
```python
import jax
import jax.numpy as jnp
from jax import lax
from jax.sharding import PartitionSpec as P


def with_halo(cells, sides, width):
    for axis, dim in sides:
        count = lax.axis_size(axis)
        ends = count - 1
        head = lax.slice_in_dim(cells, 0, width, axis=dim)
        tail = lax.slice_in_dim(cells, cells.shape[dim] - width, cells.shape[dim], axis=dim)
        cells = jnp.concatenate(
            [
                lax.ppermute(tail, axis, [(i, (i + 1) % count) for i in range(ends)]),
                cells,
                lax.ppermute(head, axis, [((i + 1) % count, i) for i in range(ends)]),
            ],
            axis=dim,
        )
    return cells


def shifted(block_rows, amount):
    return jnp.roll(block_rows, -amount, axis=0)


def conv_rows(padded, basis_blocks, block_start, block_count):
    local_rows = basis_blocks.shape[0]
    basis_count = basis_blocks.shape[1]
    block_width = basis_blocks.shape[2]
    block_most = basis_blocks.shape[4]
    lon_cells = padded.shape[1]
    channels = padded.shape[2]
    lon_blocks = lon_cells // block_width

    def one_row(row_index):
        window = lax.dynamic_slice_in_dim(padded, row_index, 3, 0).reshape(
            3, lon_blocks, block_width, channels
        )
        filters_row = basis_blocks[row_index]
        counts_row = block_count[row_index]
        starts_row = block_start[row_index]
        pieces = []
        for lat_tap in range(3):
            for block_index in range(block_most):
                pieces.append(shifted(window[lat_tap], starts_row[lat_tap] + block_index))
        stacked = jnp.stack(pieces, 1).reshape(lon_blocks, 3 * block_most * block_width, channels)
        keep = jnp.arange(block_most, dtype=jnp.int32)[None, :] < counts_row[:, None]
        weights = jnp.where(keep[None, None, :, :, None], filters_row, 0)
        weights = weights.reshape(basis_count, block_width, 3 * block_most * block_width)
        result = jnp.einsum("kaz,qzc->kqac", weights, stacked, preferred_element_type=jnp.float32)
        return result.reshape(basis_count, lon_cells, channels).astype(jnp.bfloat16)

    return lax.map(one_row, jnp.arange(local_rows, dtype=jnp.int32))


def feed_forward(cells, up_matrix, down_matrix):
    flat = cells.reshape(-1, cells.shape[2])
    hidden = jax.nn.gelu(
        jnp.dot(flat, up_matrix, preferred_element_type=jnp.float32), approximate=False
    ).astype(jnp.bfloat16)
    output = jnp.dot(hidden, down_matrix, preferred_element_type=jnp.float32)
    return output.reshape(cells.shape[0], cells.shape[1], down_matrix.shape[1])


def per_device(
    state_in, basis_blocks, block_start, block_count, mix_weight, up_weight, down_weight
):
    padded = with_halo(state_in, (("lat", 0),), 1)
    conv = conv_rows(padded, basis_blocks, block_start, block_count)
    partial_mix = jnp.einsum("rkjc,kco->rjo", conv, mix_weight, preferred_element_type=jnp.float32)
    mixed = lax.psum_scatter(partial_mix, "chan", scatter_dimension=2, tiled=True)
    state = state_in.astype(jnp.float32) + mixed
    rounded = state.astype(jnp.bfloat16)
    whole_state = lax.all_gather(rounded, "chan", axis=2, tiled=True)
    feed = lax.psum_scatter(
        feed_forward(whole_state, up_weight, down_weight), "chan", scatter_dimension=2, tiled=True
    )
    return (state + feed).astype(jnp.bfloat16)


def solution(mesh):
    placed = (
        P(("grp", "lat"), None, "chan"),
        P("lat", None, None, None, None, None),
        P("lat", None),
        P("lat", None),
        P(None, "chan", None),
        P(None, "chan"),
        P("chan", None),
    )
    return jax.shard_map(
        per_device,
        mesh=mesh,
        in_specs=placed,
        out_specs=P(("grp", "lat"), None, "chan"),
        check_vma=False,
    )
```

profile of v0, /device:TPU:0, one launch (start us, length us, event | category | flops | bytes accessed | tf_op | source)
XLA Modules:
  0.0 220.4 jit_solution(11964246259637886609)
XLA Ops:
  6.5 1.5 fusion.82
  8.1 4.9 %collective-permute-start = (bf16[1,1440,256]{2,1,0:T(8,128)(2,1)S(1)}, bf16[1,1440,256]{2,1,0:T(8,128)(2,1)S(1)}, u32[]{:S(2)}, u32[]{:S(2)}) collective-permute-start(bf16[1,1440,256]{2,1,0:T(8,128)(2,1)S(1)} %get-tuple-element.116), channel_id=1, source_target_pairs={{0,2},{2,4},{4,6},{6,8},{8,10},{10,12},{12,14},{1,3},{3,5},{5,7},{... | collective-permute-start | bytes 2211848 | tf_op jit(solution)/shard_map/ppermute | solution.py:15
  14.3 30.2 %collective-permute-done = bf16[1,1440,256]{2,1,0:T(8,128)(2,1)S(1)} collective-permute-done((bf16[1,1440,256]{2,1,0:T(8,128)(2,1)S(1)}, bf16[1,1440,256]{2,1,0:T(8,128)(2,1)S(1)}, u32[]{:S(2)}, u32[]{:S(2)}) %collective-permute-start) | collective-permute-done | bytes 737312 | tf_op jit(solution)/shard_map/ppermute | solution.py:15
  44.5 3.6 %pad_maximum_fusion = bf16[4,1440,256]{2,1,0:T(8,128)(2,1)} fusion(bf16[1,1440,256]{2,1,0:T(8,128)(2,1)} %collective-permute-done.1, bf16[2,1440,256]{2,1,0:T(8,128)(2,1)} %param.11, bf16[1,1440,256]{2,1,0:T(8,128)(2,1)S(1)} %collective-permute-done), kind=kLoop, calls=%fused_computation.90 | loop fusion | flops 2949120 | bytes 5898240 | tf_op jit(solution)/shard_map/concatenate | solution.py:13
  48.1 87.0 %while.12 = (s32[]{:T(128)}, bf16[2,5,1440,256]{3,2,1,0:T(8,128)(2,1)}, s32[2]{0:T(128)S(1)}, bf16[4,1440,256]{2,1,0:T(8,128)(2,1)}, s32[2,3]{1,0:T(2,128)S(1)},...) while((s32[]{:T(128)}, ...), condition=%wide.region_1.3_spmd, body=%wide.region_0.2_spmd.sunk | while | flops 3558866176 | bytes 53240152 | solution.py:55
  53.1 1.7 constant_dynamic-slice_fusion.8
  58.7 1.4 fusion.112
  78.0 1.8 dynamic-slice_select_fusion.2
  79.9 1.7 reshape.113
  81.5 7.6 %convert_bitcast_fusion.2 = bf16[5,18,80,256]{3,2,0,1:T(8,128)(2,1)S(1)} fusion(bf16[18,960,256,1]{2,1,3,0:T(8,128)(2,1)} %bitcast.170, bf16[5,80,960,1]{2,1,0,3:T(8,128)(2,1)} %reshape.113), kind=kOutput, calls=%fused_computation.clone.1 | convolution fusion | flops 3540787200 | bytes 13301760 | tf_op jit(solution)/shard_map/while/body/eval_jaxpr/kaz,qzc->kqac/dot_general | solution.py:52
  89.5 2.1 constant_dynamic-update-slice_fusion.2
  96.6 1.7 constant_dynamic-slice_fusion.8
  100.3 1.4 fusion.111
  121.5 1.8 dynamic-slice_select_fusion.2
  123.4 1.7 reshape.113
  125.0 7.6 %convert_bitcast_fusion.2 = bf16[5,18,80,256]{3,2,0,1:T(8,128)(2,1)S(1)} fusion(bf16[18,960,256,1]{2,1,3,0:T(8,128)(2,1)} %bitcast.170, bf16[5,80,960,1]{2,1,0,3:T(8,128)(2,1)} %reshape.113), kind=kOutput, calls=%fused_computation.clone.1 | convolution fusion | flops 3540787200 | bytes 13301760 | tf_op jit(solution)/shard_map/while/body/eval_jaxpr/kaz,qzc->kqac/dot_general | solution.py:52
  133.0 2.1 constant_dynamic-update-slice_fusion.2
  135.1 9.0 %convolution_bitcast_fusion = f32[2,1440,512]{2,1,0:T(8,128)} fusion(bf16[2,5,1440,256]{3,2,1,0:T(8,128)(2,1)} %get-tuple-element.95, bf16[5,256,512]{2,1,0:T(8,128)(2,1)S(1)} %copy-done), kind=kOutput, calls=%fused_computation.89 | convolution fusion | flops 3774873600 | bytes 14581760 | tf_op jit(solution)/shard_map/rkjc,kco->rjo/dot_general | solution.py:72
  144.1 16.3 %reduce-scatter.3.cloned.1.call-done = f32[2,1440,256]{2,1,0:T(8,128)} async-done(((f32[2,1440,512]{2,1,0:T(8,128)}), f32[2,1440,256]{2,1,0:T(8,128)}) %reduce-scatter.3.cloned.1.call-update) | async-done | bytes 2949136 | tf_op jit(solution)/shard_map/reduce_scatter | solution.py:73
  160.4 3.3 %fusion.49 = bf16[2,1440,256]{2,1,0:T(8,128)(2,1)} fusion(f32[2,1440,256]{2,1,0:T(8,128)} %reduce-scatter.3.cloned.1.call-done, bf16[2,1440,256]{2,1,0:T(8,128)(2,1)S(1)} %copy-done.1), kind=kLoop, calls=%fused_computation.94 | loop fusion | flops 2211840 | bytes 5898240 | tf_op jit(solution)/shard_map/convert_element_type | solution.py:75
  163.8 12.8 %all-gather.2.cloned.1.call-done = bf16[2,1440,512]{2,1,0:T(8,128)(2,1)} async-done(((bf16[2,1440,256]{2,1,0:T(8,128)(2,1)}), bf16[2,1440,512]{2,1,0:T(8,128)(2,1)}) %all-gather.2.cloned.1.call-update) | async-done | bytes 2949136 | tf_op jit(solution)/shard_map/all_gather | solution.py:76
  176.5 17.7 %fusion.47 = f32[2880,512]{1,0:T(8,128)} fusion(bf16[512,512]{1,0:T(8,128)(2,1)S(1)} %copy-done.2, bf16[2880,512]{1,0:T(8,128)(2,1)} %bitcast.171, bf16[512,512]{1,0:T(8,128)(2,1)} %param.16), kind=kOutput, calls=%fused_computation.93 | convolution fusion | flops 3115745280 | bytes 9895936 | tf_op jit(solution)/shard_map/dot_general | solution.py:63
  194.2 15.3 %reduce-scatter.5.cloned.1.call-done = f32[2,1440,256]{2,1,0:T(8,128)} async-done(((f32[2,1440,512]{2,1,0:T(8,128)}), f32[2,1440,256]{2,1,0:T(8,128)}) %reduce-scatter.5.cloned.1.call-update) | async-done | bytes 2949136 | tf_op jit(solution)/shard_map/reduce_scatter | solution.py:77
  209.5 4.4 %add_convert_fusion = bf16[2,1440,256]{2,1,0:T(8,128)(2,1)} fusion(f32[2,1440,256]{2,1,0:T(8,128)} %reduce-scatter.5.cloned.1.call-done, f32[2,1440,256]{2,1,0:T(8,128)} %reduce-scatter.3.cloned.1.call-done, bf16[2,1440,256]{2,1,0:T(8,128)(2,1)S(1)} %copy-done.1), kind=kLoop, calls=%fused_computation.91 | loop fusion | flops 2949120 | bytes 8847360 | tf_op jit(solution)/shard_map/convert_element_type | solution.py:80
  (54 shorter events, 33.9 us)
Async XLA Ops:
  6.5 128.5 %copy-start = (bf16[5,256,512]{2,1,0:T(8,128)(2,1)S(1)}, bf16[5,256,512]{2,1,0:T(8,128)(2,1)}, u32[]{:S(2)}) copy-start(bf16[5,256,512]{2,1,0:T(8,128)(2,1)} %param.15) | copy-start | bytes 3932164
  6.5 41.5 %copy-start.3 = (s32[2,3]{1,0:T(2,128)S(1)}, s32[2,3]{1,0:T(2,128)}, u32[]{:S(2)}) copy-start(s32[2,3]{1,0:T(2,128)} %param.13) | copy-start | bytes 76
  6.5 41.5 %copy-start.4 = (s32[2,3]{1,0:T(2,128)S(1)}, s32[2,3]{1,0:T(2,128)}, u32[]{:S(2)}) copy-start(s32[2,3]{1,0:T(2,128)} %param.14) | copy-start | bytes 76
  6.5 153.9 %reduce-scatter.3.cloned.1.call-start = ((), (), s32[]{:S(2)}) async-start(), calls=%async_computation.2 | async-start | bytes 8847360 | tf_op jit(solution)/shard_map/reduce_scatter | solution.py:73
  8.1 36.4 %collective-permute-start = (bf16[1,1440,256]{2,1,0:T(8,128)(2,1)S(1)}, bf16[1,1440,256]{2,1,0:T(8,128)(2,1)S(1)}, u32[]{:S(2)}, u32[]{:S(2)}) collective-permute-start(bf16[1,1440,256]{2,1,0:T(8,128)(2,1)S(1)} %get-tuple-element.116), channel_id=1, source_target_pairs={{0,2},{2,4},{4,6},{6,8},{8,10},{10,12},{12,14},{1,3},{3,5},{5,7},{... | collective-permute-start | bytes 2211848 | tf_op jit(solution)/shard_map/ppermute | solution.py:15
  13.0 31.5 %collective-permute-start.1 = (bf16[1,1440,256]{2,1,0:T(8,128)(2,1)S(1)}, bf16[1,1440,256]{2,1,0:T(8,128)(2,1)}, u32[]{:S(2)}, u32[]{:S(2)}) collective-permute-start(bf16[1,1440,256]{2,1,0:T(8,128)(2,1)S(1)} %get-tuple-element.117), channel_id=1, source_target_pairs={{2,0},{4,2},{6,4},{8,6},{10,8},{12,10},{14,12},{3,1},{5,3},{7,5},{... | collective-permute-start | bytes 2211848 | tf_op jit(solution)/shard_map/ppermute | solution.py:17
  144.0 16.4 %copy-start.1 = (bf16[2,1440,256]{2,1,0:T(8,128)(2,1)S(1)}, bf16[2,1440,256]{2,1,0:T(8,128)(2,1)}, u32[]{:S(2)}) copy-start(bf16[2,1440,256]{2,1,0:T(8,128)(2,1)} %param.11) | copy-start | bytes 4423684
  144.0 32.5 %copy-start.2 = (bf16[512,512]{1,0:T(8,128)(2,1)S(1)}, bf16[512,512]{1,0:T(8,128)(2,1)}, u32[]{:S(2)}) copy-start(bf16[512,512]{1,0:T(8,128)(2,1)} %param.17) | copy-start | bytes 1572868
  144.0 32.5 %all-gather.2.cloned.1.call-start = ((), (), s32[]{:S(2)}) async-start(), calls=%async_computation.3 | async-start | bytes 4423680 | tf_op jit(solution)/shard_map/all_gather | solution.py:76
  163.7 45.8 %reduce-scatter.5.cloned.1.call-start = ((), (), s32[]{:S(2)}) async-start(), calls=%async_computation.4 | async-start | bytes 8847360 | tf_op jit(solution)/shard_map/reduce_scatter | solution.py:77
Sparse Core Ops, SparseCore 0:
  144.2 16.2 reduce-scatter.2
  163.8 12.6 all-gather.1
  194.4 15.1 reduce-scatter.4
where the time goes:
time: 221 us; the launch traced here: 220 us
  waiting for transfers between devices  74.6 us (34%)
  other arithmetic  47 us (21%)
  matrix products  41.9 us (19%)
  loops' own time  21.9 us (10%)
  local copies, waits for them, and re-layouts  15.5 us (7%)
  between operations  13.1 us (6%)
  starting transfers between devices  6.3 us (3%)
    ppermute x1, waiting for transfers between devices, with_halo(): lax.ppermute(tail, axis, [(i, (i + 1) % count) for i in range(ends)])  30.2 us
    while x22, other arithmetic  29.3 us
    another operation x1, loops' own time, conv_rows(): return lax.map(one_row, jnp.arange(local_rows, dtype=jnp.int32))  21.9 us
    dot_general x1, matrix products, feed_forward(): output = jnp.dot(hidden, down_matrix, preferred_element_type=jnp.float32)  17.7 us
    reduce_scatter x1, waiting for transfers between devices, per_device(): lax.psum_scatter(partial_mix, 'chan', scatter_dimension=2, tiled=True)  16.3 us
    reduce_scatter x1, waiting for transfers between devices, per_device(): lax.psum_scatter(feed_forward(whole_state, up_weight, down_weight), 'chan...  15.3 us
    dot_general x2, matrix products, one_row(): jnp.einsum('kaz,qzc->kqac', weights, stacked, preferred_element_type=jnp....  15.3 us
    all_gather x1, waiting for transfers between devices, per_device(): whole_state = lax.all_gather(rounded, 'chan', axis=2, tiled=True)  12.8 us
  transfers between devices with their start and end apart: 5, of which 4 were waited for; matrix products, arithmetic and copies ran while one was open for 0% of the time, Pallas kernels for 0%

commit v1 on v0

v1 whole, which is shorter than its diff:
```python
import functools

import jax
import jax.numpy as jnp
from jax import lax
from jax.experimental import pallas as pl
from jax.experimental.pallas import tpu as pltpu
from jax.sharding import PartitionSpec as P

GROUP = 6


def fill_window(window, halves, width, cells):
    most = window.shape[0] - cells
    for index, half in enumerate(halves):
        lanes = slice(index * width, (index + 1) * width)
        window[:cells, lanes] = half
        window[cells:, lanes] = half[:most]


def filter_group(group, block_width, basis_count, channels, weights, windows, starts, lon_blocks, conv):
    most = (windows[0].shape[0] // block_width) - lon_blocks + 1
    for slot in range(GROUP):
        block = group * GROUP + slot
        parts = []
        for window, start in zip(windows, starts):
            first = lax.rem(block + start, lon_blocks) * block_width
            first = pl.multiple_of(first, block_width)
            parts.append(window[pl.ds(first, most * block_width), :])
        cells = parts[0] if len(parts) == 1 else jnp.concatenate(parts, axis=0)
        result = jnp.dot(weights, cells, preferred_element_type=jnp.float32).astype(jnp.bfloat16)
        for basis in range(basis_count):
            conv[slot * block_width : (slot + 1) * block_width, basis * channels : (basis + 1) * channels] = (
                result[basis * block_width : (basis + 1) * block_width]
            )


def local_kernel(
    scalars, own, other, weights, mix, result, window0, window1, conv,
    *, block_width, basis_count, lon_blocks,
):
    group = pl.program_id(0)
    cells, width = own.shape[1], own.shape[2]

    @pl.when(group == 0)
    def _():
        for row, window in enumerate((window0, window1)):
            fill_window(window, (own[row], other[row]), width, cells)

    filter_group(
        group, block_width, basis_count, 2 * width, weights[...], (window0, window1),
        (scalars[0], scalars[1]), lon_blocks, conv,
    )
    mixed = jnp.dot(conv[...], mix[...], preferred_element_type=jnp.float32)
    core = scalars[3]
    rows = pl.ds(pl.multiple_of(group * GROUP * block_width, GROUP * block_width), GROUP * block_width)
    near = own[core, rows, :].astype(jnp.float32)
    far = other[core, rows, :].astype(jnp.float32)
    low = jnp.where(core == 0, near, far)
    high = jnp.where(core == 0, far, near)
    result[:, :width] = mixed[:, :width] + low
    result[:, width:] = mixed[:, width:] + high


def gelu(x):
    return 0.5 * x * (1.0 + lax.erf(x * 0.7071067811865476))


def tail_kernel(
    scalars, own, other, weights, mix, partial, up, down, keep, send, window, conv,
    *, block_width, basis_count, lon_blocks,
):
    group = pl.program_id(0)
    cells, width = own.shape

    @pl.when(group == 0)
    def _():
        fill_window(window, (own[...], other[...]), width, cells)

    filter_group(
        group, block_width, basis_count, 2 * width, weights[...], (window,), (scalars[2],), lon_blocks, conv
    )
    state = partial[...] + jnp.dot(conv[...], mix[...], preferred_element_type=jnp.float32)
    rounded = state.astype(jnp.bfloat16)
    hidden = gelu(jnp.dot(rounded, up[...], preferred_element_type=jnp.float32)).astype(jnp.bfloat16)
    feed = jnp.dot(hidden, down[...], preferred_element_type=jnp.float32)
    total = (state + feed).astype(jnp.bfloat16)
    low, high = total[:, :width], total[:, width:]
    core = scalars[3]
    keep[...] = jnp.where(core == 0, low, high)
    send[...] = jnp.where(core == 0, high, low)


def whole(shape):
    return pl.BlockSpec(shape, lambda *_: (0,) * len(shape), pipeline_mode=pl.Buffered(1))


def per_device(
    state_in, basis_blocks, block_start, block_count, mix_weight, up_weight, down_weight
):
    core = lax.axis_index("chan")
    bands = lax.axis_size("lat")
    basis_count, block_width, taps, block_most = basis_blocks.shape[1:5]
    cells, width = state_in.shape[1:]
    channels = mix_weight.shape[2]
    lon_blocks = cells // block_width
    swap = [(0, 1), (1, 0)]
    pairs = []
    for band in range(bands - 1):
        pairs += [(2 * band + 1, 2 * band + 2), (2 * band + 2, 2 * band + 1)]

    halo_other = lax.ppermute(jnp.where(core == 0, state_in[0], state_in[1]), ("lat", "chan"), pairs)
    other = lax.ppermute(state_in, "chan", swap)
    halo_own = lax.ppermute(jnp.where(core == 0, other[0], other[1]), ("lat", "chan"), pairs)
    mix = jnp.concatenate([mix_weight, lax.ppermute(mix_weight, "chan", swap)], 1)
    mix = mix.reshape(basis_count * channels, channels)
    up = jnp.concatenate([up_weight, lax.ppermute(up_weight, "chan", swap)], 1)
    down = jnp.concatenate([down_weight, lax.ppermute(down_weight, "chan", swap)], 0)

    counts = block_count[core]
    starts = block_start[core]
    kept = jnp.arange(block_most, dtype=jnp.int32)[None, :] < counts[:, None]
    filters = jnp.where(kept[None, None, :, :, None], basis_blocks[core], 0)
    filters = filters.reshape(basis_count * block_width, taps, block_most * block_width)
    near = lax.dynamic_slice_in_dim(filters, 1 - core, 2, 1)
    near = near.reshape(basis_count * block_width, 2 * block_most * block_width)
    edge = lax.dynamic_index_in_dim(filters, 2 * core, 1, keepdims=False)
    scalars = jnp.stack([starts[1 - core], starts[2 - core], starts[2 * core], core])

    rows = GROUP * block_width
    sizes = dict(block_width=block_width, basis_count=basis_count, lon_blocks=lon_blocks)
    window = pltpu.VMEM((cells + (block_most - 1) * block_width, channels), jnp.bfloat16)
    conv = pltpu.VMEM((rows, basis_count * channels), jnp.bfloat16)
    params = pltpu.CompilerParams(vmem_limit_bytes=40 * 1024 * 1024)
    mix_flops = 2 * cells * basis_count * channels * channels

    def conv_flops(depth):
        return 2 * basis_count * cells * depth * block_most * block_width * channels

    partial = pl.pallas_call(
        functools.partial(local_kernel, **sizes),
        out_shape=jax.ShapeDtypeStruct((cells, channels), jnp.float32),
        grid_spec=pltpu.PrefetchScalarGridSpec(
            num_scalar_prefetch=1,
            grid=(cells // rows,),
            in_specs=[whole(state_in.shape), whole(other.shape), whole(near.shape), whole(mix.shape)],
            out_specs=pl.BlockSpec((rows, channels), lambda i, _: (i, 0)),
            scratch_shapes=[window, window, conv],
        ),
        compiler_params=params,
        cost_estimate=pl.CostEstimate(
            flops=mix_flops + conv_flops(2), bytes_accessed=10_000_000, transcendentals=0
        ),
        name="local_taps",
    )(scalars, state_in, other, near, mix)

    half = jax.ShapeDtypeStruct((cells, width), jnp.bfloat16)
    keep, send = pl.pallas_call(
        functools.partial(tail_kernel, **sizes),
        out_shape=(half, half),
        grid_spec=pltpu.PrefetchScalarGridSpec(
            num_scalar_prefetch=1,
            grid=(cells // rows,),
            in_specs=[
                whole(halo_own.shape), whole(halo_other.shape), whole(edge.shape), whole(mix.shape),
                pl.BlockSpec((rows, channels), lambda i, _: (i, 0)),
                whole(up.shape), whole(down.shape),
            ],
            out_specs=[pl.BlockSpec((rows, width), lambda i, _: (i, 0))] * 2,
            scratch_shapes=[window, conv],
        ),
        compiler_params=params,
        cost_estimate=pl.CostEstimate(
            flops=mix_flops + conv_flops(1) + 8 * cells * channels * channels,
            bytes_accessed=10_000_000, transcendentals=cells * up.shape[1],
        ),
        name="edge_tap_and_feed",
    )(scalars, halo_own, halo_other, edge, mix, partial, up, down)

    received = lax.ppermute(send, "chan", swap)
    first = jnp.where(core == 0, keep, received)
    second = jnp.where(core == 0, received, keep)
    return jnp.stack([first, second])


def solution(mesh):
    placed = (
        P(("grp", "lat"), None, "chan"),
        P("lat", None, None, None, None, None),
        P("lat", None),
        P("lat", None),
        P(None, "chan", None),
        P(None, "chan"),
        P("chan", None),
    )
    return jax.shard_map(
        per_device,
        mesh=mesh,
        in_specs=placed,
        out_specs=P(("grp", "lat"), None, "chan"),
        check_vma=False,
    )
```

time: 221 us -> 66.6 us (0.30)
  waiting for transfers between devices: 74.6 us -> 1.86 us
  matrix products: 41.9 us -> 0 us
  other arithmetic: 47 us -> 13 us
  Pallas kernels: 0 us -> 25.4 us
  loops' own time: 21.9 us -> 0 us
  between operations: 13.1 us -> 0.2 us
  starting transfers between devices: 6.3 us -> 13.3 us
  local copies, waits for them, and re-layouts: 15.5 us -> 12 us
    dot_general x4 -> x0, matrix products: 41.9 us -> none  [the longest x1 17.7 us: feed_forward(): output = jnp.dot(hidden, down_matrix, preferred_element_type=jnp.float32)]
    reduce_scatter x2 -> x0, waiting for transfers between devices: 31.6 us -> none  [the longest x1 16.3 us: per_device(): lax.psum_scatter(partial_mix, 'chan', scatter_dimension=2, tiled=True)]
    while x22 -> x0, other arithmetic: 29.3 us -> none
    ppermute x2 -> x7, waiting for transfers between devices: 30.2 us -> 1.86 us  [the longest x1 1.84 us: per_device(): received = lax.ppermute(send, 'chan', swap)]
    pallas_call x0 -> x2, Pallas kernels: none -> 25.4 us  [the longest x1 13.1 us: per_device(): pl.pallas_call(functools.partial(tail_kernel, **sizes), out_shape=(half,...]
    another operation x1 -> x0, loops' own time: 21.9 us -> none  [conv_rows(): return lax.map(one_row, jnp.arange(local_rows, dtype=jnp.int32))]
    all_gather x1 -> x0, waiting for transfers between devices: 12.8 us -> none  [per_device(): whole_state = lax.all_gather(rounded, 'chan', axis=2, tiled=True)]
    convert_element_type x2 -> x0, other arithmetic: 7.62 us -> none  [the longest x1 4.35 us: per_device(): return (state + feed).astype(jnp.bfloat16)]
  transfers between devices with their start and end apart: 5 -> 7, of which waited for: 4 -> 1; matrix products, arithmetic and copies ran while one was open for 0% -> 35% of each run, Pallas kernels for 0% -> 19%
where the time goes in v1:
time: 66.6 us; the launch traced here: 65.7 us
  Pallas kernels  25.4 us (38%)
  starting transfers between devices  13.3 us (20%)
  other arithmetic  13 us (20%)
  local copies, waits for them, and re-layouts  12 us (18%)
  waiting for transfers between devices  1.86 us (3%)
    pallas_call x1, Pallas kernels, per_device(): pl.pallas_call(functools.partial(tail_kernel, **sizes), out_shape=(half,...  13.1 us
    pallas_call x1, Pallas kernels, per_device(): pl.pallas_call(functools.partial(local_kernel, **sizes), out_shape=jax.Sh...  12.3 us
    ppermute x1, starting transfers between devices, per_device(): received = lax.ppermute(send, 'chan', swap)  6.89 us
    squeeze x1, local copies, waits for them, and re-layouts, per_device(): filters = jnp.where(kept[None, None, :, :, None], basis_blocks[core], 0)  4.48 us
    ppermute x1, starting transfers between devices, per_device(): up = jnp.concatenate([up_weight, lax.ppermute(up_weight, 'chan', swap)], 1)  3.51 us
    select_n x1, other arithmetic, per_device(): jnp.where(core == 0, state_in[0], state_in[1])  2.5 us
    reshape x1, local copies, waits for them, and re-layouts, per_device(): near = near.reshape(basis_count * block_width, 2 * block_most * block_width)  2.05 us
    another operation x1, other arithmetic, per_device(): jnp.stack([starts[1 - core], starts[2 - core], starts[2 * core], core])  1.89 us
  transfers between devices with their start and end apart: 7, of which 1 were waited for; matrix products, arithmetic and copies ran while one was open for 35% of the time, Pallas kernels for 19%

profile of v1, /device:TPU:0, one launch (start us, length us, event | category | flops | bytes accessed | tf_op | source)
XLA Modules:
  0.0 65.7 jit_solution(12562072667209385603)
XLA Ops:
  0.0 0.5 collective-permute-start.3
  0.5 2.5 %select_bitcast_fusion.2 = bf16[1440,256]{1,0:T(8,128)(2,1)} fusion(bf16[2,1440,256]{2,1,0:T(8,128)(2,1)} %own.1, pred[]{:T(512)S(6)} %eq.2), kind=kLoop, calls=%fused_computation.9 | loop fusion | flops 368640 | bytes 2211841 | tf_op jit(solution)/shard_map/jit(_where)/select_n | solution.py:112
  3.0 1.5 %collective-permute-start.2 = (bf16[1440,256]{1,0:T(8,128)(2,1)}, bf16[1440,256]{1,0:T(8,128)(2,1)}, u32[]{:S(2)}, u32[]{:S(2)}) collective-permute-start(bf16[1440,256]{1,0:T(8,128)(2,1)} %select_bitcast_fusion.2), channel_id=1, source_target_pairs={{1,2},{2,1},{3,4},{4,3},{5,6},{6,5},{7,8},{8,7},{9,10},{10,9},{11,... | collective-permute-start | bytes 2211848 | tf_op jit(solution)/shard_map/ppermute | solution.py:112
  4.6 3.5 %collective-permute-start.4 = (bf16[512,512]{1,0:T(8,128)(2,1)}, bf16[512,512]{1,0:T(8,128)(2,1)}, u32[]{:S(2)}, u32[]{:S(2)}) collective-permute-start(bf16[512,512]{1,0:T(8,128)(2,1)} %param.12), channel_id=1, source_target_pairs={{0,1},{1,0},{2,3},{3,2},{4,5},{5,4},{6,7},{7,6},{8,9},{9,8},{10,11... | collective-permute-start | bytes 1572872 | tf_op jit(solution)/shard_map/ppermute | solution.py:117
  8.2 1.5 %constant_dynamic-slice_fusion.1 = bf16[1,5,80,3,4,80]{5,4,3,2,1,0:T(4,128)(2,1)} fusion(bf16[2,5,80,3,4,80]{5,4,3,2,1,0:T(4,128)(2,1)S(1)} %copy-done, s32[]{:T(128)S(6)} %select_n.59), kind=kLoop, calls=%fused_computation.13 | loop fusion | bytes 1536004 | tf_op jit(solution)/shard_map/dynamic_slice | solution.py:123
  9.6 4.5 %reshape.41 = bf16[400,3,320]{2,1,0:T(4,128)(2,1)} reshape(bf16[1,5,80,3,4,80]{5,4,3,2,1,0:T(4,128)(2,1)} %constant_dynamic-slice_fusion.1) | data formatting | bytes 1536000 | tf_op jit(solution)/shard_map/squeeze | solution.py:123
  14.4 1.5 %copy_select_fusion = bf16[400,3,320]{2,0,1:T(8,128)(2,1)S(1)} fusion(bf16[400,3,320]{2,1,0:T(4,128)(2,1)} %reshape.41, pred[3,320]{1,0:T(4,128)(4,1)S(1)} %broadcast_in_dim.19), kind=kLoop, calls=%fused_computation.4 | loop fusion | flops 384000 | bytes 1536960 | tf_op jit(solution)/shard_map/jit(_where)/select_n | solution.py:123
  15.9 0.8 %copy-done.2 = bf16[400,3,320]{2,0,1:T(8,128)(2,1)} copy-done((bf16[400,3,320]{2,0,1:T(8,128)(2,1)}, bf16[400,3,320]{2,0,1:T(8,128)(2,1)S(1)}, u32[]{:S(2)}) %copy-start.2) | copy-done | bytes 768024
  16.8 1.3 %copy.10 = bf16[400,2,320]{2,1,0:T(2,128)(2,1)} copy(bf16[400,2,320]{2,0,1:T(8,128)(2,1)S(1)} %constant_dynamic-slice_fusion) | data formatting | bytes 1024000 | tf_op jit(solution)/shard_map/dynamic_slice | solution.py:125
  18.0 2.1 %reshape.40.weights = bf16[400,640]{1,0:T(8,128)(2,1)S(1)} reshape(bf16[400,2,320]{2,1,0:T(2,128)(2,1)} %copy.10) | data formatting | bytes 1024000 | tf_op jit(solution)/shard_map/reshape | solution.py:126
  20.1 0.7 %fusion.2 = (s32[1,1]{1,0:T(1,128)}, s32[1,1]{1,0:T(1,128)}, s32[1,1]{1,0:T(1,128)}) fusion(s32[2,3]{1,0:T(2,128)S(1)} %copy-done.4, s32[]{:T(128)S(6)} %select_n.60, s32[]{:T(128)S(6)} %select_n.62, s32[]{:T(128)S(6)} %select_n.66, s32[]{:T(128)S(6)} %select_n.64), kind=kLoop, calls=%fused_computation.17 | loop fusion | bytes 40 | tf_op jit(solution)/shard_map/dynamic_slice | solution.py:128
  20.8 1.9 %pad_add_fusion.scalars = s32[4]{0:T(128)S(1)} fusion(s32[1]{0:T(128)} %bitcast.3, s32[1]{0:T(128)} %bitcast.2, s32[1]{0:T(128)} %bitcast.1, s32[1]{0:T(128)} %bitcast), kind=kLoop, calls=%fused_computation.16 | loop fusion | flops 12 | bytes 32 | tf_op jit(solution)/shard_map/stack | solution.py:128
  22.7 1.0 %dynamic-slice_bitcast_fusion.weights = bf16[400,320]{1,0:T(8,128)(2,1)S(1)} fusion(bf16[400,3,320]{2,0,1:T(8,128)(2,1)} %copy-done.2, s32[]{:T(128)S(6)} %select_n.65), kind=kLoop, calls=%fused_computation.10 | loop fusion | bytes 512004 | tf_op jit(solution)/shard_map/jit(dynamic_index_in_dim)/squeeze | solution.py:127
  23.7 1.4 %pad_maximum_fusion.2.up = bf16[512,1024]{1,0:T(8,128)(2,1)S(1)} fusion(bf16[512,512]{1,0:T(8,128)(2,1)} %collective-permute-done.4, bf16[512,512]{1,0:T(8,128)(2,1)} %param.12), kind=kLoop, calls=%fused_computation.2 | loop fusion | flops 2097152 | bytes 2097152 | tf_op jit(solution)/shard_map/concatenate | solution.py:117
  25.1 1.3 %pad_maximum_fusion.3.down = bf16[1024,512]{1,0:T(8,128)(2,1)S(1)} fusion(bf16[512,512]{1,0:T(8,128)(2,1)} %collective-permute-done.5, bf16[512,512]{1,0:T(8,128)(2,1)} %param.13), kind=kLoop, calls=%fused_computation.3 | loop fusion | flops 2097152 | bytes 2097152 | tf_op jit(solution)/shard_map/concatenate | solution.py:118
  26.4 1.5 %pad_maximum_fusion = bf16[5,512,512]{2,1,0:T(8,128)(2,1)S(1)} fusion(bf16[5,256,512]{2,1,0:T(8,128)(2,1)} %collective-permute-done.3, bf16[5,256,512]{2,1,0:T(8,128)(2,1)S(1)} %copy-done.3), kind=kLoop, calls=%fused_computation | loop fusion | flops 5242880 | bytes 5242880 | tf_op jit(solution)/shard_map/concatenate | solution.py:115
  28.0 1.5 %fusion = bf16[1440,256]{1,0:T(8,128)(2,1)S(1)} fusion(bf16[2,1440,256]{2,1,0:T(8,128)(2,1)} %collective-permute-done.other, pred[]{:T(512)S(6)} %eq.2), kind=kLoop, calls=%fused_computation.6 | loop fusion | flops 368640 | bytes 2211841 | tf_op jit(solution)/shard_map/jit(_where)/select_n | solution.py:114
  29.5 0.7 %collective-permute-start.1 = (bf16[1440,256]{1,0:T(8,128)(2,1)S(1)}, bf16[1440,256]{1,0:T(8,128)(2,1)S(1)}, u32[]{:S(2)}, u32[]{:S(2)}) collective-permute-start(bf16[1440,256]{1,0:T(8,128)(2,1)S(1)} %fusion), channel_id=1, source_target_pairs={{1,2},{2,1},{3,4},{4,3},{5,6},{6,5},{7,8},{8,7},{9,10},{10,9},{11,... | collective-permute-start | bytes 2211848 | tf_op jit(solution)/shard_map/ppermute | solution.py:114
  30.2 12.3 %local_taps.1.partial = f32[1440,512]{1,0:T(8,128)S(1)} custom-call(s32[4]{0:T(128)S(1)} %pad_add_fusion.scalars, bf16[2,1440,256]{2,1,0:T(8,128)(2,1)S(1)} %copy-done.1, bf16[2,1440,256]{2,1,0:T(8,128)(2,1)} %collective-permute-done.other, bf16[400,640]{1,0:T(8,128)(2,1)S(1)} %reshape.40.weights, bf16[2560,512]{1,0:T(8,128)(2,1)S(1)} %bitcast.17), custom_call_target="tpu_custom_call" | custom-call | flops 8493465600 | bytes 10000000 | tf_op jit(solution)/shard_map/local_taps/pallas_call | solution.py:140
  42.5 13.1 %edge_tap_and_feed.1 = (bf16[1440,256]{1,0:T(8,128)(2,1)S(1)}, bf16[1440,256]{1,0:T(8,128)(2,1)S(1)}) custom-call(s32[4]{0:T(128)S(1)} %pad_add_fusion.scalars, bf16[1440,256]{1,0:T(8,128)(2,1)S(1)} %collective-permute-done.1.own, bf16[1440,256]{1,0:T(8,128)(2,1)} %collective-permute-done.2.other, bf16[400,320]{1,0:T(8,128)(2,1)S(1)} %dynamic-slice_bitcast_fusion.weights, ...), custom_call_target="tpu_custom_call" | custom-call | flops 9154068480 | bytes 10000000 | tf_op jit(solution)/shard_map/edge_tap_and_feed/pallas_call | solution.py:158
  55.6 6.9 %collective-permute-start.6 = (bf16[1440,256]{1,0:T(8,128)(2,1)S(1)}, bf16[1440,256]{1,0:T(8,128)(2,1)S(1)}, u32[]{:S(2)}, u32[]{:S(2)}) collective-permute-start(bf16[1440,256]{1,0:T(8,128)(2,1)S(1)} %get-tuple-element.8), channel_id=1, source_target_pairs={{0,1},{1,0},{2,3},{3,2},{4,5},{5,4},{6,7},{7,6},{8,9},{9,8},{10,11... | collective-permute-start | bytes 2211848 | tf_op jit(solution)/shard_map/ppermute | solution.py:180
  62.5 1.8 %collective-permute-done.6 = bf16[1440,256]{1,0:T(8,128)(2,1)S(1)} collective-permute-done((bf16[1440,256]{1,0:T(8,128)(2,1)S(1)}, bf16[1440,256]{1,0:T(8,128)(2,1)S(1)}, u32[]{:S(2)}, u32[]{:S(2)}) %collective-permute-start.6) | collective-permute-done | bytes 737312 | tf_op jit(solution)/shard_map/ppermute | solution.py:180
  64.4 0.1 select_bitcast_fusion.1
  64.5 1.2 %pad_maximum_fusion.1 = bf16[2,1440,256]{2,1,0:T(8,128)(2,1)} fusion(bf16[1,1440,256]{2,1,0:T(8,128)(2,1)S(1)} %get-tuple-element.10, bf16[1,1440,256]{2,1,0:T(8,128)(2,1)S(1)} %get-tuple-element.9), kind=kLoop, calls=%fused_computation.1 | loop fusion | flops 737280 | bytes 2949120 | tf_op jit(solution)/shard_map/stack | solution.py:183
  (24 shorter events, 0.5 us)
Async XLA Ops:
  0.0 8.2 %copy-start = (bf16[2,5,80,3,4,80]{5,4,3,2,1,0:T(4,128)(2,1)S(1)}, bf16[2,5,80,3,4,80]{5,4,3,2,1,0:T(4,128)(2,1)}, u32[]{:S(2)}) copy-start(bf16[2,5,80,3,4,80]{5,4,3,2,1,0:T(4,128)(2,1)} %param.8) | copy-start | bytes 4608004
  0.0 26.4 %collective-permute-start.3 = (bf16[5,256,512]{2,1,0:T(8,128)(2,1)}, bf16[5,256,512]{2,1,0:T(8,128)(2,1)}, u32[]{:S(2)}, u32[]{:S(2)}) collective-permute-start(bf16[5,256,512]{2,1,0:T(8,128)(2,1)} %param.11), channel_id=1, source_target_pairs={{0,1},{1,0},{2,3},{3,2},{4,5},{5,4},{6,7},{7,6},{8,9},{9,8},{10,11... | collective-permute-start | bytes 3932168 | tf_op jit(solution)/shard_map/ppermute | solution.py:115
  0.5 27.5 %collective-permute-start = (bf16[2,1440,256]{2,1,0:T(8,128)(2,1)}, bf16[2,1440,256]{2,1,0:T(8,128)(2,1)}, u32[]{:S(2)}, u32[]{:S(2)}) collective-permute-start(bf16[2,1440,256]{2,1,0:T(8,128)(2,1)} %own.1), channel_id=1, source_target_pairs={{0,1},{1,0},{2,3},{3,2},{4,5},{5,4},{6,7},{7,6},{8,9},{9,8},{10,11... | collective-permute-start | bytes 4423688 | tf_op jit(solution)/shard_map/ppermute | solution.py:113
  3.0 39.5 %collective-permute-start.2 = (bf16[1440,256]{1,0:T(8,128)(2,1)}, bf16[1440,256]{1,0:T(8,128)(2,1)}, u32[]{:S(2)}, u32[]{:S(2)}) collective-permute-start(bf16[1440,256]{1,0:T(8,128)(2,1)} %select_bitcast_fusion.2), channel_id=1, source_target_pairs={{1,2},{2,1},{3,4},{4,3},{5,6},{6,5},{7,8},{8,7},{9,10},{10,9},{11,... | collective-permute-start | bytes 2211848 | tf_op jit(solution)/shard_map/ppermute | solution.py:112
  4.6 19.1 %collective-permute-start.4 = (bf16[512,512]{1,0:T(8,128)(2,1)}, bf16[512,512]{1,0:T(8,128)(2,1)}, u32[]{:S(2)}, u32[]{:S(2)}) collective-permute-start(bf16[512,512]{1,0:T(8,128)(2,1)} %param.12), channel_id=1, source_target_pairs={{0,1},{1,0},{2,3},{3,2},{4,5},{5,4},{6,7},{7,6},{8,9},{9,8},{10,11... | collective-permute-start | bytes 1572872 | tf_op jit(solution)/shard_map/ppermute | solution.py:117
  8.1 17.1 %collective-permute-start.5 = (bf16[512,512]{1,0:T(8,128)(2,1)}, bf16[512,512]{1,0:T(8,128)(2,1)}, u32[]{:S(2)}, u32[]{:S(2)}) collective-permute-start(bf16[512,512]{1,0:T(8,128)(2,1)} %param.13), channel_id=1, source_target_pairs={{0,1},{1,0},{2,3},{3,2},{4,5},{5,4},{6,7},{7,6},{8,9},{9,8},{10,11... | collective-permute-start | bytes 1572872 | tf_op jit(solution)/shard_map/ppermute | solution.py:118
  8.2 5.9 %copy-start.5 = (s32[2,3]{1,0:T(2,128)S(1)}, s32[2,3]{1,0:T(2,128)}, u32[]{:S(2)}) copy-start(s32[2,3]{1,0:T(2,128)} %param.10) | copy-start | bytes 76
  15.8 0.9 %copy-start.2 = (bf16[400,3,320]{2,0,1:T(8,128)(2,1)}, bf16[400,3,320]{2,0,1:T(8,128)(2,1)S(1)}, u32[]{:S(2)}) copy-start(bf16[400,3,320]{2,0,1:T(8,128)(2,1)S(1)} %copy_select_fusion) | copy-start | bytes 2304004
  15.8 4.3 %copy-start.4 = (s32[2,3]{1,0:T(2,128)S(1)}, s32[2,3]{1,0:T(2,128)}, u32[]{:S(2)}) copy-start(s32[2,3]{1,0:T(2,128)} %param.9) | copy-start | bytes 76
  23.7 2.7 %copy-start.3 = (bf16[5,256,512]{2,1,0:T(8,128)(2,1)S(1)}, bf16[5,256,512]{2,1,0:T(8,128)(2,1)}, u32[]{:S(2)}) copy-start(bf16[5,256,512]{2,1,0:T(8,128)(2,1)} %param.11) | copy-start | bytes 3932164
  27.9 2.3 %copy-start.1 = (bf16[2,1440,256]{2,1,0:T(8,128)(2,1)S(1)}, bf16[2,1440,256]{2,1,0:T(8,128)(2,1)}, u32[]{:S(2)}) copy-start(bf16[2,1440,256]{2,1,0:T(8,128)(2,1)} %own.1) | copy-start | bytes 4423684
  29.5 13.0 %collective-permute-start.1 = (bf16[1440,256]{1,0:T(8,128)(2,1)S(1)}, bf16[1440,256]{1,0:T(8,128)(2,1)S(1)}, u32[]{:S(2)}, u32[]{:S(2)}) collective-permute-start(bf16[1440,256]{1,0:T(8,128)(2,1)S(1)} %fusion), channel_id=1, source_target_pairs={{1,2},{2,1},{3,4},{4,3},{5,6},{6,5},{7,8},{8,7},{9,10},{10,9},{11,... | collective-permute-start | bytes 2211848 | tf_op jit(solution)/shard_map/ppermute | solution.py:114
  55.6 8.7 %collective-permute-start.6 = (bf16[1440,256]{1,0:T(8,128)(2,1)S(1)}, bf16[1440,256]{1,0:T(8,128)(2,1)S(1)}, u32[]{:S(2)}, u32[]{:S(2)}) collective-permute-start(bf16[1440,256]{1,0:T(8,128)(2,1)S(1)} %get-tuple-element.8), channel_id=1, source_target_pairs={{0,1},{1,0},{2,3},{3,2},{4,5},{5,4},{6,7},{7,6},{8,9},{9,8},{10,11... | collective-permute-start | bytes 2211848 | tf_op jit(solution)/shard_map/ppermute | solution.py:180

commit v2 on v0

v2 whole, which is shorter than its diff:
```python
import functools

import jax
import jax.numpy as jnp
from jax import lax
from jax.experimental import pallas as pl
from jax.experimental.pallas import tpu as pltpu
from jax.sharding import PartitionSpec as P

GROUP = 9
FIRST = 8
TILE = 16


def start_all(copies):
    for copy in copies:
        copy.start()
    return copies


def wait_all(copies):
    for copy in copies:
        copy.wait()


def halo_start(block_start, core):
    return block_start[core, 2 * core]


def block_rows(block, block_width, blocks=1):
    return pl.ds(pl.multiple_of(block * block_width, block_width), blocks * block_width)


def home_block(place, start, lon_blocks):
    return lax.rem(place + lon_blocks - start, lon_blocks)


def spread_filters(basis, counts, core, filters, block_most):
    rows_out, taps, width = filters.shape[1], filters.shape[0], basis.shape[1]
    pieces = taps * block_most
    size = TILE * pieces
    row = lax.broadcasted_iota(jnp.int32, (size, size), 0)
    column = lax.broadcasted_iota(jnp.int32, (size, size), 1)
    order = (column == lax.rem(row, TILE) * pieces + row // TILE).astype(jnp.float32).astype(jnp.bfloat16)
    for tile in range(rows_out // TILE):
        sorted_rows = jnp.dot(
            order, basis[tile * size : (tile + 1) * size, :], preferred_element_type=jnp.float32
        ).astype(jnp.bfloat16)
        for tap in range(taps):
            for block in range(block_most):
                at = (tap * block_most + block) * TILE
                piece = sorted_rows[at : at + TILE]
                filters[tap, tile * TILE : (tile + 1) * TILE, block * width : (block + 1) * width] = (
                    jnp.where(block < counts[core, tap], piece, jnp.zeros_like(piece))
                )


def filter_kernel(block_count, basis_from, near, edge, basis, filters, sem, *, block_most):
    core = lax.axis_index("chan")
    rows = basis.shape[0]
    depth = filters.shape[2]
    copy = pltpu.make_async_copy(
        basis_from.at[pl.ds(pl.multiple_of(core * rows, rows), rows), :], basis, sem
    )
    copy.start()
    copy.wait()
    spread_filters(basis, block_count, core, filters, block_most)
    near[:, :depth] = filters[1 - core]
    near[:, depth:] = filters[2 - core]
    edge[...] = filters[2 * core]


def local_kernel(
    block_start, near, own, other, conv_own, conv_other, residual, window0, window1,
    *, lon_blocks, block_width, block_most,
):
    core = lax.axis_index("chan")
    cells, width = own.shape[1:]
    for row, window in enumerate((window0, window1)):
        extra = window.shape[0] - cells
        for half, source in enumerate((own, other)):
            lanes = slice(half * width, (half + 1) * width)
            window[:cells, lanes] = source[row]
            window[cells:, lanes] = source[row, :extra]
    start = halo_start(block_start, core)
    for place in range(lon_blocks):
        source = block_rows(home_block(place, start, lon_blocks), block_width)
        target = slice(place * block_width, (place + 1) * block_width)
        mine = own[core, source, :].astype(jnp.float32)
        theirs = other[core, source, :].astype(jnp.float32)
        residual[target, :width] = jnp.where(core == 0, mine, theirs)
        residual[target, width:] = jnp.where(core == 0, theirs, mine)
    starts = (block_start[core, 1 - core], block_start[core, 2 - core])

    def group_step(group, carry):
        for slot in range(GROUP):
            block = group * GROUP + slot
            parts = []
            for window, start in zip((window0, window1), starts):
                place = lax.rem(block + start, lon_blocks)
                parts.append(window[block_rows(place, block_width, block_most), :])
            result = jnp.dot(near[...], jnp.concatenate(parts, axis=0), preferred_element_type=jnp.float32)
            conv_own[block] = result[:, :width]
            conv_other[block] = result[:, width:]
        return carry

    lax.fori_loop(0, lon_blocks // GROUP, group_step, 0)


def halo_conv(first, places, start, lon_blocks, block_width, window, edge_filter, conv_local, conv):
    depth = edge_filter.shape[1]
    width = window.shape[1]
    for slot in range(places):
        home = home_block(first + slot, start, lon_blocks)
        result = conv_local[home] + jnp.dot(
            edge_filter[...], window[slot * block_width : slot * block_width + depth, :],
            preferred_element_type=jnp.float32,
        )
        rounded = result.astype(jnp.bfloat16)
        for basis in range(edge_filter.shape[0] // block_width):
            conv[
                slot * block_width : (slot + 1) * block_width, basis * width : (basis + 1) * width
            ] = rounded[basis * block_width : (basis + 1) * block_width]


def first_half_kernel(
    block_start, half, edge_filter, conv_local, mix, residual, result, window, conv, *, lon_blocks, block_width
):
    core = lax.axis_index("chan")
    start = halo_start(block_start, core)
    cells = half.shape[0]
    window[:cells, :] = half[...]
    window[cells:, :] = half[: window.shape[0] - cells, :]
    rows = GROUP * block_width
    for group in range(lon_blocks // GROUP):
        halo_conv(
            group * GROUP, GROUP, start, lon_blocks, block_width,
            window.at[group * rows :, :], edge_filter, conv_local, conv,
        )
        here = slice(group * rows, (group + 1) * rows)
        result[here, :] = residual[here, :] + jnp.dot(conv[...], mix[...], preferred_element_type=jnp.float32)


def gelu(x):
    return 0.5 * x * (1.0 + lax.erf(x * 0.7071067811865476))


def tail_kernel(block_start, *refs, first, places, lon_blocks, block_width, pieces, ordered):
    halves, refs = refs[: len(pieces)], refs[len(pieces) + ordered :]
    (edge_filter, conv_local, partial, mix, up, up_other, down, down_other, keep, send, window, conv) = refs
    core = lax.axis_index("chan")
    start = halo_start(block_start, core)
    width = window.shape[1]
    at = 0
    for half, (low, high) in zip(halves, pieces):
        window[at : at + high - low, :] = half[low:high, :]
        at += high - low
    halo_conv(first, places, start, lon_blocks, block_width, window, edge_filter, conv_local, conv)
    mixed = jnp.dot(conv[...], mix[...], preferred_element_type=jnp.float32)
    state = partial[first * block_width : (first + places) * block_width, :] + mixed
    rounded = state.astype(jnp.bfloat16)
    total = state
    for inward, outward in ((up, down), (up_other, down_other)):
        hidden = gelu(jnp.dot(rounded, inward[...], preferred_element_type=jnp.float32)).astype(jnp.bfloat16)
        total += jnp.dot(hidden, outward[...], preferred_element_type=jnp.float32)
    total = total.astype(jnp.bfloat16)
    low, high = total[:, :width], total[:, width:]
    keep[...] = jnp.where(core == 0, low, high)
    send[...] = jnp.where(core == 0, high, low)


def stage_kernel(*refs):
    *refs, sems = refs
    count = len(refs) // 2
    wait_all(start_all([
        pltpu.make_async_copy(refs[index], refs[count + index], sems.at[index]) for index in range(count)
    ]))


def place_kernel(block_start, *refs, kept, received, lon_blocks, block_width):
    result, sems = refs[-2:]
    core = lax.axis_index("chan")
    jobs = []
    for index, (source, first) in enumerate(zip(refs, kept + received)):
        row = core if index < len(kept) else 1 - core
        places = source.shape[0] // block_width
        home = home_block(first, halo_start(block_start, row), lon_blocks)
        before_wrap = jnp.minimum(lon_blocks - home, places)
        for count in range(1, places + 1):
            size = count * block_width
            copies = [pltpu.make_async_copy(
                source.at[:size, :], result.at[row, block_rows(home, block_width, count), :], sems.at[index, 0]
            )]
            if count < places:
                copies.append(pltpu.make_async_copy(
                    source.at[size:, :], result.at[row, : source.shape[0] - size, :], sems.at[index, 1]
                ))
            jobs.append((before_wrap == count, copies))
    for started in (True, False):
        for chosen, copies in jobs:

            @pl.when(chosen)
            def _():
                if started:
                    start_all(copies)
                else:
                    wait_all(copies)


def limit(mebibytes):
    return pltpu.CompilerParams(vmem_limit_bytes=mebibytes * 1024 * 1024)


def cost(flops=1000):
    return pl.CostEstimate(flops=flops, bytes_accessed=1000, transcendentals=0)


def anywhere(count):
    return [pl.BlockSpec(memory_space=pl.ANY)] * count


def vmem(count):
    return [pl.BlockSpec(memory_space=pltpu.VMEM)] * count


def per_device(
    state_in, basis_blocks, block_start, block_count, mix_weight, up_weight, down_weight
):
    core = lax.axis_index("chan")
    bands = lax.axis_size("lat")
    local_rows, basis_count, block_width, taps, block_most = basis_blocks.shape[:5]
    cells, width = state_in.shape[1:]
    channels = mix_weight.shape[2]
    lon_blocks = cells // block_width
    depth = block_most * block_width
    filter_rows = basis_count * block_width
    swap = [(0, 1), (1, 0)]
    pairs = []
    for band in range(bands - 1):
        pairs += [(2 * band + 1, 2 * band + 2), (2 * band + 2, 2 * band + 1)]

    sizes = dict(block_width=block_width, lon_blocks=lon_blocks)
    smem = [pl.BlockSpec(memory_space=pltpu.SMEM)]
    cut = (FIRST + block_most - 1) * block_width
    edge, state_in = lax.optimization_barrier((state_in[core], state_in))
    halo_other = lax.ppermute(edge, ("lat", "chan"), pairs)
    other = lax.ppermute(state_in, "chan", swap)
    relay = other[core]
    halo_first = lax.ppermute(relay[:cut], ("lat", "chan"), pairs)
    halo_last = lax.ppermute(relay[cut:], ("lat", "chan"), pairs)
    basis_flat = basis_blocks.reshape(local_rows * filter_rows * taps * block_most, block_width)
    near_filter, edge_filter = pl.pallas_call(
        functools.partial(filter_kernel, block_most=block_most),
        out_shape=[
            jax.ShapeDtypeStruct((filter_rows, span * depth), jnp.bfloat16) for span in (taps - 1, 1)
        ],
        in_specs=smem + anywhere(1),
        out_specs=vmem(2),
        scratch_shapes=[
            pltpu.VMEM((basis_flat.shape[0] // local_rows, block_width), jnp.bfloat16),
            pltpu.VMEM((taps, filter_rows, depth), jnp.bfloat16),
            pltpu.SemaphoreType.DMA,
        ],
        compiler_params=limit(8),
        cost_estimate=cost(),
        name="spread_filters",
    )(block_count, basis_flat)
    mix_other = lax.ppermute(mix_weight, "chan", swap)
    up_other = lax.ppermute(up_weight, "chan", swap)
    down_other = lax.ppermute(down_weight, "chan", swap)

    conv_shape = jax.ShapeDtypeStruct((lon_blocks, filter_rows, width), jnp.float32)
    wide_window = pltpu.VMEM((cells + depth - block_width, channels), jnp.bfloat16)
    state_shape = jax.ShapeDtypeStruct((cells, channels), jnp.float32)
    conv_own, conv_other, residual = pl.pallas_call(
        functools.partial(local_kernel, block_most=block_most, **sizes),
        out_shape=(conv_shape, conv_shape, state_shape),
        in_specs=smem + vmem(3),
        out_specs=vmem(3),
        scratch_shapes=[wide_window, wide_window],
        compiler_params=limit(14),
        cost_estimate=cost(),
        name="local_taps",
    )(block_start, near_filter, state_in, other)

    weights = (
        mix_other.reshape(basis_count * width, channels), mix_weight.reshape(basis_count * width, channels),
        up_weight, up_other, down_weight, down_other,
    )
    mix_other, *weights = pl.pallas_call(
        stage_kernel,
        out_shape=[jax.ShapeDtypeStruct(array.shape, array.dtype) for array in weights],
        in_specs=anywhere(len(weights)),
        out_specs=vmem(len(weights)),
        scratch_shapes=[pltpu.SemaphoreType.DMA((len(weights),))],
        compiler_params=limit(8),
        cost_estimate=cost(),
        name="stage_weights",
    )(*weights)

    partial = pl.pallas_call(
        functools.partial(first_half_kernel, **sizes),
        out_shape=state_shape,
        in_specs=smem + vmem(5),
        out_specs=vmem(1)[0],
        scratch_shapes=[
            pltpu.VMEM((cells + depth - block_width, width), jnp.bfloat16),
            pltpu.VMEM((GROUP * block_width, basis_count * width), jnp.bfloat16),
        ],
        input_output_aliases={5: 0},
        compiler_params=limit(14),
        cost_estimate=cost(),
        name="edge_tap_first_half",
    )(block_start, halo_other, edge_filter, conv_other, mix_other, residual)

    overlap = (block_most - 1) * block_width
    plans = (
        (0, FIRST, [(0, cut)], (halo_first,)),
        (
            FIRST, lon_blocks - FIRST,
            [(cut - overlap, cut), (0, cells - cut), (0, overlap)], (halo_first, halo_last, halo_first),
        ),
    )
    kept, received, done = [], [], []
    for first, places, pieces, halves in plans:
        half = jax.ShapeDtypeStruct((places * block_width, width), jnp.bfloat16)
        keep, send = pl.pallas_call(
            functools.partial(
                tail_kernel, first=first, places=places, pieces=pieces, ordered=len(done), **sizes
            ),
            out_shape=(half, half),
            in_specs=smem + vmem(len(pieces)) + anywhere(len(done)) + vmem(8),
            out_specs=vmem(2),
            scratch_shapes=[
                pltpu.VMEM(((places + block_most - 1) * block_width, width), jnp.bfloat16),
                pltpu.VMEM((places * block_width, basis_count * width), jnp.bfloat16),
            ],
            compiler_params=limit(14),
            cost_estimate=cost(10**10 if done else 1000),
            name="edge_tap_and_feed",
        )(block_start, *halves, *done, edge_filter, conv_own, partial, *weights)
        if received:
            send, received[-1] = lax.optimization_barrier((send, received[-1]))
        kept.append(keep)
        done = [keep]
        received.append(lax.ppermute(send, "chan", swap))

    result = jax.ShapeDtypeStruct(state_in.shape, state_in.dtype)
    placed = pl.pallas_call(
        functools.partial(place_kernel, kept=[0, FIRST], received=[0], **sizes),
        out_shape=result,
        in_specs=smem + vmem(3),
        out_specs=anywhere(1)[0],
        scratch_shapes=[pltpu.SemaphoreType.DMA((3, 2))],
        cost_estimate=cost(),
        compiler_params=limit(4),
        name="place_rows",
    )(block_start, *kept, received[0])

    def place_last(starts, source, before, *refs):
        place_kernel(starts, source, *refs, kept=[], received=[FIRST], **sizes)

    return pl.pallas_call(
        place_last,
        out_shape=result,
        in_specs=smem + vmem(1) + anywhere(1),
        out_specs=anywhere(1)[0],
        scratch_shapes=[pltpu.SemaphoreType.DMA((1, 2))],
        input_output_aliases={2: 0},
        cost_estimate=cost(),
        compiler_params=limit(4),
        name="place_last_rows",
    )(block_start, received[1], placed)


def solution(mesh):
    placed = (
        P(("grp", "lat"), None, "chan"),
        P("lat", None, None, None, None, None),
        P("lat", None),
        P("lat", None),
        P(None, "chan", None),
        P(None, "chan"),
        P("chan", None),
    )
    return jax.shard_map(
        per_device,
        mesh=mesh,
        in_specs=placed,
        out_specs=P(("grp", "lat"), None, "chan"),
        check_vma=False,
    )
```

time: 221 us -> 51.7 us (0.23)
  waiting for transfers between devices: 74.6 us -> 0.13 us
  other arithmetic: 47 us -> 0 us
  matrix products: 41.9 us -> 0 us
  Pallas kernels: 0 us -> 29.1 us
  loops' own time: 21.9 us -> 0 us
  between operations: 13.1 us -> 0.34 us
  local copies, waits for them, and re-layouts: 15.5 us -> 4.69 us
  starting transfers between devices: 6.3 us -> 16.6 us
    dot_general x4 -> x0, matrix products: 41.9 us -> none  [the longest x1 17.7 us: feed_forward(): output = jnp.dot(hidden, down_matrix, preferred_element_type=jnp.float32)]
    reduce_scatter x2 -> x0, waiting for transfers between devices: 31.6 us -> none  [the longest x1 16.3 us: per_device(): lax.psum_scatter(partial_mix, 'chan', scatter_dimension=2, tiled=True)]
    ppermute x2 -> x9, waiting for transfers between devices: 30.2 us -> 0.13 us  [the longest x2 0.11 us: per_device(): received.append(lax.ppermute(send, 'chan', swap))]
    while x22 -> x0, other arithmetic: 29.3 us -> none
    pallas_call x0 -> x8, Pallas kernels: none -> 29.1 us  [the longest x2 9.71 us: per_device(): pl.pallas_call(functools.partial(tail_kernel, first=first, places=places,...]
    another operation x1 -> x0, loops' own time: 21.9 us -> none  [conv_rows(): return lax.map(one_row, jnp.arange(local_rows, dtype=jnp.int32))]
    all_gather x1 -> x0, waiting for transfers between devices: 12.8 us -> none  [per_device(): whole_state = lax.all_gather(rounded, 'chan', axis=2, tiled=True)]
    ppermute x2 -> x9, starting transfers between devices: 6.21 us -> 16.6 us  [the longest x2 8.79 us: per_device(): received.append(lax.ppermute(send, 'chan', swap))]
  transfers between devices with their start and end apart: 5 -> 9, of which waited for: 4 -> 1; matrix products, arithmetic and copies ran while one was open for 0% -> 2% of each run, Pallas kernels for 0% -> 55%
where the time goes in v2:
time: 51.7 us; the launch traced here: 50.8 us
  Pallas kernels  29.1 us (56%)
  starting transfers between devices  16.6 us (32%)
  local copies, waits for them, and re-layouts  4.69 us (9%)
    pallas_call x2, Pallas kernels, per_device(): pl.pallas_call(functools.partial(tail_kernel, first=first, places=places,...  9.71 us
    ppermute x2, starting transfers between devices, per_device(): received.append(lax.ppermute(send, 'chan', swap))  8.79 us
    pallas_call x1, Pallas kernels, per_device(): pl.pallas_call(functools.partial(local_kernel, block_most=block_most, **s...  7.23 us
    pallas_call x1, Pallas kernels, per_device(): pl.pallas_call(functools.partial(first_half_kernel, **sizes), out_shape=s...  5.55 us
    ppermute x1, starting transfers between devices, per_device(): down_other = lax.ppermute(down_weight, 'chan', swap)  3.06 us
    squeeze x1, local copies, waits for them, and re-layouts, per_device(): edge, state_in = lax.optimization_barrier((state_in[core], state_in))  2.14 us
    pallas_call x1, Pallas kernels, per_device(): pl.pallas_call(functools.partial(filter_kernel, block_most=block_most), o...  1.96 us
    unnamed x14, local copies, waits for them, and re-layouts  1.71 us
  transfers between devices with their start and end apart: 9, of which 1 were waited for; matrix products, arithmetic and copies ran while one was open for 2% of the time, Pallas kernels for 55%

profile of v2, /device:TPU:0, one launch (start us, length us, event | category | flops | bytes accessed | tf_op | source)
XLA Modules:
  0.0 50.8 jit_solution(3580552918958234871)
XLA Ops:
  0.0 2.1 %dynamic-slice_bitcast_fusion = bf16[1440,256]{1,0:T(8,128)(2,1)} fusion(bf16[2,1440,256]{2,1,0:T(8,128)(2,1)} %own, s32[]{:T(128)S(6)} %select_n.4), kind=kLoop, calls=%fused_computation | loop fusion | bytes 1474564 | tf_op jit(solution)/shard_map/squeeze | solution.py:245
  2.1 0.5 collective-permute-start
  2.6 0.1 collective-permute-start.4
  2.7 0.5 collective-permute-start.5
  3.1 1.5 %collective-permute-start.3 = (bf16[1440,256]{1,0:T(8,128)(2,1)}, bf16[1440,256]{1,0:T(8,128)(2,1)}, u32[]{:S(2)}, u32[]{:S(2)}) collective-permute-start(bf16[1440,256]{1,0:T(8,128)(2,1)} %dynamic-slice_bitcast_fusion), channel_id=1, source_target_pairs={{1,2},{2,1},{3,4},{4,3},{5,6},{6,5},{7,8},{8,7},{9,10},{10,9},{11,... | collective-permute-start | bytes 2211848 | tf_op jit(solution)/shard_map/ppermute | solution.py:246
  4.7 3.1 %collective-permute-start.6 = (bf16[512,512]{1,0:T(8,128)(2,1)}, bf16[512,512]{1,0:T(8,128)(2,1)}, u32[]{:S(2)}, u32[]{:S(2)}) collective-permute-start(bf16[512,512]{1,0:T(8,128)(2,1)} %refs_4_.1), channel_id=1, source_target_pairs={{0,1},{1,0},{2,3},{3,2},{4,5},{5,4},{6,7},{7,6},{8,9},{9,8},{10,11... | collective-permute-start | bytes 1572872 | tf_op jit(solution)/shard_map/ppermute | solution.py:270
  7.7 0.8 %dynamic-slice_bitcast_fusion.1 = bf16[880,256]{1,0:T(8,128)(2,1)} fusion(bf16[2,1440,256]{2,1,0:T(8,128)(2,1)S(1)} %collective-permute-done.other, s32[]{:T(128)S(6)} %select_n.4), kind=kLoop, calls=%fused_computation.1 | loop fusion | bytes 901124 | tf_op jit(solution)/shard_map/slice | solution.py:249
  8.5 1.4 %collective-permute-start.1 = (bf16[880,256]{1,0:T(8,128)(2,1)}, bf16[880,256]{1,0:T(8,128)(2,1)}, u32[]{:S(2)}, u32[]{:S(2)}) collective-permute-start(bf16[880,256]{1,0:T(8,128)(2,1)} %dynamic-slice_bitcast_fusion.1), channel_id=1, source_target_pairs={{1,2},{2,1},{3,4},{4,3},{5,6},{6,5},{7,8},{8,7},{9,10},{10,9},{11,... | collective-permute-start | bytes 1351688 | tf_op jit(solution)/shard_map/ppermute | solution.py:249
  10.0 0.0 collective-permute-done.5.refs_3_
  10.0 0.8 %collective-permute-start.2 = (bf16[560,256]{1,0:T(8,128)(2,1)S(1)}, bf16[560,256]{1,0:T(8,128)(2,1)S(1)}, u32[]{:S(2)}, u32[]{:S(2)}) collective-permute-start(bf16[560,256]{1,0:T(8,128)(2,1)S(1)} %dynamic-slice_bitcast_fusion.2), channel_id=1, source_target_pairs={{1,2},{2,1},{3,4},{4,3},{5,6},{6,5},{7,8},{8,7},{9,10},{10,9},{11,... | collective-permute-start | bytes 860168 | tf_op jit(solution)/shard_map/ppermute | solution.py:250
  10.8 0.0 copy-start.1
  10.8 1.7 %copy-done.1 = bf16[2,5,80,3,4,80]{5,4,3,2,1,0:T(4,128)(2,1)S(1)} copy-done((bf16[2,5,80,3,4,80]{5,4,3,2,1,0:T(4,128)(2,1)S(1)}, bf16[2,5,80,3,4,80]{5,4,3,2,1,0:T(4,128)(2,1)}, u32[]{:S(2)}) %copy-start.1) | copy-done | bytes 1536024
  12.5 2.0 %spread_filters.1 = (bf16[400,640]{1,0:T(8,128)(2,1)S(1)}, bf16[400,320]{1,0:T(8,128)(2,1)S(1)}) custom-call(s32[2,3]{1,0:T(2,128)S(1)} %copy-done.6, bf16[9600,80]{1,0:T(8,128)(2,1)S(1)} %bitcast.9), custom_call_target="tpu_custom_call" | custom-call | flops 1000 | bytes 1000 | tf_op jit(solution)/shard_map/spread_filters/pallas_call | solution.py:252
  14.6 0.0 copy-start.5
  14.6 1.7 %stage_weights.1 = (bf16[1280,512]{1,0:T(8,128)(2,1)S(1)}, bf16[1280,512]{1,0:T(8,128)(2,1)S(1)}, bf16[512,512]{1,0:T(8,128)(2,1)S(1)}, bf16[512,512]{1,0:T(8,12...) custom-call(bf16[1280,512]{1,0:T(8,128)(2,1)} %bitcast.4.refs_0_, ...), custom_call_target="tpu_custom_call" | custom-call | flops 1000 | bytes 1000 | tf_op jit(solution)/shard_map/stage_weights/pallas_call | solution.py:290
  16.3 7.2 %local_taps.1 = (f32[18,400,256]{2,1,0:T(8,128)S(1)}, f32[18,400,256]{2,1,0:T(8,128)S(1)}, f32[1440,512]{1,0:T(8,128)S(1)}) custom-call(s32[2,3]{1,0:T(2,128)S(1)} %copy-done.5, bf16[400,640]{1,0:T(8,128)(2,1)S(1)} %get-tuple-element.26.near, bf16[2,1440,256]{2,1,0:T(8,128)(2,1)S(1)} %copy-done, bf16[2,1440,256]{2,1,0:T(8,128)(2,1)S(1)} %collective-permute-done.other), custom_call_target="tpu_custom_call" | custom-call | flops 1000 | bytes 1000 | tf_op jit(solution)/shard_map/local_taps/pallas_call | solution.py:275
  23.5 5.5 %edge_tap_first_half.1.refs_3_.refs_6_ = f32[1440,512]{1,0:T(8,128)S(1)} custom-call(s32[2,3]{1,0:T(2,128)S(1)} %copy-done.5, bf16[1440,256]{1,0:T(8,128)(2,1)} %collective-permute-done.3.half, bf16[400,320]{1,0:T(8,128)(2,1)S(1)} %get-tuple-element.25.edge_filter.refs_1_.refs_4_, ...), custom_call_target="tpu_custom_call", output_to_operand_aliasing={{}: (5, {})} | custom-call | flops 1000 | bytes 1000 | tf_op jit(solution)/shard_map/edge_tap_first_half/pallas_call | solution.py:301
  29.1 4.4 %edge_tap_and_feed.2 = (bf16[640,256]{1,0:T(8,128)(2,1)S(1)}, bf16[640,256]{1,0:T(8,128)(2,1)S(1)}) custom-call(s32[2,3]{1,0:T(2,128)S(1)} %copy-done.5, bf16[880,256]{1,0:T(8,128)(2,1)} %collective-permute-done.1.refs_0_.refs_2_, bf16[400,320]{1,0:T(8,128)(2,1)S(1)} %get-tuple-element.25.edge_filter.refs_1_.refs_4_, ...), custom_call_target="tpu_custom_call" | custom-call | flops 1000 | bytes 1000 | tf_op jit(solution)/shard_map/edge_tap_and_feed/pallas_call | solution.py:327
  33.5 8.7 %collective-permute-start.7 = (bf16[640,256]{1,0:T(8,128)(2,1)S(1)}, bf16[640,256]{1,0:T(8,128)(2,1)S(1)}, u32[]{:S(2)}, u32[]{:S(2)}) collective-permute-start(bf16[640,256]{1,0:T(8,128)(2,1)S(1)} %get-tuple-element.39), channel_id=1, source_target_pairs={{0,1},{1,0},{2,3},{3,2},{4,5},{5,4},{6,7},{7,6},{8,9},{9,8},{10,11... | collective-permute-start | bytes 983048 | tf_op jit(solution)/shard_map/ppermute | solution.py:346
  42.2 5.3 %edge_tap_and_feed.3 = (bf16[800,256]{1,0:T(8,128)(2,1)S(1)}, bf16[800,256]{1,0:T(8,128)(2,1)S(1)}) custom-call(s32[2,3]{1,0:T(2,128)S(1)} %copy-done.5, bf16[880,256]{1,0:T(8,128)(2,1)} %collective-permute-done.1.refs_0_.refs_2_, bf16[560,256]{1,0:T(8,128)(2,1)S(1)} %collective-permute-done.2.refs_1_, ...), custom_call_target="tpu_custom_call" | custom-call | flops 10000000000 | bytes 1000 | tf_op jit(solution)/shard_map/edge_tap_and_feed/pallas_call | solution.py:327
  47.5 0.1 collective-permute-start.8
  47.6 1.6 %place_rows.1.before = bf16[2,1440,256]{2,1,0:T(8,128)(2,1)} custom-call(s32[2,3]{1,0:T(2,128)S(1)} %copy-done.5, bf16[640,256]{1,0:T(8,128)(2,1)S(1)} %get-tuple-element.37.refs_3_.refs_0_, bf16[800,256]{1,0:T(8,128)(2,1)S(1)} %get-tuple-element.41.refs_1_, bf16[640,256]{1,0:T(8,128)(2,1)S(1)} %collective-permute-done.7.refs_2_), custom_call_target="tpu_custom_call" | custom-call | flops 1000 | bytes 1000 | tf_op jit(solution)/shard_map/place_rows/pallas_call | solution.py:349
  49.2 0.1 collective-permute-done.8.source
  49.3 1.3 %place_last_rows.1 = bf16[2,1440,256]{2,1,0:T(8,128)(2,1)} custom-call(s32[2,3]{1,0:T(2,128)S(1)} %copy-done.5, bf16[800,256]{1,0:T(8,128)(2,1)S(1)} %collective-permute-done.8.source, bf16[2,1440,256]{2,1,0:T(8,128)(2,1)} %place_rows.1.before), custom_call_target="tpu_custom_call", output_to_operand_aliasing={{}: (2, {})} | custom-call | flops 1000 | bytes 1000 | tf_op jit(solution)/shard_map/place_last_rows/pallas_call | solution.py:363
  (19 shorter events, 0.1 us)
Async XLA Ops:
  0.0 2.1 %copy-start = (bf16[2,1440,256]{2,1,0:T(8,128)(2,1)S(1)}, bf16[2,1440,256]{2,1,0:T(8,128)(2,1)}, u32[]{:S(2)}) copy-start(bf16[2,1440,256]{2,1,0:T(8,128)(2,1)} %own) | copy-start | bytes 4423684
  0.0 10.8 %copy-start.6 = (s32[2,3]{1,0:T(2,128)S(1)}, s32[2,3]{1,0:T(2,128)}, u32[]{:S(2)}) copy-start(s32[2,3]{1,0:T(2,128)} %block_count.1) | copy-start | bytes 76
  2.1 5.6 %collective-permute-start = (bf16[2,1440,256]{2,1,0:T(8,128)(2,1)S(1)}, bf16[2,1440,256]{2,1,0:T(8,128)(2,1)S(1)}, u32[]{:S(2)}, u32[]{:S(2)}) collective-permute-start(bf16[2,1440,256]{2,1,0:T(8,128)(2,1)S(1)} %copy-done), channel_id=1, source_target_pairs={{0,1},{1,0},{2,3},{3,2},{4,5},{5,4},{6,7},{7,6},{8,9},{9,8},{10,11... | collective-permute-start | bytes 4423688 | tf_op jit(solution)/shard_map/ppermute | solution.py:247
  2.6 11.9 %collective-permute-start.4 = (bf16[5,256,512]{2,1,0:T(8,128)(2,1)}, bf16[5,256,512]{2,1,0:T(8,128)(2,1)}, u32[]{:S(2)}, u32[]{:S(2)}) collective-permute-start(bf16[5,256,512]{2,1,0:T(8,128)(2,1)} %param.11), channel_id=1, source_target_pairs={{0,1},{1,0},{2,3},{3,2},{4,5},{5,4},{6,7},{7,6},{8,9},{9,8},{10,11... | collective-permute-start | bytes 3932168 | tf_op jit(solution)/shard_map/ppermute | solution.py:268
  2.7 7.3 %collective-permute-start.5 = (bf16[512,512]{1,0:T(8,128)(2,1)}, bf16[512,512]{1,0:T(8,128)(2,1)}, u32[]{:S(2)}, u32[]{:S(2)}) collective-permute-start(bf16[512,512]{1,0:T(8,128)(2,1)} %refs_2_.1), channel_id=1, source_target_pairs={{0,1},{1,0},{2,3},{3,2},{4,5},{5,4},{6,7},{7,6},{8,9},{9,8},{10,11... | collective-permute-start | bytes 1572872 | tf_op jit(solution)/shard_map/ppermute | solution.py:269
  3.1 20.4 %collective-permute-start.3 = (bf16[1440,256]{1,0:T(8,128)(2,1)}, bf16[1440,256]{1,0:T(8,128)(2,1)}, u32[]{:S(2)}, u32[]{:S(2)}) collective-permute-start(bf16[1440,256]{1,0:T(8,128)(2,1)} %dynamic-slice_bitcast_fusion), channel_id=1, source_target_pairs={{1,2},{2,1},{3,4},{4,3},{5,6},{6,5},{7,8},{8,7},{9,10},{10,9},{11,... | collective-permute-start | bytes 2211848 | tf_op jit(solution)/shard_map/ppermute | solution.py:246
  4.7 9.9 %collective-permute-start.6 = (bf16[512,512]{1,0:T(8,128)(2,1)}, bf16[512,512]{1,0:T(8,128)(2,1)}, u32[]{:S(2)}, u32[]{:S(2)}) collective-permute-start(bf16[512,512]{1,0:T(8,128)(2,1)} %refs_4_.1), channel_id=1, source_target_pairs={{0,1},{1,0},{2,3},{3,2},{4,5},{5,4},{6,7},{7,6},{8,9},{9,8},{10,11... | collective-permute-start | bytes 1572872 | tf_op jit(solution)/shard_map/ppermute | solution.py:270
  7.7 6.8 %copy-start.4 = (bf16[512,512]{1,0:T(8,128)(2,1)S(1)}, bf16[512,512]{1,0:T(8,128)(2,1)}, u32[]{:S(2)}) copy-start(bf16[512,512]{1,0:T(8,128)(2,1)} %refs_4_.1) | copy-start | bytes 1572868
  8.5 20.5 %collective-permute-start.1 = (bf16[880,256]{1,0:T(8,128)(2,1)}, bf16[880,256]{1,0:T(8,128)(2,1)}, u32[]{:S(2)}, u32[]{:S(2)}) collective-permute-start(bf16[880,256]{1,0:T(8,128)(2,1)} %dynamic-slice_bitcast_fusion.1), channel_id=1, source_target_pairs={{1,2},{2,1},{3,4},{4,3},{5,6},{6,5},{7,8},{8,7},{9,10},{10,9},{11,... | collective-permute-start | bytes 1351688 | tf_op jit(solution)/shard_map/ppermute | solution.py:249
  10.0 4.6 %copy-start.3 = (bf16[512,512]{1,0:T(8,128)(2,1)S(1)}, bf16[512,512]{1,0:T(8,128)(2,1)}, u32[]{:S(2)}) copy-start(bf16[512,512]{1,0:T(8,128)(2,1)} %refs_2_.1) | copy-start | bytes 1572868
  10.0 32.2 %collective-permute-start.2 = (bf16[560,256]{1,0:T(8,128)(2,1)S(1)}, bf16[560,256]{1,0:T(8,128)(2,1)S(1)}, u32[]{:S(2)}, u32[]{:S(2)}) collective-permute-start(bf16[560,256]{1,0:T(8,128)(2,1)S(1)} %dynamic-slice_bitcast_fusion.2), channel_id=1, source_target_pairs={{1,2},{2,1},{3,4},{4,3},{5,6},{6,5},{7,8},{8,7},{9,10},{10,9},{11,... | collective-permute-start | bytes 860168 | tf_op jit(solution)/shard_map/ppermute | solution.py:250
  10.8 1.7 %copy-start.1 = (bf16[2,5,80,3,4,80]{5,4,3,2,1,0:T(4,128)(2,1)S(1)}, bf16[2,5,80,3,4,80]{5,4,3,2,1,0:T(4,128)(2,1)}, u32[]{:S(2)}) copy-start(bf16[2,5,80,3,4,80]{5,4,3,2,1,0:T(4,128)(2,1)} %param.8) | copy-start | bytes 4608004
  12.5 2.0 %copy-start.2 = (bf16[5,256,512]{2,1,0:T(8,128)(2,1)S(1)}, bf16[5,256,512]{2,1,0:T(8,128)(2,1)}, u32[]{:S(2)}) copy-start(bf16[5,256,512]{2,1,0:T(8,128)(2,1)} %param.11) | copy-start | bytes 3932164
  14.6 1.7 %copy-start.5 = (s32[2,3]{1,0:T(2,128)S(1)}, s32[2,3]{1,0:T(2,128)}, u32[]{:S(2)}) copy-start(s32[2,3]{1,0:T(2,128)} %starts.1) | copy-start | bytes 76
  33.5 14.0 %collective-permute-start.7 = (bf16[640,256]{1,0:T(8,128)(2,1)S(1)}, bf16[640,256]{1,0:T(8,128)(2,1)S(1)}, u32[]{:S(2)}, u32[]{:S(2)}) collective-permute-start(bf16[640,256]{1,0:T(8,128)(2,1)S(1)} %get-tuple-element.39), channel_id=1, source_target_pairs={{0,1},{1,0},{2,3},{3,2},{4,5},{5,4},{6,7},{7,6},{8,9},{9,8},{10,11... | collective-permute-start | bytes 983048 | tf_op jit(solution)/shard_map/ppermute | solution.py:346
  47.5 1.8 %collective-permute-start.8 = (bf16[800,256]{1,0:T(8,128)(2,1)S(1)}, bf16[800,256]{1,0:T(8,128)(2,1)S(1)}, u32[]{:S(2)}, u32[]{:S(2)}) collective-permute-start(bf16[800,256]{1,0:T(8,128)(2,1)S(1)} %get-tuple-element.40), channel_id=1, source_target_pairs={{0,1},{1,0},{2,3},{3,2},{4,5},{5,4},{6,7},{7,6},{8,9},{9,8},{10,11... | collective-permute-start | bytes 1228808 | tf_op jit(solution)/shard_map/ppermute | solution.py:346

commit v3 on v2

--- a/solution.py
+++ b/solution.py
@@ -31,8 +31,12 @@
     return pl.ds(pl.multiple_of(block * block_width, block_width), blocks * block_width)
 
 
+def wrap(block, lon_blocks):
+    return jnp.where(block >= lon_blocks, block - lon_blocks, block)
+
+
 def home_block(place, start, lon_blocks):
-    return lax.rem(place + lon_blocks - start, lon_blocks)
+    return jnp.where(place < start, place + lon_blocks - start, place - start)
 
 
 def spread_filters(basis, counts, core, filters, block_most):
@@ -71,11 +75,14 @@
 
 
 def local_kernel(
-    block_start, near, own, other, conv_own, conv_other, residual, window0, window1,
+    block_start, near, own_from, other, conv_own, conv_other, residual, own, window0, window1, sem,
     *, lon_blocks, block_width, block_most,
 ):
     core = lax.axis_index("chan")
     cells, width = own.shape[1:]
+    copy = pltpu.make_async_copy(own_from, own, sem)
+    copy.start()
+    copy.wait()
     for row, window in enumerate((window0, window1)):
         extra = window.shape[0] - cells
         for half, source in enumerate((own, other)):
@@ -94,25 +101,25 @@
 
     def group_step(group, carry):
         for slot in range(GROUP):
-            block = group * GROUP + slot
+            place = group * GROUP + slot
+            home = home_block(place, start, lon_blocks)
             parts = []
-            for window, start in zip((window0, window1), starts):
-                place = lax.rem(block + start, lon_blocks)
-                parts.append(window[block_rows(place, block_width, block_most), :])
+            for window, tap_start in zip((window0, window1), starts):
+                source = wrap(home + tap_start, lon_blocks)
+                parts.append(window[block_rows(source, block_width, block_most), :])
             result = jnp.dot(near[...], jnp.concatenate(parts, axis=0), preferred_element_type=jnp.float32)
-            conv_own[block] = result[:, :width]
-            conv_other[block] = result[:, width:]
+            conv_own[place] = result[:, :width]
+            conv_other[place] = result[:, width:]
         return carry
 
     lax.fori_loop(0, lon_blocks // GROUP, group_step, 0)
 
 
-def halo_conv(first, places, start, lon_blocks, block_width, window, edge_filter, conv_local, conv):
+def halo_conv(first, places, block_width, window, edge_filter, conv_local, conv):
     depth = edge_filter.shape[1]
     width = window.shape[1]
     for slot in range(places):
-        home = home_block(first + slot, start, lon_blocks)
-        result = conv_local[home] + jnp.dot(
+        result = conv_local[first + slot] + jnp.dot(
             edge_filter[...], window[slot * block_width : slot * block_width + depth, :],
             preferred_element_type=jnp.float32,
         )
@@ -123,19 +130,14 @@
             ] = rounded[basis * block_width : (basis + 1) * block_width]
 
 
-def first_half_kernel(
-    block_start, half, edge_filter, conv_local, mix, residual, result, window, conv, *, lon_blocks, block_width
-):
-    core = lax.axis_index("chan")
-    start = halo_start(block_start, core)
+def first_half_kernel(half, edge_filter, conv_local, mix, residual, result, window, conv, *, block_width):
     cells = half.shape[0]
     window[:cells, :] = half[...]
     window[cells:, :] = half[: window.shape[0] - cells, :]
     rows = GROUP * block_width
-    for group in range(lon_blocks // GROUP):
+    for group in range(cells // rows):
         halo_conv(
-            group * GROUP, GROUP, start, lon_blocks, block_width,
-            window.at[group * rows :, :], edge_filter, conv_local, conv,
+            group * GROUP, GROUP, block_width, window.at[group * rows :, :], edge_filter, conv_local, conv
         )
         here = slice(group * rows, (group + 1) * rows)
         result[here, :] = residual[here, :] + jnp.dot(conv[...], mix[...], preferred_element_type=jnp.float32)
@@ -145,17 +147,16 @@
     return 0.5 * x * (1.0 + lax.erf(x * 0.7071067811865476))
 
 
-def tail_kernel(block_start, *refs, first, places, lon_blocks, block_width, pieces, ordered):
+def tail_kernel(*refs, first, places, block_width, pieces, ordered):
     halves, refs = refs[: len(pieces)], refs[len(pieces) + ordered :]
     (edge_filter, conv_local, partial, mix, up, up_other, down, down_other, keep, send, window, conv) = refs
     core = lax.axis_index("chan")
-    start = halo_start(block_start, core)
     width = window.shape[1]
     at = 0
     for half, (low, high) in zip(halves, pieces):
         window[at : at + high - low, :] = half[low:high, :]
         at += high - low
-    halo_conv(first, places, start, lon_blocks, block_width, window, edge_filter, conv_local, conv)
+    halo_conv(first, places, block_width, window, edge_filter, conv_local, conv)
     mixed = jnp.dot(conv[...], mix[...], preferred_element_type=jnp.float32)
     state = partial[first * block_width : (first + places) * block_width, :] + mixed
     rounded = state.astype(jnp.bfloat16)
@@ -183,28 +184,63 @@
     jobs = []
     for index, (source, first) in enumerate(zip(refs, kept + received)):
         row = core if index < len(kept) else 1 - core
-        places = source.shape[0] // block_width
         home = home_block(first, halo_start(block_start, row), lon_blocks)
-        before_wrap = jnp.minimum(lon_blocks - home, places)
-        for count in range(1, places + 1):
-            size = count * block_width
-            copies = [pltpu.make_async_copy(
-                source.at[:size, :], result.at[row, block_rows(home, block_width, count), :], sems.at[index, 0]
-            )]
-            if count < places:
-                copies.append(pltpu.make_async_copy(
-                    source.at[size:, :], result.at[row, : source.shape[0] - size, :], sems.at[index, 1]
-                ))
-            jobs.append((before_wrap == count, copies))
-    for started in (True, False):
-        for chosen, copies in jobs:
-
-            @pl.when(chosen)
-            def _():
-                if started:
-                    start_all(copies)
-                else:
-                    wait_all(copies)
+        jobs.append((source, row, home, source.shape[0] // block_width, sems.at[index]))
+
+    def begin(job, count):
+        source, row, home, places, sem = job
+        size = count * block_width
+        pltpu.make_async_copy(
+            source.at[:size, :], result.at[row, block_rows(home, block_width, count), :], sem
+        ).start()
+        if count < places:
+            pltpu.make_async_copy(
+                source.at[size:, :], result.at[row, : source.shape[0] - size, :], sem
+            ).start()
+
+    def choose(job, low, high):
+        if low == high:
+            begin(job, low)
+            return
+        middle = (low + high) // 2
+        early = lon_blocks - job[2] <= middle
+        pl.when(early)(lambda: choose(job, low, middle))
+        pl.when(jnp.logical_not(early))(lambda: choose(job, middle + 1, high))
+
+    for job in jobs:
+        choose(job, 1, job[3])
+    for source, row, _, _, sem in jobs:
+        pltpu.make_async_copy(source, result.at[row, : source.shape[0], :], sem).wait()
+
+
+def relay_kernel(other, first, last):
+    core = lax.axis_index("chan")
+    cut = first.shape[0]
+    first[...] = other[core, :cut, :]
+    last[...] = other[core, cut:, :]
+
+
+def edge_kernel(rows, result, sem):
+    copy = pltpu.make_async_copy(rows.at[lax.axis_index("chan")], result, sem)
+    copy.start()
+    copy.wait()
+
+
+def edge_row(rows):
+    return pl.pallas_call(
+        edge_kernel,
+        out_shape=pltpu.VMEM(rows.shape[1:], rows.dtype),
+        in_specs=anywhere(1),
+        out_specs=vmem(1)[0],
+        scratch_shapes=[pltpu.SemaphoreType.DMA],
+        compiler_params=limit(4),
+        cost_estimate=cost(),
+        name="edge_row",
+    )(in_hbm(rows))
+
+
+def in_hbm(array):
+    return pltpu.with_memory_space_constraint(array, pltpu.HBM)
 
 
 def limit(mebibytes):
@@ -242,12 +278,19 @@
     sizes = dict(block_width=block_width, lon_blocks=lon_blocks)
     smem = [pl.BlockSpec(memory_space=pltpu.SMEM)]
     cut = (FIRST + block_most - 1) * block_width
-    edge, state_in = lax.optimization_barrier((state_in[core], state_in))
+    edge = edge_row(state_in)
     halo_other = lax.ppermute(edge, ("lat", "chan"), pairs)
     other = lax.ppermute(state_in, "chan", swap)
-    relay = other[core]
-    halo_first = lax.ppermute(relay[:cut], ("lat", "chan"), pairs)
-    halo_last = lax.ppermute(relay[cut:], ("lat", "chan"), pairs)
+    relay = pl.pallas_call(
+        relay_kernel,
+        out_shape=[jax.ShapeDtypeStruct((rows, width), state_in.dtype) for rows in (cut, cells - cut)],
+        in_specs=vmem(1),
+        out_specs=vmem(2),
+        compiler_params=limit(4),
+        cost_estimate=cost(),
+        name="relay_rows",
+    )(other)
+    halo_first, halo_last = [lax.ppermute(rows, ("lat", "chan"), pairs) for rows in relay]
     basis_flat = basis_blocks.reshape(local_rows * filter_rows * taps * block_most, block_width)
     near_filter, edge_filter = pl.pallas_call(
         functools.partial(filter_kernel, block_most=block_most),
@@ -264,7 +307,7 @@
         compiler_params=limit(8),
         cost_estimate=cost(),
         name="spread_filters",
-    )(block_count, basis_flat)
+    )(block_count, in_hbm(basis_flat))
     mix_other = lax.ppermute(mix_weight, "chan", swap)
     up_other = lax.ppermute(up_weight, "chan", swap)
     down_other = lax.ppermute(down_weight, "chan", swap)
@@ -275,17 +318,20 @@
     conv_own, conv_other, residual = pl.pallas_call(
         functools.partial(local_kernel, block_most=block_most, **sizes),
         out_shape=(conv_shape, conv_shape, state_shape),
-        in_specs=smem + vmem(3),
+        in_specs=smem + vmem(1) + anywhere(1) + vmem(1),
         out_specs=vmem(3),
-        scratch_shapes=[wide_window, wide_window],
+        scratch_shapes=[
+            pltpu.VMEM(state_in.shape, state_in.dtype), wide_window, wide_window, pltpu.SemaphoreType.DMA
+        ],
         compiler_params=limit(14),
         cost_estimate=cost(),
         name="local_taps",
-    )(block_start, near_filter, state_in, other)
+    )(block_start, near_filter, in_hbm(state_in), other)
 
     weights = (
-        mix_other.reshape(basis_count * width, channels), mix_weight.reshape(basis_count * width, channels),
-        up_weight, up_other, down_weight, down_other,
+        mix_other.reshape(basis_count * width, channels),
+        in_hbm(mix_weight.reshape(basis_count * width, channels)),
+        in_hbm(up_weight), up_other, in_hbm(down_weight), down_other,
     )
     mix_other, *weights = pl.pallas_call(
         stage_kernel,
@@ -299,19 +345,19 @@
     )(*weights)
 
     partial = pl.pallas_call(
-        functools.partial(first_half_kernel, **sizes),
+        functools.partial(first_half_kernel, block_width=block_width),
         out_shape=state_shape,
-        in_specs=smem + vmem(5),
+        in_specs=vmem(5),
         out_specs=vmem(1)[0],
         scratch_shapes=[
             pltpu.VMEM((cells + depth - block_width, width), jnp.bfloat16),
             pltpu.VMEM((GROUP * block_width, basis_count * width), jnp.bfloat16),
         ],
-        input_output_aliases={5: 0},
+        input_output_aliases={4: 0},
         compiler_params=limit(14),
         cost_estimate=cost(),
         name="edge_tap_first_half",
-    )(block_start, halo_other, edge_filter, conv_other, mix_other, residual)
+    )(halo_other, edge_filter, conv_other, mix_other, residual)
 
     overlap = (block_most - 1) * block_width
     plans = (
@@ -326,10 +372,10 @@
         half = jax.ShapeDtypeStruct((places * block_width, width), jnp.bfloat16)
         keep, send = pl.pallas_call(
             functools.partial(
-                tail_kernel, first=first, places=places, pieces=pieces, ordered=len(done), **sizes
+                tail_kernel, first=first, places=places, pieces=pieces, ordered=len(done), block_width=block_width
             ),
             out_shape=(half, half),
-            in_specs=smem + vmem(len(pieces)) + anywhere(len(done)) + vmem(8),
+            in_specs=vmem(len(pieces)) + anywhere(len(done)) + vmem(8),
             out_specs=vmem(2),
             scratch_shapes=[
                 pltpu.VMEM(((places + block_most - 1) * block_width, width), jnp.bfloat16),
@@ -338,7 +384,7 @@
             compiler_params=limit(14),
             cost_estimate=cost(10**10 if done else 1000),
             name="edge_tap_and_feed",
-        )(block_start, *halves, *done, edge_filter, conv_own, partial, *weights)
+        )(*halves, *done, edge_filter, conv_own, partial, *weights)
         if received:
             send, received[-1] = lax.optimization_barrier((send, received[-1]))
         kept.append(keep)
@@ -351,7 +397,7 @@
         out_shape=result,
         in_specs=smem + vmem(3),
         out_specs=anywhere(1)[0],
-        scratch_shapes=[pltpu.SemaphoreType.DMA((3, 2))],
+        scratch_shapes=[pltpu.SemaphoreType.DMA((3,))],
         cost_estimate=cost(),
         compiler_params=limit(4),
         name="place_rows",
@@ -365,7 +411,7 @@
         out_shape=result,
         in_specs=smem + vmem(1) + anywhere(1),
         out_specs=anywhere(1)[0],
-        scratch_shapes=[pltpu.SemaphoreType.DMA((1, 2))],
+        scratch_shapes=[pltpu.SemaphoreType.DMA((1,))],
         input_output_aliases={2: 0},
         cost_estimate=cost(),
         compiler_params=limit(4),

time: 51.7 us -> 47.1 us (0.911)
  local copies, waits for them, and re-layouts: 4.69 us -> 0.01 us
    pallas_call x2, Pallas kernels: 9.71 us -> 7.48 us  [per_device(): pl.pallas_call(functools.partial(tail_kernel, first=first, places=places,...]
    squeeze x1 -> x0, local copies, waits for them, and re-layouts: 2.14 us -> none  [per_device(): edge, state_in = lax.optimization_barrier((state_in[core], state_in))]
    unnamed x14 -> x6, local copies, waits for them, and re-layouts: 1.71 us -> 0.01 us
    pallas_call x1, Pallas kernels: 7.23 us -> 8.48 us  [per_device(): pl.pallas_call(functools.partial(local_kernel, block_most=block_most, **s...]
    ppermute x2, starting transfers between devices: 8.79 us -> 9.87 us  [per_device(): received.append(lax.ppermute(send, 'chan', swap))]
    pallas_call x1, Pallas kernels: 1.96 us -> 2.95 us  [per_device(): pl.pallas_call(functools.partial(filter_kernel, block_most=block_most), o...]
    ppermute x1, starting transfers between devices: 3.06 us -> 3.97 us  [per_device(): down_other = lax.ppermute(down_weight, 'chan', swap)]
    ppermute x2, starting transfers between devices: 2.24 us -> 1.37 us  [per_device(): lax.ppermute(rows, ('lat', 'chan'), pairs)]
  transfers between devices with their start and end apart: 9 -> 9, of which waited for: 1 -> 1; matrix products, arithmetic and copies ran while one was open for 2% -> 0% of each run, Pallas kernels for 55% -> 60%
where the time goes in v3:
time: 47.1 us; the launch traced here: 46.5 us
  Pallas kernels  29.2 us (62%)
  starting transfers between devices  16.9 us (36%)
    ppermute x2, starting transfers between devices, per_device(): received.append(lax.ppermute(send, 'chan', swap))  9.87 us
    pallas_call x1, Pallas kernels, per_device(): pl.pallas_call(functools.partial(local_kernel, block_most=block_most, **s...  8.48 us
    pallas_call x2, Pallas kernels, per_device(): pl.pallas_call(functools.partial(tail_kernel, first=first, places=places,...  7.48 us
    pallas_call x1, Pallas kernels, per_device(): pl.pallas_call(functools.partial(first_half_kernel, block_width=block_wid...  4.48 us
    ppermute x1, starting transfers between devices, per_device(): down_other = lax.ppermute(down_weight, 'chan', swap)  3.97 us
    pallas_call x1, Pallas kernels, per_device(): pl.pallas_call(functools.partial(filter_kernel, block_most=block_most), o...  2.95 us
    pallas_call x1, Pallas kernels, per_device(): pl.pallas_call(stage_kernel, out_shape=[jax.ShapeDtypeStruct(array.shape,...  1.74 us
    pallas_call x1, Pallas kernels, per_device(): pl.pallas_call(functools.partial(place_kernel, kept=[0, FIRST], received=...  1.58 us
  transfers between devices with their start and end apart: 9, of which 1 were waited for; matrix products, arithmetic and copies ran while one was open for 0% of the time, Pallas kernels for 60%

profile of v3, /device:TPU:0, one launch (start us, length us, event | category | flops | bytes accessed | tf_op | source)
XLA Modules:
  0.0 46.5 jit_solution(1583276585982394562)
XLA Ops:
  0.0 0.5 collective-permute-start
  0.5 0.1 collective-permute-start.4
  0.5 0.4 collective-permute-start.5
  1.0 1.1 %edge_row.1 = bf16[1440,256]{1,0:T(8,128)(2,1)S(1)} custom-call(bf16[2,1440,256]{2,1,0:T(8,128)(2,1)} %rows.1), custom_call_target="tpu_custom_call" | custom-call | flops 1000 | bytes 1000 | tf_op jit(solution)/shard_map/edge_row/pallas_call | solution.py:230
  2.1 0.7 %collective-permute-start.3 = (bf16[1440,256]{1,0:T(8,128)(2,1)S(1)}, bf16[1440,256]{1,0:T(8,128)(2,1)S(1)}, u32[]{:S(2)}, u32[]{:S(2)}) collective-permute-start(bf16[1440,256]{1,0:T(8,128)(2,1)S(1)} %edge_row.1), channel_id=1, source_target_pairs={{1,2},{2,1},{3,4},{4,3},{5,6},{6,5},{7,8},{8,7},{9,10},{10,9},{11,... | collective-permute-start | bytes 2211848 | tf_op jit(solution)/shard_map/ppermute | solution.py:282
  2.8 4.0 %collective-permute-start.6 = (bf16[512,512]{1,0:T(8,128)(2,1)S(1)}, bf16[512,512]{1,0:T(8,128)(2,1)S(1)}, u32[]{:S(2)}, u32[]{:S(2)}) collective-permute-start(bf16[512,512]{1,0:T(8,128)(2,1)S(1)} %copy-done.2), channel_id=1, source_target_pairs={{0,1},{1,0},{2,3},{3,2},{4,5},{5,4},{6,7},{7,6},{8,9},{9,8},{10,11... | collective-permute-start | bytes 1572872 | tf_op jit(solution)/shard_map/ppermute | solution.py:313
  6.8 0.0 collective-permute-done.other
  6.9 0.7 %collective-permute-start.1 = (bf16[880,256]{1,0:T(8,128)(2,1)S(1)}, bf16[880,256]{1,0:T(8,128)(2,1)S(1)}, u32[]{:S(2)}, u32[]{:S(2)}) collective-permute-start(bf16[880,256]{1,0:T(8,128)(2,1)S(1)} %get-tuple-element.24), channel_id=1, source_target_pairs={{1,2},{2,1},{3,4},{4,3},{5,6},{6,5},{7,8},{8,7},{9,10},{10,9},{11,... | collective-permute-start | bytes 1351688 | tf_op jit(solution)/shard_map/ppermute | solution.py:293
  7.6 0.7 %collective-permute-start.2 = (bf16[560,256]{1,0:T(8,128)(2,1)S(1)}, bf16[560,256]{1,0:T(8,128)(2,1)S(1)}, u32[]{:S(2)}, u32[]{:S(2)}) collective-permute-start(bf16[560,256]{1,0:T(8,128)(2,1)S(1)} %get-tuple-element.25), channel_id=1, source_target_pairs={{1,2},{2,1},{3,4},{4,3},{5,6},{6,5},{7,8},{8,7},{9,10},{10,9},{11,... | collective-permute-start | bytes 860168 | tf_op jit(solution)/shard_map/ppermute | solution.py:293
  8.3 2.9 %spread_filters.1 = (bf16[400,640]{1,0:T(8,128)(2,1)S(1)}, bf16[400,320]{1,0:T(8,128)(2,1)S(1)}) custom-call(s32[2,3]{1,0:T(2,128)S(1)} %copy-done.1, bf16[9600,80]{1,0:T(8,128)(2,1)} %bitcast.4), custom_call_target="tpu_custom_call" | custom-call | flops 1000 | bytes 1000 | tf_op jit(solution)/shard_map/spread_filters/pallas_call | solution.py:295
  11.2 0.0 collective-permute-done.4
  11.2 0.0 copy-start
  11.2 1.7 %stage_weights.1 = (bf16[1280,512]{1,0:T(8,128)(2,1)S(1)}, bf16[1280,512]{1,0:T(8,128)(2,1)S(1)}, bf16[512,512]{1,0:T(8,128)(2,1)S(1)}, bf16[512,512]{1,0:T(8,12...) custom-call(bf16[1280,512]{1,0:T(8,128)(2,1)S(1)} %bitcast.3, bf16[1280,512]{1,0:T(8,128)(2,1)} %bitcast.5, ...), custom_call_target="tpu_custom_call" | custom-call | flops 1000 | bytes 1000 | tf_op jit(solution)/shard_map/stage_weights/pallas_call | solution.py:336
  13.0 8.5 %local_taps.1 = (f32[18,400,256]{2,1,0:T(8,128)S(1)}, f32[18,400,256]{2,1,0:T(8,128)S(1)}, f32[1440,512]{1,0:T(8,128)S(1)}) custom-call(s32[2,3]{1,0:T(2,128)S(1)} %copy-done, bf16[400,640]{1,0:T(8,128)(2,1)S(1)} %get-tuple-element.27.near, bf16[2,1440,256]{2,1,0:T(8,128)(2,1)} %rows.1, bf16[2,1440,256]{2,1,0:T(8,128)(2,1)S(1)} %collective-permute-done.other), custom_call_target="tpu_custom_call" | custom-call | flops 1000 | bytes 1000 | tf_op jit(solution)/shard_map/local_taps/pallas_call | solution.py:318
  21.5 0.0 collective-permute-done.3.half
  21.5 4.5 %edge_tap_first_half.1.refs_3_.refs_6_ = f32[1440,512]{1,0:T(8,128)S(1)} custom-call(bf16[1440,256]{1,0:T(8,128)(2,1)S(1)} %collective-permute-done.3.half, bf16[400,320]{1,0:T(8,128)(2,1)S(1)} %get-tuple-element.26.edge_filter.refs_1_.refs_4_, f32[18,400,256]{2,1,0:T(8,128)S(1)} %get-tuple-element.29.conv_local, ...), custom_call_target="tpu_custom_call", output_to_operand_aliasing={{}: (4, {})} | custom-call | flops 1000 | bytes 1000 | tf_op jit(solution)/shard_map/edge_tap_first_half/pallas_call | solution.py:347
  26.0 3.3 %edge_tap_and_feed.2 = (bf16[640,256]{1,0:T(8,128)(2,1)S(1)}, bf16[640,256]{1,0:T(8,128)(2,1)S(1)}) custom-call(bf16[880,256]{1,0:T(8,128)(2,1)S(1)} %collective-permute-done.1.refs_0_.refs_2_, bf16[400,320]{1,0:T(8,128)(2,1)S(1)} %get-tuple-element.26.edge_filter.refs_1_.refs_4_, f32[18,400,256]{2,1,0:T(8,128)S(1)} %get-tuple-element.28.refs_2_.refs_5_, ...), custom_call_target="tpu_custom_call" | custom-call | flops 1000 | bytes 1000 | tf_op jit(solution)/shard_map/edge_tap_and_feed/pallas_call | solution.py:373
  29.4 9.8 %collective-permute-start.7 = (bf16[640,256]{1,0:T(8,128)(2,1)S(1)}, bf16[640,256]{1,0:T(8,128)(2,1)S(1)}, u32[]{:S(2)}, u32[]{:S(2)}) collective-permute-start(bf16[640,256]{1,0:T(8,128)(2,1)S(1)} %get-tuple-element.39), channel_id=1, source_target_pairs={{0,1},{1,0},{2,3},{3,2},{4,5},{5,4},{6,7},{7,6},{8,9},{9,8},{10,11... | collective-permute-start | bytes 983048 | tf_op jit(solution)/shard_map/ppermute | solution.py:392
  39.1 0.0 collective-permute-done.2.refs_1_
  39.2 4.1 %edge_tap_and_feed.3 = (bf16[800,256]{1,0:T(8,128)(2,1)S(1)}, bf16[800,256]{1,0:T(8,128)(2,1)S(1)}) custom-call(bf16[880,256]{1,0:T(8,128)(2,1)S(1)} %collective-permute-done.1.refs_0_.refs_2_, bf16[560,256]{1,0:T(8,128)(2,1)S(1)} %collective-permute-done.2.refs_1_, bf16[880,256]{1,0:T(8,128)(2,1)S(1)} %collective-permute-done.1.refs_0_.refs_2_, ...), custom_call_target="tpu_custom_call" | custom-call | flops 10000000000 | bytes 1000 | tf_op jit(solution)/shard_map/edge_tap_and_feed/pallas_call | solution.py:373
  43.3 0.1 collective-permute-start.8
  43.4 1.6 %place_rows.1.before = bf16[2,1440,256]{2,1,0:T(8,128)(2,1)} custom-call(s32[2,3]{1,0:T(2,128)S(1)} %copy-done, bf16[640,256]{1,0:T(8,128)(2,1)S(1)} %get-tuple-element.37.refs_3_.refs_0_, bf16[800,256]{1,0:T(8,128)(2,1)S(1)} %get-tuple-element.41.refs_1_, bf16[640,256]{1,0:T(8,128)(2,1)S(1)} %collective-permute-done.7.refs_2_), custom_call_target="tpu_custom_call" | custom-call | flops 1000 | bytes 1000 | tf_op jit(solution)/shard_map/place_rows/pallas_call | solution.py:395
  45.0 0.1 collective-permute-done.8.source
  45.1 1.3 %place_last_rows.1 = bf16[2,1440,256]{2,1,0:T(8,128)(2,1)} custom-call(s32[2,3]{1,0:T(2,128)S(1)} %copy-done, bf16[800,256]{1,0:T(8,128)(2,1)S(1)} %collective-permute-done.8.source, bf16[2,1440,256]{2,1,0:T(8,128)(2,1)} %place_rows.1.before), custom_call_target="tpu_custom_call", output_to_operand_aliasing={{}: (2, {})} | custom-call | flops 1000 | bytes 1000 | tf_op jit(solution)/shard_map/place_last_rows/pallas_call | solution.py:409
  (10 shorter events, 0.1 us)
Async XLA Ops:
  0.0 2.8 %copy-start.2 = (bf16[512,512]{1,0:T(8,128)(2,1)S(1)}, bf16[512,512]{1,0:T(8,128)(2,1)}, u32[]{:S(2)}) copy-start(bf16[512,512]{1,0:T(8,128)(2,1)} %refs_4_.1) | copy-start | bytes 1572868
  0.0 8.2 %copy-start.1 = (s32[2,3]{1,0:T(2,128)S(1)}, s32[2,3]{1,0:T(2,128)}, u32[]{:S(2)}) copy-start(s32[2,3]{1,0:T(2,128)} %block_count.1) | copy-start | bytes 76
  0.0 6.8 %collective-permute-start = (bf16[2,1440,256]{2,1,0:T(8,128)(2,1)}, bf16[2,1440,256]{2,1,0:T(8,128)(2,1)S(1)}, u32[]{:S(2)}, u32[]{:S(2)}) collective-permute-start(bf16[2,1440,256]{2,1,0:T(8,128)(2,1)} %rows.1), channel_id=1, source_target_pairs={{0,1},{1,0},{2,3},{3,2},{4,5},{5,4},{6,7},{7,6},{8,9},{9,8},{10,11... | collective-permute-start | bytes 4423688 | tf_op jit(solution)/shard_map/ppermute | solution.py:283
  0.5 10.8 %collective-permute-start.4 = (bf16[5,256,512]{2,1,0:T(8,128)(2,1)}, bf16[5,256,512]{2,1,0:T(8,128)(2,1)S(1)}, u32[]{:S(2)}, u32[]{:S(2)}) collective-permute-start(bf16[5,256,512]{2,1,0:T(8,128)(2,1)} %param.11), channel_id=1, source_target_pairs={{0,1},{1,0},{2,3},{3,2},{4,5},{5,4},{6,7},{7,6},{8,9},{9,8},{10,11... | collective-permute-start | bytes 3932168 | tf_op jit(solution)/shard_map/ppermute | solution.py:311
  0.5 7.0 %collective-permute-start.5 = (bf16[512,512]{1,0:T(8,128)(2,1)}, bf16[512,512]{1,0:T(8,128)(2,1)S(1)}, u32[]{:S(2)}, u32[]{:S(2)}) collective-permute-start(bf16[512,512]{1,0:T(8,128)(2,1)} %refs_2_.1), channel_id=1, source_target_pairs={{0,1},{1,0},{2,3},{3,2},{4,5},{5,4},{6,7},{7,6},{8,9},{9,8},{10,11... | collective-permute-start | bytes 1572872 | tf_op jit(solution)/shard_map/ppermute | solution.py:312
  2.1 19.4 %collective-permute-start.3 = (bf16[1440,256]{1,0:T(8,128)(2,1)S(1)}, bf16[1440,256]{1,0:T(8,128)(2,1)S(1)}, u32[]{:S(2)}, u32[]{:S(2)}) collective-permute-start(bf16[1440,256]{1,0:T(8,128)(2,1)S(1)} %edge_row.1), channel_id=1, source_target_pairs={{1,2},{2,1},{3,4},{4,3},{5,6},{6,5},{7,8},{8,7},{9,10},{10,9},{11,... | collective-permute-start | bytes 2211848 | tf_op jit(solution)/shard_map/ppermute | solution.py:282
  2.8 8.4 %collective-permute-start.6 = (bf16[512,512]{1,0:T(8,128)(2,1)S(1)}, bf16[512,512]{1,0:T(8,128)(2,1)S(1)}, u32[]{:S(2)}, u32[]{:S(2)}) collective-permute-start(bf16[512,512]{1,0:T(8,128)(2,1)S(1)} %copy-done.2), channel_id=1, source_target_pairs={{0,1},{1,0},{2,3},{3,2},{4,5},{5,4},{6,7},{7,6},{8,9},{9,8},{10,11... | collective-permute-start | bytes 1572872 | tf_op jit(solution)/shard_map/ppermute | solution.py:313
  6.9 19.1 %collective-permute-start.1 = (bf16[880,256]{1,0:T(8,128)(2,1)S(1)}, bf16[880,256]{1,0:T(8,128)(2,1)S(1)}, u32[]{:S(2)}, u32[]{:S(2)}) collective-permute-start(bf16[880,256]{1,0:T(8,128)(2,1)S(1)} %get-tuple-element.24), channel_id=1, source_target_pairs={{1,2},{2,1},{3,4},{4,3},{5,6},{6,5},{7,8},{8,7},{9,10},{10,9},{11,... | collective-permute-start | bytes 1351688 | tf_op jit(solution)/shard_map/ppermute | solution.py:293
  7.6 31.6 %collective-permute-start.2 = (bf16[560,256]{1,0:T(8,128)(2,1)S(1)}, bf16[560,256]{1,0:T(8,128)(2,1)S(1)}, u32[]{:S(2)}, u32[]{:S(2)}) collective-permute-start(bf16[560,256]{1,0:T(8,128)(2,1)S(1)} %get-tuple-element.25), channel_id=1, source_target_pairs={{1,2},{2,1},{3,4},{4,3},{5,6},{6,5},{7,8},{8,7},{9,10},{10,9},{11,... | collective-permute-start | bytes 860168 | tf_op jit(solution)/shard_map/ppermute | solution.py:293
  11.2 1.8 %copy-start = (s32[2,3]{1,0:T(2,128)S(1)}, s32[2,3]{1,0:T(2,128)}, u32[]{:S(2)}) copy-start(s32[2,3]{1,0:T(2,128)} %starts.1) | copy-start | bytes 76
  29.4 13.9 %collective-permute-start.7 = (bf16[640,256]{1,0:T(8,128)(2,1)S(1)}, bf16[640,256]{1,0:T(8,128)(2,1)S(1)}, u32[]{:S(2)}, u32[]{:S(2)}) collective-permute-start(bf16[640,256]{1,0:T(8,128)(2,1)S(1)} %get-tuple-element.39), channel_id=1, source_target_pairs={{0,1},{1,0},{2,3},{3,2},{4,5},{5,4},{6,7},{7,6},{8,9},{9,8},{10,11... | collective-permute-start | bytes 983048 | tf_op jit(solution)/shard_map/ppermute | solution.py:392
  43.3 1.8 %collective-permute-start.8 = (bf16[800,256]{1,0:T(8,128)(2,1)S(1)}, bf16[800,256]{1,0:T(8,128)(2,1)S(1)}, u32[]{:S(2)}, u32[]{:S(2)}) collective-permute-start(bf16[800,256]{1,0:T(8,128)(2,1)S(1)} %get-tuple-element.40), channel_id=1, source_target_pairs={{0,1},{1,0},{2,3},{3,2},{4,5},{5,4},{6,7},{7,6},{8,9},{9,8},{10,11... | collective-permute-start | bytes 1228808 | tf_op jit(solution)/shard_map/ppermute | solution.py:392

commit v4 on v3

v4 whole, which is shorter than its diff:
```python
import functools

import jax
import jax.numpy as jnp
from jax import lax
from jax.experimental import pallas as pl
from jax.experimental.pallas import tpu as pltpu
from jax.sharding import PartitionSpec as P

GROUP = 9
TILE = 16
FIRST_CUTS = (0, 11, 18)
LAST_CUTS = (0, 8, 13, 18)


def start_all(copies):
    for copy in copies:
        copy.start()
    return copies


def wait_all(copies):
    for copy in copies:
        copy.wait()


def halo_start(block_start, core):
    return block_start[core, 2 * core]


def block_rows(block, block_width, blocks=1):
    return pl.ds(pl.multiple_of(block * block_width, block_width), blocks * block_width)


def wrap(block, lon_blocks):
    return jnp.where(block >= lon_blocks, block - lon_blocks, block)


def home_block(place, start, lon_blocks):
    return jnp.where(place < start, place + lon_blocks - start, place - start)


def spread_filters(basis, counts, core, filters, block_most):
    rows_out, taps, width = filters.shape[1], filters.shape[0], basis.shape[1]
    pieces = taps * block_most
    size = TILE * pieces
    row = lax.broadcasted_iota(jnp.int32, (size, size), 0)
    column = lax.broadcasted_iota(jnp.int32, (size, size), 1)
    order = (column == lax.rem(row, TILE) * pieces + row // TILE).astype(jnp.float32).astype(jnp.bfloat16)
    for tile in range(rows_out // TILE):
        sorted_rows = jnp.dot(
            order, basis[tile * size : (tile + 1) * size, :], preferred_element_type=jnp.float32
        ).astype(jnp.bfloat16)
        for tap in range(taps):
            for block in range(block_most):
                at = (tap * block_most + block) * TILE
                piece = sorted_rows[at : at + TILE]
                filters[tap, tile * TILE : (tile + 1) * TILE, block * width : (block + 1) * width] = (
                    jnp.where(block < counts[core, tap], piece, jnp.zeros_like(piece))
                )


def stage_weights(core, sources, targets, sem, width):
    (mix, mix_other, up, up_other, down, down_other) = sources
    (mix_to, mix_other_to, up_to, down_to) = targets
    pairs = []
    for place, half in enumerate((core, 1 - core)):
        theirs = pl.ds(pl.multiple_of(half * width, width), width)
        ours = slice(place * width, (place + 1) * width)
        pairs += [(mix.at[:, theirs], mix_to.at[:, ours]), (mix_other.at[:, theirs], mix_other_to.at[:, ours])]
        for index, (rows, columns) in enumerate(((up, down), (up_other, down_other))):
            units = slice(index * rows.shape[1], (index + 1) * rows.shape[1])
            pairs += [
                (rows.at[theirs, :], up_to.at[ours, units]),
                (columns.at[:, theirs], down_to.at[units, ours]),
            ]
    return [pltpu.make_async_copy(source, target, sem.at[index]) for index, (source, target) in enumerate(pairs)]


def local_kernel(
    block_start, block_count, basis_from, own_from, other, *refs, lon_blocks, block_width, block_most
):
    sources, refs = refs[:6], refs[6:]
    conv_own, conv_other, residual, edge_filter, *targets = refs[:8]
    own, basis, filters, near, window0, window1, own_sem, basis_sem, weight_sems = refs[8:]
    core = lax.axis_index("chan")
    cells, width = own.shape[1:]
    depth = block_most * block_width
    rows = basis.shape[0]
    first_copies = start_all([
        pltpu.make_async_copy(
            basis_from.at[pl.ds(pl.multiple_of(core * rows, rows), rows), :], basis, basis_sem
        ),
        pltpu.make_async_copy(own_from, own, own_sem),
    ])
    weight_copies = start_all(stage_weights(core, sources, targets, weight_sems, width))
    start = halo_start(block_start, core)
    fills = ((0, other), (1, own))
    for which, (half, source) in enumerate(fills):
        lanes = slice((1 - half) * width, (2 - half) * width)
        if which == 1:
            wait_all(first_copies)
        for row, window in enumerate((window0, window1)):
            window[:cells, lanes] = source[row]
            window[cells:, lanes] = source[row, : window.shape[0] - cells]
        for place in range(lon_blocks):
            home = block_rows(home_block(place, start, lon_blocks), block_width)
            residual[place * block_width : (place + 1) * block_width, lanes] = (
                source[core, home, :].astype(jnp.float32)
            )
    spread_filters(basis, block_count, core, filters, block_most)
    near[:, :depth] = filters[1 - core]
    near[:, depth:] = filters[2 - core]
    edge_filter[...] = filters[2 * core]
    starts = (block_start[core, 1 - core], block_start[core, 2 - core])

    def group_step(group, carry):
        for slot in range(GROUP):
            place = group * GROUP + slot
            home = home_block(place, start, lon_blocks)
            parts = []
            for window, tap_start in zip((window0, window1), starts):
                source = wrap(home + tap_start, lon_blocks)
                parts.append(window[block_rows(source, block_width, block_most), :])
            result = jnp.dot(near[...], jnp.concatenate(parts, axis=0), preferred_element_type=jnp.float32)
            conv_own[place] = result[:, :width]
            conv_other[place] = result[:, width:]
        return carry

    lax.fori_loop(0, lon_blocks // GROUP, group_step, 0)
    wait_all(weight_copies)


def halo_mix(first, places, block_width, halves, spans, edge_filter, conv_local, mix, window, conv):
    at = 0
    for half, (low, high) in zip(halves, spans):
        window[at : at + high - low, :] = half[low:high, :]
        at += high - low
    depth = edge_filter.shape[1]
    width = window.shape[1]
    for slot in range(places):
        result = conv_local[first + slot] + jnp.dot(
            edge_filter[...], window[slot * block_width : slot * block_width + depth, :],
            preferred_element_type=jnp.float32,
        )
        rounded = result.astype(jnp.bfloat16)
        for basis in range(edge_filter.shape[0] // block_width):
            conv[
                slot * block_width : (slot + 1) * block_width, basis * width : (basis + 1) * width
            ] = rounded[basis * block_width : (basis + 1) * block_width]
    return jnp.dot(conv[...], mix[...], preferred_element_type=jnp.float32)


def first_half_kernel(*refs, plan, ordered, block_width):
    halves, refs = refs[: len(plan["spans"])], refs[len(plan["spans"]) + ordered :]
    edge_filter, conv_local, mix, residual, result, window, conv = refs
    first, places = plan["first"], plan["places"]
    mixed = halo_mix(
        first, places, block_width, halves, plan["spans"], edge_filter, conv_local, mix, window, conv
    )
    result[...] = residual[first * block_width : (first + places) * block_width, :] + mixed


def gelu(x):
    return 0.5 * x * (1.0 + lax.erf(x * 0.7071067811865476))


def tail_kernel(*refs, plan, ordered, block_width, state_spans):
    count = len(plan["spans"])
    halves, refs = refs[:count], refs[count + ordered :]
    partials, refs = refs[: len(state_spans)], refs[len(state_spans) :]
    edge_filter, conv_local, mix, up, down, keep, send, window, conv = refs
    mixed = halo_mix(
        plan["first"], plan["places"], block_width, halves, plan["spans"], edge_filter, conv_local, mix,
        window, conv,
    )
    before = [partial[low:high, :] for partial, (low, high) in zip(partials, state_spans)]
    state = mixed + (before[0] if len(before) == 1 else jnp.concatenate(before, axis=0))
    width = send.shape[1]
    hidden = gelu(
        jnp.dot(state.astype(jnp.bfloat16), up[...], preferred_element_type=jnp.float32)
    ).astype(jnp.bfloat16)
    total = state + jnp.dot(hidden, down[...], preferred_element_type=jnp.float32)
    total = total.astype(jnp.bfloat16)
    first = plan["first"] * block_width
    keep[first : first + total.shape[0], :] = total[:, :width]
    send[...] = total[:, width:]


def begin_place(source, result, row, home, sem, lon_blocks, block_width):
    places = source.shape[0] // block_width

    def begin(count):
        size = count * block_width
        pltpu.make_async_copy(
            source.at[:size, :], result.at[row, block_rows(home, block_width, count), :], sem
        ).start()
        if count < places:
            pltpu.make_async_copy(
                source.at[size:, :], result.at[row, : source.shape[0] - size, :], sem
            ).start()

    def choose(low, high):
        if low == high:
            begin(low)
            return
        middle = (low + high) // 2
        early = lon_blocks - home <= middle
        pl.when(early)(lambda: choose(low, middle))
        pl.when(jnp.logical_not(early))(lambda: choose(middle + 1, high))

    choose(1, places)
    return pltpu.make_async_copy(source, result.at[row, : source.shape[0], :], sem)


def scalar_start(block_start, row):
    shape = block_start.shape
    here = jnp.logical_and(
        lax.broadcasted_iota(jnp.int32, shape, 0) == row, lax.broadcasted_iota(jnp.int32, shape, 1) == 2 * row
    )
    return jnp.max(jnp.where(here, block_start[...].astype(jnp.float32), 0.0)).astype(jnp.int32)


def place_kernel(block_start, keep, *refs, firsts, lon_blocks, block_width):
    *received, result, sems = refs
    core = lax.axis_index("chan")
    waits = []
    for index, (source, first) in enumerate(zip((keep, *received), (0, *firsts))):
        row = 1 - core if index else core
        if index < 2:
            start = scalar_start(block_start, row)
        waits.append(begin_place(
            source, result, row, home_block(first, start, lon_blocks), sems.at[index], lon_blocks, block_width
        ))
    wait_all(waits)


def place_last_kernel(block_start, source, before, result, sem, *, first, lon_blocks, block_width):
    row = 1 - lax.axis_index("chan")
    home = home_block(first, scalar_start(block_start, row), lon_blocks)
    begin_place(source, result, row, home, sem, lon_blocks, block_width).wait()


def relay_kernel(other, *pieces):
    core = lax.axis_index("chan")
    at = 0
    for piece in pieces:
        piece[...] = other[core, at : at + piece.shape[0], :]
        at += piece.shape[0]


def edge_kernel(rows, *refs):
    *pieces, sems = refs
    core = lax.axis_index("chan")
    at = 0
    copies = []
    for index, piece in enumerate(pieces):
        copies.append(
            pltpu.make_async_copy(rows.at[core, at : at + piece.shape[0], :], piece, sems.at[index])
        )
        at += piece.shape[0]
    wait_all(start_all(copies))


def in_hbm(array):
    return pltpu.with_memory_space_constraint(array, pltpu.HBM)


def limit(mebibytes):
    return pltpu.CompilerParams(vmem_limit_bytes=mebibytes * 1024 * 1024)


def cost(flops=1000):
    return pl.CostEstimate(flops=flops, bytes_accessed=1000, transcendentals=0)


def anywhere(count):
    return [pl.BlockSpec(memory_space=pl.ANY)] * count


def vmem(count):
    return [pl.BlockSpec(memory_space=pltpu.VMEM)] * count


def plans_of(cuts, lon_blocks, block_width, block_most):
    reach = block_most - 1
    plans = []
    first = 0
    for index in range(1, len(cuts)):
        last = cuts[index] - reach if index < len(cuts) - 1 else lon_blocks
        need = []
        for block in range(first, last + reach):
            block %= lon_blocks
            piece = max(which for which in range(len(cuts) - 1) if cuts[which] <= block)
            low = (block - cuts[piece]) * block_width
            if need and need[-1][0] == piece and need[-1][2] == low:
                need[-1][2] = low + block_width
            else:
                need.append([piece, low, low + block_width])
        plans.append(dict(
            first=first, places=last - first,
            pieces=[piece for piece, _, _ in need], spans=[(low, high) for _, low, high in need],
        ))
        first = last
    return plans


def per_device(
    state_in, basis_blocks, block_start, block_count, mix_weight, up_weight, down_weight
):
    bands = lax.axis_size("lat")
    local_rows, basis_count, block_width, taps, block_most = basis_blocks.shape[:5]
    cells, width = state_in.shape[1:]
    channels = mix_weight.shape[2]
    units = 2 * up_weight.shape[1]
    lon_blocks = cells // block_width
    depth = block_most * block_width
    filter_rows = basis_count * block_width
    swap = [(0, 1), (1, 0)]
    pairs = []
    for band in range(bands - 1):
        pairs += [(2 * band + 1, 2 * band + 2), (2 * band + 2, 2 * band + 1)]

    sizes = dict(block_width=block_width, lon_blocks=lon_blocks)
    smem = [pl.BlockSpec(memory_space=pltpu.SMEM)]
    narrow = state_in.dtype

    def row_pieces(cuts):
        return [pltpu.VMEM(((high - low) * block_width, width), narrow) for low, high in zip(cuts, cuts[1:])]

    edge = pl.pallas_call(
        edge_kernel,
        out_shape=row_pieces(FIRST_CUTS),
        in_specs=anywhere(1),
        out_specs=vmem(len(FIRST_CUTS) - 1),
        scratch_shapes=[pltpu.SemaphoreType.DMA((len(FIRST_CUTS) - 1,))],
        compiler_params=limit(4),
        cost_estimate=cost(),
        name="edge_row",
    )(in_hbm(state_in))
    halo_other = [lax.ppermute(piece, ("lat", "chan"), pairs) for piece in edge]
    other = lax.ppermute(state_in, "chan", swap)
    relay = pl.pallas_call(
        relay_kernel,
        out_shape=row_pieces(LAST_CUTS),
        in_specs=vmem(1),
        out_specs=vmem(len(LAST_CUTS) - 1),
        compiler_params=limit(4),
        cost_estimate=cost(),
        name="relay_rows",
    )(other)
    halo_own = [lax.ppermute(piece, ("lat", "chan"), pairs) for piece in relay]
    mix_other = lax.ppermute(mix_weight, "chan", swap)
    up_other = lax.ppermute(up_weight, "chan", swap)
    down_other = lax.ppermute(down_weight, "chan", swap)

    basis_flat = basis_blocks.reshape(local_rows * filter_rows * taps * block_most, block_width)
    mixing = (basis_count * width, channels)
    weights = (
        in_hbm(mix_weight.reshape(mixing)), mix_other.reshape(mixing),
        in_hbm(up_weight), up_other, in_hbm(down_weight), down_other,
    )
    conv_shape = jax.ShapeDtypeStruct((lon_blocks, filter_rows, width), jnp.float32)
    wide_window = pltpu.VMEM((cells + depth - block_width, channels), narrow)
    staged = [mixing, mixing, (channels, units), (units, channels)]
    conv_own, conv_other, residual, edge_filter, mix_own, mix_other, up, down = pl.pallas_call(
        functools.partial(local_kernel, block_most=block_most, **sizes),
        out_shape=[
            conv_shape, conv_shape, jax.ShapeDtypeStruct((cells, channels), jnp.float32),
            jax.ShapeDtypeStruct((filter_rows, depth), narrow),
            *[jax.ShapeDtypeStruct(shape, narrow) for shape in staged],
        ],
        in_specs=smem * 2 + anywhere(2) + vmem(1) + anywhere(len(weights)),
        out_specs=vmem(4 + len(staged)),
        scratch_shapes=[
            pltpu.VMEM(state_in.shape, narrow),
            pltpu.VMEM((basis_flat.shape[0] // local_rows, block_width), narrow),
            pltpu.VMEM((taps, filter_rows, depth), narrow),
            pltpu.VMEM((filter_rows, 2 * depth), narrow),
            wide_window, wide_window,
            pltpu.SemaphoreType.DMA, pltpu.SemaphoreType.DMA, pltpu.SemaphoreType.DMA((12,)),
        ],
        compiler_params=limit(16),
        cost_estimate=cost(),
        name="local_taps",
    )(block_start, block_count, in_hbm(basis_flat), in_hbm(state_in), other, *weights)

    def halo_scratch(plan):
        return [
            pltpu.VMEM(((plan["places"] + block_most - 1) * block_width, width), narrow),
            pltpu.VMEM((plan["places"] * block_width, basis_count * width), narrow),
        ]

    partials = []
    first_plans = plans_of(FIRST_CUTS, lon_blocks, block_width, block_most)
    for plan in first_plans:
        done = partials[-1:]
        partials.append(pl.pallas_call(
            functools.partial(first_half_kernel, plan=plan, ordered=len(done), block_width=block_width),
            out_shape=jax.ShapeDtypeStruct((plan["places"] * block_width, channels), jnp.float32),
            in_specs=vmem(len(plan["pieces"])) + anywhere(len(done)) + vmem(4),
            out_specs=vmem(1)[0],
            scratch_shapes=halo_scratch(plan),
            compiler_params=limit(10),
            cost_estimate=cost(4 * 10**9 if done else 1000),
            name="edge_tap_first_half",
        )(*[halo_other[piece] for piece in plan["pieces"]], *done, edge_filter, conv_other, mix_other, residual))

    received, done, firsts = [], partials[-1:], []
    last_plans = plans_of(LAST_CUTS, lon_blocks, block_width, block_most)
    for plan in last_plans:
        low, high = plan["first"], plan["first"] + plan["places"]
        states, state_spans = [], []
        for partial, other_plan in zip(partials, first_plans):
            begin = max(low, other_plan["first"])
            end = min(high, other_plan["first"] + other_plan["places"])
            if begin < end:
                states.append(partial)
                state_spans.append((
                    (begin - other_plan["first"]) * block_width, (end - other_plan["first"]) * block_width
                ))
        rows = plan["places"] * block_width
        keep, send = pl.pallas_call(
            functools.partial(
                tail_kernel, plan=plan, ordered=len(done), block_width=block_width, state_spans=state_spans
            ),
            out_shape=[jax.ShapeDtypeStruct((size, width), narrow) for size in (cells, rows)],
            in_specs=vmem(len(plan["pieces"])) + anywhere(len(done)) + vmem(len(states) + 5),
            out_specs=vmem(2),
            scratch_shapes=halo_scratch(plan),
            input_output_aliases={len(plan["pieces"]): 0} if received else {},
            compiler_params=limit(14),
            cost_estimate=cost(1000 if low == 0 else 10**10),
            name="edge_tap_and_feed",
        )(
            *[halo_own[piece] for piece in plan["pieces"]], *done, *states,
            edge_filter, conv_own, mix_own, up, down,
        )
        if received:
            send, received[-1] = lax.optimization_barrier((send, received[-1]))
        firsts.append(low)
        done = [keep]
        received.append(lax.ppermute(send, "chan", swap))

    result = jax.ShapeDtypeStruct(state_in.shape, narrow)
    placed = pl.pallas_call(
        functools.partial(place_kernel, firsts=firsts[:-1], **sizes),
        out_shape=result,
        in_specs=vmem(len(firsts) + 1),
        out_specs=anywhere(1)[0],
        scratch_shapes=[pltpu.SemaphoreType.DMA((len(firsts),))],
        cost_estimate=cost(),
        compiler_params=limit(4),
        name="place_rows",
    )(block_start, keep, *received[:-1])

    return pl.pallas_call(
        functools.partial(place_last_kernel, first=firsts[-1], **sizes),
        out_shape=result,
        in_specs=vmem(2) + anywhere(1),
        out_specs=anywhere(1)[0],
        scratch_shapes=[pltpu.SemaphoreType.DMA],
        input_output_aliases={2: 0},
        cost_estimate=cost(),
        compiler_params=limit(4),
        name="place_last_rows",
    )(block_start, received[-1], placed)


def solution(mesh):
    placed = (
        P(("grp", "lat"), None, "chan"),
        P("lat", None, None, None, None, None),
        P("lat", None),
        P("lat", None),
        P(None, "chan", None),
        P(None, "chan"),
        P("chan", None),
    )
    return jax.shard_map(
        per_device,
        mesh=mesh,
        in_specs=placed,
        out_specs=P(("grp", "lat"), None, "chan"),
        check_vma=False,
    )
```

time: 47.1 us -> 45.7 us (0.970)
  Pallas kernels: 29.2 us -> 24.9 us
  waiting for transfers between devices: 0.17 us -> 2.75 us
  starting transfers between devices: 16.9 us -> 17.5 us
    pallas_call x9, Pallas kernels: 20.8 us -> 15.1 us  [the longest x3 7.65 us: per_device(): pl.pallas_call(functools.partial(tail_kernel, plan=plan, ordered=len(done...]
    ppermute x1, starting transfers between devices: 3.97 us -> 0.08 us  [per_device(): down_other = lax.ppermute(down_weight, 'chan', swap)]
    ppermute x2 -> x3, starting transfers between devices: 9.87 us -> 13.1 us  [per_device(): received.append(lax.ppermute(send, 'chan', swap))]
    ppermute x1, waiting for transfers between devices: 0.01 us -> 1.88 us  [per_device(): up_other = lax.ppermute(up_weight, 'chan', swap)]
    pallas_call x1, Pallas kernels: 8.48 us -> 9.8 us  [per_device(): pl.pallas_call(functools.partial(local_kernel, block_most=block_most, **s...]
    ppermute x3 -> x5, starting transfers between devices: 2.08 us -> 3.36 us  [the longest x3 2 us: per_device(): halo_own = [lax.ppermute(piece, ('lat', 'chan'), pairs) for piece in relay]]
    ppermute x1, waiting for transfers between devices: 0.01 us -> 0.7 us  [per_device(): other = lax.ppermute(state_in, 'chan', swap)]
  transfers between devices with their start and end apart: 9 -> 12, of which waited for: 1 -> 4; matrix products, arithmetic and copies ran while one was open for 0% -> 0% of each run, Pallas kernels for 60% -> 53%
where the time goes in v4:
time: 45.7 us; the launch traced here: 45.4 us
  Pallas kernels  24.9 us (54%)
  starting transfers between devices  17.5 us (38%)
  waiting for transfers between devices  2.75 us (6%)
    ppermute x3, starting transfers between devices, per_device(): received.append(lax.ppermute(send, 'chan', swap))  13.1 us
    pallas_call x1, Pallas kernels, per_device(): pl.pallas_call(functools.partial(local_kernel, block_most=block_most, **s...  9.8 us
    pallas_call x3, Pallas kernels, per_device(): pl.pallas_call(functools.partial(tail_kernel, plan=plan, ordered=len(done...  7.65 us
    pallas_call x2, Pallas kernels, per_device(): pl.pallas_call(functools.partial(first_half_kernel, plan=plan, ordered=le...  4.23 us
    ppermute x3, starting transfers between devices, per_device(): halo_own = [lax.ppermute(piece, ('lat', 'chan'), pairs) for piece in relay]  2 us
    ppermute x1, waiting for transfers between devices, per_device(): up_other = lax.ppermute(up_weight, 'chan', swap)  1.88 us
    ppermute x2, starting transfers between devices, per_device(): halo_other = [lax.ppermute(piece, ('lat', 'chan'), pairs) for piece in edge]  1.36 us
    pallas_call x1, Pallas kernels, per_device(): pl.pallas_call(functools.partial(place_kernel, firsts=firsts[:-1], **size...  1.17 us
  transfers between devices with their start and end apart: 12, of which 4 were waited for; matrix products, arithmetic and copies ran while one was open for 0% of the time, Pallas kernels for 53%

profile of v4, /device:TPU:0, one launch (start us, length us, event | category | flops | bytes accessed | tf_op | source)
XLA Modules:
  0.0 45.4 jit_solution(15909955242191091185)
XLA Ops:
  0.0 0.5 collective-permute-start
  0.5 0.1 collective-permute-start.6
  0.5 0.4 collective-permute-start.7
  1.0 0.1 collective-permute-start.8
  1.0 1.1 %edge_row.1 = (bf16[880,256]{1,0:T(8,128)(2,1)S(1)}, bf16[560,256]{1,0:T(8,128)(2,1)S(1)}) custom-call(bf16[2,1440,256]{2,1,0:T(8,128)(2,1)} %own_from.1), custom_call_target="tpu_custom_call" | custom-call | flops 1000 | bytes 1000 | tf_op jit(solution)/shard_map/edge_row/pallas_call | solution.py:331
  2.2 0.7 %collective-permute-start.4 = (bf16[880,256]{1,0:T(8,128)(2,1)S(1)}, bf16[880,256]{1,0:T(8,128)(2,1)S(1)}, u32[]{:S(2)}, u32[]{:S(2)}) collective-permute-start(bf16[880,256]{1,0:T(8,128)(2,1)S(1)} %get-tuple-element.31), channel_id=1, source_target_pairs={{1,2},{2,1},{3,4},{4,3},{5,6},{6,5},{7,8},{8,7},{9,10},{10,9},{11,... | collective-permute-start | bytes 1351688 | tf_op jit(solution)/shard_map/ppermute | solution.py:341
  2.9 0.7 %collective-permute-done.other = bf16[2,1440,256]{2,1,0:T(8,128)(2,1)S(1)} collective-permute-done((bf16[2,1440,256]{2,1,0:T(8,128)(2,1)}, bf16[2,1440,256]{2,1,0:T(8,128)(2,1)S(1)}, u32[]{:S(2)}, u32[]{:S(2)}) %collective-permute-start) | collective-permute-done | bytes 1474592 | tf_op jit(solution)/shard_map/ppermute | solution.py:342
  3.6 0.7 %collective-permute-start.5 = (bf16[560,256]{1,0:T(8,128)(2,1)S(1)}, bf16[560,256]{1,0:T(8,128)(2,1)S(1)}, u32[]{:S(2)}, u32[]{:S(2)}) collective-permute-start(bf16[560,256]{1,0:T(8,128)(2,1)S(1)} %get-tuple-element.32), channel_id=1, source_target_pairs={{1,2},{2,1},{3,4},{4,3},{5,6},{6,5},{7,8},{8,7},{9,10},{10,9},{11,... | collective-permute-start | bytes 860168 | tf_op jit(solution)/shard_map/ppermute | solution.py:341
  4.3 1.9 %collective-permute-done.7.refs_3_ = bf16[512,512]{1,0:T(8,128)(2,1)S(1)} collective-permute-done((bf16[512,512]{1,0:T(8,128)(2,1)}, bf16[512,512]{1,0:T(8,128)(2,1)S(1)}, u32[]{:S(2)}, u32[]{:S(2)}) %collective-permute-start.7) | collective-permute-done | bytes 524320 | tf_op jit(solution)/shard_map/ppermute | solution.py:354
  6.2 0.7 %collective-permute-start.3 = (bf16[640,256]{1,0:T(8,128)(2,1)S(1)}, bf16[640,256]{1,0:T(8,128)(2,1)S(1)}, u32[]{:S(2)}, u32[]{:S(2)}) collective-permute-start(bf16[640,256]{1,0:T(8,128)(2,1)S(1)} %get-tuple-element.30), channel_id=1, source_target_pairs={{1,2},{2,1},{3,4},{4,3},{5,6},{6,5},{7,8},{8,7},{9,10},{10,9},{11,... | collective-permute-start | bytes 983048 | tf_op jit(solution)/shard_map/ppermute | solution.py:352
  6.9 0.7 %collective-permute-start.1 = (bf16[400,256]{1,0:T(8,128)(2,1)S(1)}, bf16[400,256]{1,0:T(8,128)(2,1)S(1)}, u32[]{:S(2)}, u32[]{:S(2)}) collective-permute-start(bf16[400,256]{1,0:T(8,128)(2,1)S(1)} %get-tuple-element.28), channel_id=1, source_target_pairs={{1,2},{2,1},{3,4},{4,3},{5,6},{6,5},{7,8},{8,7},{9,10},{10,9},{11,... | collective-permute-start | bytes 614408 | tf_op jit(solution)/shard_map/ppermute | solution.py:352
  7.6 0.7 %collective-permute-start.2 = (bf16[400,256]{1,0:T(8,128)(2,1)S(1)}, bf16[400,256]{1,0:T(8,128)(2,1)S(1)}, u32[]{:S(2)}, u32[]{:S(2)}) collective-permute-start(bf16[400,256]{1,0:T(8,128)(2,1)S(1)} %get-tuple-element.29), channel_id=1, source_target_pairs={{1,2},{2,1},{3,4},{4,3},{5,6},{6,5},{7,8},{8,7},{9,10},{10,9},{11,... | collective-permute-start | bytes 614408 | tf_op jit(solution)/shard_map/ppermute | solution.py:352
  8.3 9.8 %local_taps.1 = (f32[18,400,256]{2,1,0:T(8,128)S(1)}, f32[18,400,256]{2,1,0:T(8,128)S(1)}, f32[1440,512]{1,0:T(8,128)S(1)}, bf16[400,320]{1,0:T(8,128)(2,1)S(1)}...) custom-call(s32[2,3]{1,0:T(2,128)S(1)} %copy-done, ...), custom_call_target="tpu_custom_call" | custom-call | flops 1000 | bytes 1000 | tf_op jit(solution)/shard_map/local_taps/pallas_call | solution.py:366
  18.1 1.9 %edge_tap_first_half.2.refs_3_.refs_2_ = f32[640,512]{1,0:T(8,128)S(1)} custom-call(bf16[880,256]{1,0:T(8,128)(2,1)S(1)} %collective-permute-done.4.refs_0_.refs_2_, bf16[400,320]{1,0:T(8,128)(2,1)S(1)} %get-tuple-element.33.refs_1_.refs_4_.refs_3_.refs_5_, f32[18,400,256]{2,1,0:T(8,128)S(1)} %get-tuple-element.34.refs_2_.refs_5_, ...), custom_call_target="tpu_custom_call" | custom-call | flops 1000 | bytes 1000 | tf_op jit(solution)/shard_map/edge_tap_first_half/pallas_call | solution.py:398
  20.1 2.3 %edge_tap_first_half.3.refs_1_.refs_4_ = f32[800,512]{1,0:T(8,128)S(1)} custom-call(bf16[880,256]{1,0:T(8,128)(2,1)S(1)} %collective-permute-done.4.refs_0_.refs_2_, bf16[560,256]{1,0:T(8,128)(2,1)S(1)} %collective-permute-done.5.refs_1_, bf16[880,256]{1,0:T(8,128)(2,1)S(1)} %collective-permute-done.4.refs_0_.refs_2_, ...), custom_call_target="tpu_custom_call" | custom-call | flops 4000000000 | bytes 1000 | tf_op jit(solution)/shard_map/edge_tap_first_half/pallas_call | solution.py:398
  22.4 2.2 %edge_tap_and_feed.3 = (bf16[1440,256]{1,0:T(8,128)(2,1)S(1)}, bf16[400,256]{1,0:T(8,128)(2,1)S(1)}) custom-call(bf16[640,256]{1,0:T(8,128)(2,1)S(1)} %collective-permute-done.3.refs_0_.refs_2_, f32[800,512]{1,0:T(8,128)S(1)} %edge_tap_first_half.3.refs_1_.refs_4_, f32[640,512]{1,0:T(8,128)S(1)} %edge_tap_first_half.2.refs_3_.refs_2_, ...), custom_call_target="tpu_custom_call" | custom-call | flops 1000 | bytes 1000 | tf_op jit(solution)/shard_map/edge_tap_and_feed/pallas_call | solution.py:423
  24.6 12.5 %collective-permute-start.9 = (bf16[400,256]{1,0:T(8,128)(2,1)S(1)}, bf16[400,256]{1,0:T(8,128)(2,1)S(1)}, u32[]{:S(2)}, u32[]{:S(2)}) collective-permute-start(bf16[400,256]{1,0:T(8,128)(2,1)S(1)} %get-tuple-element.45), channel_id=1, source_target_pairs={{0,1},{1,0},{2,3},{3,2},{4,5},{5,4},{6,7},{7,6},{8,9},{9,8},{10,11... | collective-permute-start | bytes 614408 | tf_op jit(solution)/shard_map/ppermute | solution.py:443
  37.1 2.2 %edge_tap_and_feed.4 = (bf16[1440,256]{1,0:T(8,128)(2,1)S(1)}, bf16[400,256]{1,0:T(8,128)(2,1)S(1)}) custom-call(bf16[640,256]{1,0:T(8,128)(2,1)S(1)} %collective-permute-done.3.refs_0_.refs_2_, bf16[400,256]{1,0:T(8,128)(2,1)S(1)} %collective-permute-done.1.refs_1_.refs_0_, ...), custom_call_target="tpu_custom_call", output_to_operand_aliasing={{0}: (2, {})} | custom-call | flops 10000000000 | bytes 1000 | tf_op jit(solution)/shard_map/edge_tap_and_feed/pallas_call | solution.py:423
  39.3 0.1 collective-permute-start.10
  39.4 3.3 %edge_tap_and_feed.5 = (bf16[1440,256]{1,0:T(8,128)(2,1)S(1)}, bf16[640,256]{1,0:T(8,128)(2,1)S(1)}) custom-call(bf16[400,256]{1,0:T(8,128)(2,1)S(1)} %collective-permute-done.1.refs_1_.refs_0_, bf16[400,256]{1,0:T(8,128)(2,1)S(1)} %collective-permute-done.2.refs_1_, ...), custom_call_target="tpu_custom_call", output_to_operand_aliasing={{0}: (3, {})} | custom-call | flops 10000000000 | bytes 1000 | tf_op jit(solution)/shard_map/edge_tap_and_feed/pallas_call | solution.py:423
  42.7 0.6 %collective-permute-start.11 = (bf16[640,256]{1,0:T(8,128)(2,1)S(1)}, bf16[640,256]{1,0:T(8,128)(2,1)S(1)}, u32[]{:S(2)}, u32[]{:S(2)}) collective-permute-start(bf16[640,256]{1,0:T(8,128)(2,1)S(1)} %get-tuple-element.47), channel_id=1, source_target_pairs={{0,1},{1,0},{2,3},{3,2},{4,5},{5,4},{6,7},{7,6},{8,9},{9,8},{10,11... | collective-permute-start | bytes 983048 | tf_op jit(solution)/shard_map/ppermute | solution.py:443
  43.2 1.2 %place_rows.1.before = bf16[2,1440,256]{2,1,0:T(8,128)(2,1)} custom-call(s32[2,3]{1,0:T(2,128)S(1)} %copy-done, bf16[1440,256]{1,0:T(8,128)(2,1)S(1)} %get-tuple-element.48.keep, bf16[400,256]{1,0:T(8,128)(2,1)S(1)} %collective-permute-done.9.refs_0_, bf16[400,256]{1,0:T(8,128)(2,1)S(1)} %collective-permute-done.10.refs_1_), custom_call_target="tpu_custom_call" | custom-call | flops 1000 | bytes 1000 | tf_op jit(solution)/shard_map/place_rows/pallas_call | solution.py:446
  44.4 0.1 collective-permute-done.11.source
  44.5 0.9 %place_last_rows.1 = bf16[2,1440,256]{2,1,0:T(8,128)(2,1)} custom-call(s32[2,3]{1,0:T(2,128)S(1)} %copy-done, bf16[640,256]{1,0:T(8,128)(2,1)S(1)} %collective-permute-done.11.source, bf16[2,1440,256]{2,1,0:T(8,128)(2,1)} %place_rows.1.before), custom_call_target="tpu_custom_call", output_to_operand_aliasing={{}: (2, {})} | custom-call | flops 1000 | bytes 1000 | tf_op jit(solution)/shard_map/place_last_rows/pallas_call | solution.py:457
  (14 shorter events, 0.2 us)
Async XLA Ops:
  0.0 8.3 %copy-start.1 = (s32[2,3]{1,0:T(2,128)S(1)}, s32[2,3]{1,0:T(2,128)}, u32[]{:S(2)}) copy-start(s32[2,3]{1,0:T(2,128)} %block_count.1) | copy-start | bytes 76
  0.0 8.3 %copy-start = (s32[2,3]{1,0:T(2,128)S(1)}, s32[2,3]{1,0:T(2,128)}, u32[]{:S(2)}) copy-start(s32[2,3]{1,0:T(2,128)} %block_start.5) | copy-start | bytes 76
  0.0 3.6 %collective-permute-start = (bf16[2,1440,256]{2,1,0:T(8,128)(2,1)}, bf16[2,1440,256]{2,1,0:T(8,128)(2,1)S(1)}, u32[]{:S(2)}, u32[]{:S(2)}) collective-permute-start(bf16[2,1440,256]{2,1,0:T(8,128)(2,1)} %own_from.1), channel_id=1, source_target_pairs={{0,1},{1,0},{2,3},{3,2},{4,5},{5,4},{6,7},{7,6},{8,9},{9,8},{10,11... | collective-permute-start | bytes 4423688 | tf_op jit(solution)/shard_map/ppermute | solution.py:342
  0.5 7.2 %collective-permute-start.6 = (bf16[5,256,512]{2,1,0:T(8,128)(2,1)}, bf16[5,256,512]{2,1,0:T(8,128)(2,1)S(1)}, u32[]{:S(2)}, u32[]{:S(2)}) collective-permute-start(bf16[5,256,512]{2,1,0:T(8,128)(2,1)} %param.11), channel_id=1, source_target_pairs={{0,1},{1,0},{2,3},{3,2},{4,5},{5,4},{6,7},{7,6},{8,9},{9,8},{10,11... | collective-permute-start | bytes 3932168 | tf_op jit(solution)/shard_map/ppermute | solution.py:353
  0.5 5.7 %collective-permute-start.7 = (bf16[512,512]{1,0:T(8,128)(2,1)}, bf16[512,512]{1,0:T(8,128)(2,1)S(1)}, u32[]{:S(2)}, u32[]{:S(2)}) collective-permute-start(bf16[512,512]{1,0:T(8,128)(2,1)} %refs_2_.1), channel_id=1, source_target_pairs={{0,1},{1,0},{2,3},{3,2},{4,5},{5,4},{6,7},{7,6},{8,9},{9,8},{10,11... | collective-permute-start | bytes 1572872 | tf_op jit(solution)/shard_map/ppermute | solution.py:354
  1.0 6.0 %collective-permute-start.8 = (bf16[512,512]{1,0:T(8,128)(2,1)}, bf16[512,512]{1,0:T(8,128)(2,1)S(1)}, u32[]{:S(2)}, u32[]{:S(2)}) collective-permute-start(bf16[512,512]{1,0:T(8,128)(2,1)} %refs_4_.1), channel_id=1, source_target_pairs={{0,1},{1,0},{2,3},{3,2},{4,5},{5,4},{6,7},{7,6},{8,9},{9,8},{10,11... | collective-permute-start | bytes 1572872 | tf_op jit(solution)/shard_map/ppermute | solution.py:355
  2.2 16.0 %collective-permute-start.4 = (bf16[880,256]{1,0:T(8,128)(2,1)S(1)}, bf16[880,256]{1,0:T(8,128)(2,1)S(1)}, u32[]{:S(2)}, u32[]{:S(2)}) collective-permute-start(bf16[880,256]{1,0:T(8,128)(2,1)S(1)} %get-tuple-element.31), channel_id=1, source_target_pairs={{1,2},{2,1},{3,4},{4,3},{5,6},{6,5},{7,8},{8,7},{9,10},{10,9},{11,... | collective-permute-start | bytes 1351688 | tf_op jit(solution)/shard_map/ppermute | solution.py:341
  3.6 16.5 %collective-permute-start.5 = (bf16[560,256]{1,0:T(8,128)(2,1)S(1)}, bf16[560,256]{1,0:T(8,128)(2,1)S(1)}, u32[]{:S(2)}, u32[]{:S(2)}) collective-permute-start(bf16[560,256]{1,0:T(8,128)(2,1)S(1)} %get-tuple-element.32), channel_id=1, source_target_pairs={{1,2},{2,1},{3,4},{4,3},{5,6},{6,5},{7,8},{8,7},{9,10},{10,9},{11,... | collective-permute-start | bytes 860168 | tf_op jit(solution)/shard_map/ppermute | solution.py:341
  6.2 16.2 %collective-permute-start.3 = (bf16[640,256]{1,0:T(8,128)(2,1)S(1)}, bf16[640,256]{1,0:T(8,128)(2,1)S(1)}, u32[]{:S(2)}, u32[]{:S(2)}) collective-permute-start(bf16[640,256]{1,0:T(8,128)(2,1)S(1)} %get-tuple-element.30), channel_id=1, source_target_pairs={{1,2},{2,1},{3,4},{4,3},{5,6},{6,5},{7,8},{8,7},{9,10},{10,9},{11,... | collective-permute-start | bytes 983048 | tf_op jit(solution)/shard_map/ppermute | solution.py:352
  6.9 30.2 %collective-permute-start.1 = (bf16[400,256]{1,0:T(8,128)(2,1)S(1)}, bf16[400,256]{1,0:T(8,128)(2,1)S(1)}, u32[]{:S(2)}, u32[]{:S(2)}) collective-permute-start(bf16[400,256]{1,0:T(8,128)(2,1)S(1)} %get-tuple-element.28), channel_id=1, source_target_pairs={{1,2},{2,1},{3,4},{4,3},{5,6},{6,5},{7,8},{8,7},{9,10},{10,9},{11,... | collective-permute-start | bytes 614408 | tf_op jit(solution)/shard_map/ppermute | solution.py:352
  7.6 31.8 %collective-permute-start.2 = (bf16[400,256]{1,0:T(8,128)(2,1)S(1)}, bf16[400,256]{1,0:T(8,128)(2,1)S(1)}, u32[]{:S(2)}, u32[]{:S(2)}) collective-permute-start(bf16[400,256]{1,0:T(8,128)(2,1)S(1)} %get-tuple-element.29), channel_id=1, source_target_pairs={{1,2},{2,1},{3,4},{4,3},{5,6},{6,5},{7,8},{8,7},{9,10},{10,9},{11,... | collective-permute-start | bytes 614408 | tf_op jit(solution)/shard_map/ppermute | solution.py:352
  24.6 14.7 %collective-permute-start.9 = (bf16[400,256]{1,0:T(8,128)(2,1)S(1)}, bf16[400,256]{1,0:T(8,128)(2,1)S(1)}, u32[]{:S(2)}, u32[]{:S(2)}) collective-permute-start(bf16[400,256]{1,0:T(8,128)(2,1)S(1)} %get-tuple-element.45), channel_id=1, source_target_pairs={{0,1},{1,0},{2,3},{3,2},{4,5},{5,4},{6,7},{7,6},{8,9},{9,8},{10,11... | collective-permute-start | bytes 614408 | tf_op jit(solution)/shard_map/ppermute | solution.py:443
  39.3 3.4 %collective-permute-start.10 = (bf16[400,256]{1,0:T(8,128)(2,1)S(1)}, bf16[400,256]{1,0:T(8,128)(2,1)S(1)}, u32[]{:S(2)}, u32[]{:S(2)}) collective-permute-start(bf16[400,256]{1,0:T(8,128)(2,1)S(1)} %get-tuple-element.46), channel_id=1, source_target_pairs={{0,1},{1,0},{2,3},{3,2},{4,5},{5,4},{6,7},{7,6},{8,9},{9,8},{10,11... | collective-permute-start | bytes 614408 | tf_op jit(solution)/shard_map/ppermute | solution.py:443
  42.7 1.8 %collective-permute-start.11 = (bf16[640,256]{1,0:T(8,128)(2,1)S(1)}, bf16[640,256]{1,0:T(8,128)(2,1)S(1)}, u32[]{:S(2)}, u32[]{:S(2)}) collective-permute-start(bf16[640,256]{1,0:T(8,128)(2,1)S(1)} %get-tuple-element.47), channel_id=1, source_target_pairs={{0,1},{1,0},{2,3},{3,2},{4,5},{5,4},{6,7},{7,6},{8,9},{9,8},{10,11... | collective-permute-start | bytes 983048 | tf_op jit(solution)/shard_map/ppermute | solution.py:443

commit v5 on v4

--- a/solution.py
+++ b/solution.py
@@ -9,7 +9,7 @@
 
 GROUP = 9
 TILE = 16
-FIRST_CUTS = (0, 11, 18)
+FIRST_CUTS = (0, 18)
 LAST_CUTS = (0, 8, 13, 18)
 
 
@@ -166,8 +166,8 @@
 
 
 def tail_kernel(*refs, plan, ordered, block_width, state_spans):
-    count = len(plan["spans"])
-    halves, refs = refs[:count], refs[count + ordered :]
+    count = plan["all"]
+    halves, refs = [refs[piece] for piece in plan["pieces"]], refs[count + ordered :]
     partials, refs = refs[: len(state_spans)], refs[len(state_spans) :]
     edge_filter, conv_local, mix, up, down, keep, send, window, conv = refs
     mixed = halo_mix(
@@ -184,7 +184,8 @@
     total = total.astype(jnp.bfloat16)
     first = plan["first"] * block_width
     keep[first : first + total.shape[0], :] = total[:, :width]
-    send[...] = total[:, width:]
+    first -= plan["sent_from"] * block_width
+    send[first : first + total.shape[0], :] = total[:, width:]
 
 
 def begin_place(source, result, row, home, sem, lon_blocks, block_width):
@@ -241,7 +242,7 @@
     begin_place(source, result, row, home, sem, lon_blocks, block_width).wait()
 
 
-def relay_kernel(other, *pieces):
+def relay_kernel(other, ordered, *pieces):
     core = lax.axis_index("chan")
     at = 0
     for piece in pieces:
@@ -340,16 +341,6 @@
     )(in_hbm(state_in))
     halo_other = [lax.ppermute(piece, ("lat", "chan"), pairs) for piece in edge]
     other = lax.ppermute(state_in, "chan", swap)
-    relay = pl.pallas_call(
-        relay_kernel,
-        out_shape=row_pieces(LAST_CUTS),
-        in_specs=vmem(1),
-        out_specs=vmem(len(LAST_CUTS) - 1),
-        compiler_params=limit(4),
-        cost_estimate=cost(),
-        name="relay_rows",
-    )(other)
-    halo_own = [lax.ppermute(piece, ("lat", "chan"), pairs) for piece in relay]
     mix_other = lax.ppermute(mix_weight, "chan", swap)
     up_other = lax.ppermute(up_weight, "chan", swap)
     down_other = lax.ppermute(down_weight, "chan", swap)
@@ -385,6 +376,17 @@
         name="local_taps",
     )(block_start, block_count, in_hbm(basis_flat), in_hbm(state_in), other, *weights)
 
+    relay = pl.pallas_call(
+        relay_kernel,
+        out_shape=row_pieces(LAST_CUTS),
+        in_specs=vmem(1) + anywhere(1),
+        out_specs=vmem(len(LAST_CUTS) - 1),
+        compiler_params=limit(4),
+        cost_estimate=cost(),
+        name="relay_rows",
+    )(other, edge_filter)
+    halo_own = [lax.ppermute(piece, ("lat", "chan"), pairs) for piece in relay]
+
     def halo_scratch(plan):
         return [
             pltpu.VMEM(((plan["places"] + block_most - 1) * block_width, width), narrow),
@@ -402,12 +404,13 @@
             out_specs=vmem(1)[0],
             scratch_shapes=halo_scratch(plan),
             compiler_params=limit(10),
-            cost_estimate=cost(4 * 10**9 if done else 1000),
+            cost_estimate=cost(6 * 10**10),
             name="edge_tap_first_half",
         )(*[halo_other[piece] for piece in plan["pieces"]], *done, edge_filter, conv_other, mix_other, residual))
 
-    received, done, firsts = [], partials[-1:], []
+    sends, done = {}, partials[-1:]
     last_plans = plans_of(LAST_CUTS, lon_blocks, block_width, block_most)
+    firsts = (0, last_plans[-1]["first"])
     for plan in last_plans:
         low, high = plan["first"], plan["first"] + plan["places"]
         states, state_spans = [], []
@@ -419,29 +422,33 @@
                 state_spans.append((
                     (begin - other_plan["first"]) * block_width, (end - other_plan["first"]) * block_width
                 ))
-        rows = plan["places"] * block_width
+        plan["sent_from"] = max(place for place in firsts if place <= low)
+        sent = (firsts[1] if plan["sent_from"] == 0 else lon_blocks) - plan["sent_from"]
+        plan["all"] = max(plan["pieces"]) + 1
+        aliases = {plan["all"] + index: index for index in range(len(done))} if low else {}
+        used = [vmem(1) if piece in plan["pieces"] else anywhere(1) for piece in range(plan["all"])]
         keep, send = pl.pallas_call(
             functools.partial(
                 tail_kernel, plan=plan, ordered=len(done), block_width=block_width, state_spans=state_spans
             ),
-            out_shape=[jax.ShapeDtypeStruct((size, width), narrow) for size in (cells, rows)],
-            in_specs=vmem(len(plan["pieces"])) + anywhere(len(done)) + vmem(len(states) + 5),
+            out_shape=[jax.ShapeDtypeStruct((size, width), narrow) for size in (cells, sent * block_width)],
+            in_specs=sum(used, []) + anywhere(len(done)) + vmem(len(states) + 5),
             out_specs=vmem(2),
             scratch_shapes=halo_scratch(plan),
-            input_output_aliases={len(plan["pieces"]): 0} if received else {},
+            input_output_aliases=aliases,
             compiler_params=limit(14),
-            cost_estimate=cost(1000 if low == 0 else 10**10),
+            cost_estimate=cost(10**10 if high == lon_blocks else 1000),
             name="edge_tap_and_feed",
         )(
-            *[halo_own[piece] for piece in plan["pieces"]], *done, *states,
+            *halo_own[: plan["all"]], *done, *states,
             edge_filter, conv_own, mix_own, up, down,
         )
-        if received:
-            send, received[-1] = lax.optimization_barrier((send, received[-1]))
-        firsts.append(low)
-        done = [keep]
-        received.append(lax.ppermute(send, "chan", swap))
-
+        sends[plan["sent_from"]] = send
+        done = [keep] if high == firsts[1] else [keep, send]
+
+    early = lax.ppermute(sends[0], "chan", swap)
+    late, early = lax.optimization_barrier((sends[firsts[1]], early))
+    late = lax.ppermute(late, "chan", swap)
     result = jax.ShapeDtypeStruct(state_in.shape, narrow)
     placed = pl.pallas_call(
         functools.partial(place_kernel, firsts=firsts[:-1], **sizes),
@@ -452,7 +459,7 @@
         cost_estimate=cost(),
         compiler_params=limit(4),
         name="place_rows",
-    )(block_start, keep, *received[:-1])
+    )(block_start, keep, early)
 
     return pl.pallas_call(
         functools.partial(place_last_kernel, first=firsts[-1], **sizes),
@@ -464,7 +471,7 @@
         cost_estimate=cost(),
         compiler_params=limit(4),
         name="place_last_rows",
-    )(block_start, received[-1], placed)
+    )(block_start, late, placed)
 
 
 def solution(mesh):

time: 45.7 us -> 45.3 us (level)
    ppermute x3 -> x2, starting transfers between devices: 13.1 us -> 9.23 us  [the longest x1 9.15 us: per_device(): early = lax.ppermute(sends[0], 'chan', swap)]
    ppermute x1, starting transfers between devices: 0.43 us -> 4.32 us  [per_device(): up_other = lax.ppermute(up_weight, 'chan', swap)]
    ppermute x1, waiting for transfers between devices: 0.7 us -> 0.01 us  [per_device(): other = lax.ppermute(state_in, 'chan', swap)]
    ppermute x1, waiting for transfers between devices: 0.07 us -> 0.75 us  [per_device(): down_other = lax.ppermute(down_weight, 'chan', swap)]
    ppermute x2 -> x1, starting transfers between devices: 1.36 us -> 0.71 us  [per_device(): halo_other = [lax.ppermute(piece, ('lat', 'chan'), pairs) for piece in edge]]
    pallas_call x2 -> x1, Pallas kernels: 4.23 us -> 4.12 us  [per_device(): pl.pallas_call(functools.partial(first_half_kernel, plan=plan, ordered=le...]
  transfers between devices with their start and end apart: 12 -> 10, of which waited for: 4 -> 3; matrix products, arithmetic and copies ran while one was open for 0% -> 0% of each run, Pallas kernels for 53% -> 53%
where the time goes in v5:
time: 45.3 us; the launch traced here: 45 us
  Pallas kernels  24.8 us (55%)
  starting transfers between devices  17.2 us (38%)
  waiting for transfers between devices  2.67 us (6%)
    pallas_call x1, Pallas kernels, per_device(): pl.pallas_call(functools.partial(local_kernel, block_most=block_most, **s...  9.81 us
    ppermute x1, starting transfers between devices, per_device(): early = lax.ppermute(sends[0], 'chan', swap)  9.15 us
    pallas_call x3, Pallas kernels, per_device(): pl.pallas_call(functools.partial(tail_kernel, plan=plan, ordered=len(done...  7.71 us
    ppermute x1, starting transfers between devices, per_device(): up_other = lax.ppermute(up_weight, 'chan', swap)  4.32 us
    pallas_call x1, Pallas kernels, per_device(): pl.pallas_call(functools.partial(first_half_kernel, plan=plan, ordered=le...  4.12 us
    ppermute x3, starting transfers between devices, per_device(): halo_own = [lax.ppermute(piece, ('lat', 'chan'), pairs) for piece in relay]  2.21 us
    ppermute x1, waiting for transfers between devices, per_device(): up_other = lax.ppermute(up_weight, 'chan', swap)  1.45 us
    pallas_call x1, Pallas kernels, per_device(): pl.pallas_call(functools.partial(place_kernel, firsts=firsts[:-1], **size...  1.15 us
  transfers between devices with their start and end apart: 10, of which 3 were waited for; matrix products, arithmetic and copies ran while one was open for 0% of the time, Pallas kernels for 53%

profile of v5, /device:TPU:0, one launch (start us, length us, event | category | flops | bytes accessed | tf_op | source)
XLA Modules:
  0.0 45.0 jit_solution(5159740815720548900)
XLA Ops:
  0.0 0.5 %collective-permute-start = (bf16[2,1440,256]{2,1,0:T(8,128)(2,1)}, bf16[2,1440,256]{2,1,0:T(8,128)(2,1)S(1)}, u32[]{:S(2)}, u32[]{:S(2)}) collective-permute-start(bf16[2,1440,256]{2,1,0:T(8,128)(2,1)} %rows.1), channel_id=1, source_target_pairs={{0,1},{1,0},{2,3},{3,2},{4,5},{5,4},{6,7},{7,6},{8,9},{9,8},{10,11... | collective-permute-start | bytes 4423688 | tf_op jit(solution)/shard_map/ppermute | solution.py:343
  0.5 0.1 collective-permute-start.1
  0.6 1.1 %edge_row.1 = bf16[1440,256]{1,0:T(8,128)(2,1)S(1)} custom-call(bf16[2,1440,256]{2,1,0:T(8,128)(2,1)} %rows.1), custom_call_target="tpu_custom_call" | custom-call | flops 1000 | bytes 1000 | tf_op jit(solution)/shard_map/edge_row/pallas_call | solution.py:332
  1.8 0.7 %collective-permute-start.7 = (bf16[1440,256]{1,0:T(8,128)(2,1)S(1)}, bf16[1440,256]{1,0:T(8,128)(2,1)S(1)}, u32[]{:S(2)}, u32[]{:S(2)}) collective-permute-start(bf16[1440,256]{1,0:T(8,128)(2,1)S(1)} %edge_row.1), channel_id=1, source_target_pairs={{1,2},{2,1},{3,4},{4,3},{5,6},{6,5},{7,8},{8,7},{9,10},{10,9},{11,... | collective-permute-start | bytes 2211848 | tf_op jit(solution)/shard_map/ppermute | solution.py:342
  2.5 4.3 %collective-permute-start.2 = (bf16[512,512]{1,0:T(8,128)(2,1)S(1)}, bf16[512,512]{1,0:T(8,128)(2,1)S(1)}, u32[]{:S(2)}, u32[]{:S(2)}) collective-permute-start(bf16[512,512]{1,0:T(8,128)(2,1)S(1)} %copy-done.2), channel_id=1, source_target_pairs={{0,1},{1,0},{2,3},{3,2},{4,5},{5,4},{6,7},{7,6},{8,9},{9,8},{10,11... | collective-permute-start | bytes 1572872 | tf_op jit(solution)/shard_map/ppermute | solution.py:345
  6.8 0.1 collective-permute-start.3
  6.9 1.4 %collective-permute-done.2.refs_3_ = bf16[512,512]{1,0:T(8,128)(2,1)S(1)} collective-permute-done((bf16[512,512]{1,0:T(8,128)(2,1)S(1)}, bf16[512,512]{1,0:T(8,128)(2,1)S(1)}, u32[]{:S(2)}, u32[]{:S(2)}) %collective-permute-start.2) | collective-permute-done | bytes 524320 | tf_op jit(solution)/shard_map/ppermute | solution.py:345
  8.3 0.7 %collective-permute-done.3.refs_5_ = bf16[512,512]{1,0:T(8,128)(2,1)S(1)} collective-permute-done((bf16[512,512]{1,0:T(8,128)(2,1)S(1)}, bf16[512,512]{1,0:T(8,128)(2,1)S(1)}, u32[]{:S(2)}, u32[]{:S(2)}) %collective-permute-start.3) | collective-permute-done | bytes 524320 | tf_op jit(solution)/shard_map/ppermute | solution.py:346
  9.1 9.8 %local_taps.1 = (f32[18,400,256]{2,1,0:T(8,128)S(1)}, f32[18,400,256]{2,1,0:T(8,128)S(1)}, f32[1440,512]{1,0:T(8,128)S(1)}, bf16[400,320]{1,0:T(8,128)(2,1)S(1)}...) custom-call(s32[2,3]{1,0:T(2,128)S(1)} %copy-done, ...), custom_call_target="tpu_custom_call" | custom-call | flops 1000 | bytes 1000 | tf_op jit(solution)/shard_map/local_taps/pallas_call | solution.py:357
  18.9 0.1 relay_rows.1
  19.0 0.7 %collective-permute-start.4 = (bf16[640,256]{1,0:T(8,128)(2,1)S(1)}, bf16[640,256]{1,0:T(8,128)(2,1)S(1)}, u32[]{:S(2)}, u32[]{:S(2)}) collective-permute-start(bf16[640,256]{1,0:T(8,128)(2,1)S(1)} %get-tuple-element.25), channel_id=1, source_target_pairs={{1,2},{2,1},{3,4},{4,3},{5,6},{6,5},{7,8},{8,7},{9,10},{10,9},{11,... | collective-permute-start | bytes 983048 | tf_op jit(solution)/shard_map/ppermute | solution.py:388
  19.7 0.7 %collective-permute-start.5 = (bf16[400,256]{1,0:T(8,128)(2,1)S(1)}, bf16[400,256]{1,0:T(8,128)(2,1)S(1)}, u32[]{:S(2)}, u32[]{:S(2)}) collective-permute-start(bf16[400,256]{1,0:T(8,128)(2,1)S(1)} %get-tuple-element.26), channel_id=1, source_target_pairs={{1,2},{2,1},{3,4},{4,3},{5,6},{6,5},{7,8},{8,7},{9,10},{10,9},{11,... | collective-permute-start | bytes 614408 | tf_op jit(solution)/shard_map/ppermute | solution.py:388
  20.4 0.9 %collective-permute-start.6 = (bf16[400,256]{1,0:T(8,128)(2,1)S(1)}, bf16[400,256]{1,0:T(8,128)(2,1)S(1)}, u32[]{:S(2)}, u32[]{:S(2)}) collective-permute-start(bf16[400,256]{1,0:T(8,128)(2,1)S(1)} %get-tuple-element.27), channel_id=1, source_target_pairs={{1,2},{2,1},{3,4},{4,3},{5,6},{6,5},{7,8},{8,7},{9,10},{10,9},{11,... | collective-permute-start | bytes 614408 | tf_op jit(solution)/shard_map/ppermute | solution.py:388
  21.2 4.1 %edge_tap_first_half.1.refs_1_.refs_2_.refs_4_ = f32[1440,512]{1,0:T(8,128)S(1)} custom-call(bf16[1440,256]{1,0:T(8,128)(2,1)S(1)} %collective-permute-done.7.refs_0_.refs_1_, bf16[1440,256]{1,0:T(8,128)(2,1)S(1)} %collective-permute-done.7.refs_0_.refs_1_, bf16[400,320]{1,0:T(8,128)(2,1)S(1)} %get-tuple-element.24.ordered.refs_2_.refs_3_.refs_5_, ...), custom_call_target="tpu_custom_call" | custom-call | flops 60000002048 | bytes 1000 | tf_op jit(solution)/shard_map/edge_tap_first_half/pallas_call | solution.py:400
  25.4 0.0 collective-permute-done.4.refs_0_
  25.4 2.2 %edge_tap_and_feed.3 = (bf16[1440,256]{1,0:T(8,128)(2,1)S(1)}, bf16[800,256]{1,0:T(8,128)(2,1)S(1)}) custom-call(bf16[640,256]{1,0:T(8,128)(2,1)S(1)} %collective-permute-done.4.refs_0_, f32[1440,512]{1,0:T(8,128)S(1)} %edge_tap_first_half.1.refs_1_.refs_2_.refs_4_, f32[1440,512]{1,0:T(8,128)S(1)} %edge_tap_first_half.1.refs_1_.refs_2_.refs_4_, ...), custom_call_target="tpu_custom_call" | custom-call | flops 1000 | bytes 1000 | tf_op jit(solution)/shard_map/edge_tap_and_feed/pallas_call | solution.py:430
  27.6 0.0 collective-permute-done.5.refs_1_
  27.6 2.2 %edge_tap_and_feed.4 = (bf16[1440,256]{1,0:T(8,128)(2,1)S(1)}, bf16[800,256]{1,0:T(8,128)(2,1)S(1)}) custom-call(bf16[640,256]{1,0:T(8,128)(2,1)S(1)} %collective-permute-done.4.refs_0_, bf16[400,256]{1,0:T(8,128)(2,1)S(1)} %collective-permute-done.5.refs_1_, ...), custom_call_target="tpu_custom_call", output_to_operand_aliasing={{0}: (2, {}), {1}: (3, {})} | custom-call | flops 1000 | bytes 1000 | tf_op jit(solution)/shard_map/edge_tap_and_feed/pallas_call | solution.py:430
  29.8 9.2 %collective-permute-start.8 = (bf16[800,256]{1,0:T(8,128)(2,1)S(1)}, bf16[800,256]{1,0:T(8,128)(2,1)S(1)}, u32[]{:S(2)}, u32[]{:S(2)}) collective-permute-start(bf16[800,256]{1,0:T(8,128)(2,1)S(1)} %get-tuple-element.39), channel_id=1, source_target_pairs={{0,1},{1,0},{2,3},{3,2},{4,5},{5,4},{6,7},{7,6},{8,9},{9,8},{10,11... | collective-permute-start | bytes 1228808 | tf_op jit(solution)/shard_map/ppermute | solution.py:449
  39.0 3.3 %edge_tap_and_feed.5 = (bf16[1440,256]{1,0:T(8,128)(2,1)S(1)}, bf16[640,256]{1,0:T(8,128)(2,1)S(1)}) custom-call(bf16[640,256]{1,0:T(8,128)(2,1)S(1)} %collective-permute-done.4.refs_0_, bf16[400,256]{1,0:T(8,128)(2,1)S(1)} %collective-permute-done.5.refs_1_, bf16[400,256]{1,0:T(8,128)(2,1)S(1)} %collective-permute-done.6.refs_2_, ...), custom_call_target="tpu_custom_call", output_to_operand_aliasing={{0}: (3, {})} | custom-call | flops 10000000000 | bytes 1000 | tf_op jit(solution)/shard_map/edge_tap_and_feed/pallas_call | solution.py:430
  42.3 0.1 collective-permute-start.9
  42.4 1.1 %place_rows.1.before = bf16[2,1440,256]{2,1,0:T(8,128)(2,1)} custom-call(s32[2,3]{1,0:T(2,128)S(1)} %copy-done, bf16[1440,256]{1,0:T(8,128)(2,1)S(1)} %get-tuple-element.41.keep, bf16[800,256]{1,0:T(8,128)(2,1)S(1)} %collective-permute-done.8.refs_0_), custom_call_target="tpu_custom_call" | custom-call | flops 1000 | bytes 1000 | tf_op jit(solution)/shard_map/place_rows/pallas_call | solution.py:453
  43.5 0.5 %collective-permute-done.9.source = bf16[640,256]{1,0:T(8,128)(2,1)S(1)} collective-permute-done((bf16[640,256]{1,0:T(8,128)(2,1)S(1)}, bf16[640,256]{1,0:T(8,128)(2,1)S(1)}, u32[]{:S(2)}, u32[]{:S(2)}) %collective-permute-start.9) | collective-permute-done | bytes 327712 | tf_op jit(solution)/shard_map/ppermute | solution.py:451
  44.0 0.9 %place_last_rows.1 = bf16[2,1440,256]{2,1,0:T(8,128)(2,1)} custom-call(s32[2,3]{1,0:T(2,128)S(1)} %copy-done, bf16[640,256]{1,0:T(8,128)(2,1)S(1)} %collective-permute-done.9.source, bf16[2,1440,256]{2,1,0:T(8,128)(2,1)} %place_rows.1.before), custom_call_target="tpu_custom_call", output_to_operand_aliasing={{}: (2, {})} | custom-call | flops 1000 | bytes 1000 | tf_op jit(solution)/shard_map/place_last_rows/pallas_call | solution.py:464
  (13 shorter events, 0.0 us)
Async XLA Ops:
  0.0 2.5 %copy-start.2 = (bf16[512,512]{1,0:T(8,128)(2,1)S(1)}, bf16[512,512]{1,0:T(8,128)(2,1)}, u32[]{:S(2)}) copy-start(bf16[512,512]{1,0:T(8,128)(2,1)} %refs_2_.1) | copy-start | bytes 1572868
  0.0 6.8 %copy-start.3 = (bf16[512,512]{1,0:T(8,128)(2,1)S(1)}, bf16[512,512]{1,0:T(8,128)(2,1)}, u32[]{:S(2)}) copy-start(bf16[512,512]{1,0:T(8,128)(2,1)} %refs_4_.1) | copy-start | bytes 1572868
  0.0 9.1 %copy-start = (s32[2,3]{1,0:T(2,128)S(1)}, s32[2,3]{1,0:T(2,128)}, u32[]{:S(2)}) copy-start(s32[2,3]{1,0:T(2,128)} %block_start.5) | copy-start | bytes 76
  0.0 9.1 %copy-start.1 = (s32[2,3]{1,0:T(2,128)S(1)}, s32[2,3]{1,0:T(2,128)}, u32[]{:S(2)}) copy-start(s32[2,3]{1,0:T(2,128)} %block_count.1) | copy-start | bytes 76
  0.0 9.1 %collective-permute-start = (bf16[2,1440,256]{2,1,0:T(8,128)(2,1)}, bf16[2,1440,256]{2,1,0:T(8,128)(2,1)S(1)}, u32[]{:S(2)}, u32[]{:S(2)}) collective-permute-start(bf16[2,1440,256]{2,1,0:T(8,128)(2,1)} %rows.1), channel_id=1, source_target_pairs={{0,1},{1,0},{2,3},{3,2},{4,5},{5,4},{6,7},{7,6},{8,9},{9,8},{10,11... | collective-permute-start | bytes 4423688 | tf_op jit(solution)/shard_map/ppermute | solution.py:343
  0.5 8.6 %collective-permute-start.1 = (bf16[5,256,512]{2,1,0:T(8,128)(2,1)}, bf16[5,256,512]{2,1,0:T(8,128)(2,1)S(1)}, u32[]{:S(2)}, u32[]{:S(2)}) collective-permute-start(bf16[5,256,512]{2,1,0:T(8,128)(2,1)} %param.11), channel_id=1, source_target_pairs={{0,1},{1,0},{2,3},{3,2},{4,5},{5,4},{6,7},{7,6},{8,9},{9,8},{10,11... | collective-permute-start | bytes 3932168 | tf_op jit(solution)/shard_map/ppermute | solution.py:344
  1.8 19.5 %collective-permute-start.7 = (bf16[1440,256]{1,0:T(8,128)(2,1)S(1)}, bf16[1440,256]{1,0:T(8,128)(2,1)S(1)}, u32[]{:S(2)}, u32[]{:S(2)}) collective-permute-start(bf16[1440,256]{1,0:T(8,128)(2,1)S(1)} %edge_row.1), channel_id=1, source_target_pairs={{1,2},{2,1},{3,4},{4,3},{5,6},{6,5},{7,8},{8,7},{9,10},{10,9},{11,... | collective-permute-start | bytes 2211848 | tf_op jit(solution)/shard_map/ppermute | solution.py:342
  2.5 5.9 %collective-permute-start.2 = (bf16[512,512]{1,0:T(8,128)(2,1)S(1)}, bf16[512,512]{1,0:T(8,128)(2,1)S(1)}, u32[]{:S(2)}, u32[]{:S(2)}) collective-permute-start(bf16[512,512]{1,0:T(8,128)(2,1)S(1)} %copy-done.2), channel_id=1, source_target_pairs={{0,1},{1,0},{2,3},{3,2},{4,5},{5,4},{6,7},{7,6},{8,9},{9,8},{10,11... | collective-permute-start | bytes 1572872 | tf_op jit(solution)/shard_map/ppermute | solution.py:345
  6.8 2.3 %collective-permute-start.3 = (bf16[512,512]{1,0:T(8,128)(2,1)S(1)}, bf16[512,512]{1,0:T(8,128)(2,1)S(1)}, u32[]{:S(2)}, u32[]{:S(2)}) collective-permute-start(bf16[512,512]{1,0:T(8,128)(2,1)S(1)} %copy-done.3), channel_id=1, source_target_pairs={{0,1},{1,0},{2,3},{3,2},{4,5},{5,4},{6,7},{7,6},{8,9},{9,8},{10,11... | collective-permute-start | bytes 1572872 | tf_op jit(solution)/shard_map/ppermute | solution.py:346
  19.0 6.4 %collective-permute-start.4 = (bf16[640,256]{1,0:T(8,128)(2,1)S(1)}, bf16[640,256]{1,0:T(8,128)(2,1)S(1)}, u32[]{:S(2)}, u32[]{:S(2)}) collective-permute-start(bf16[640,256]{1,0:T(8,128)(2,1)S(1)} %get-tuple-element.25), channel_id=1, source_target_pairs={{1,2},{2,1},{3,4},{4,3},{5,6},{6,5},{7,8},{8,7},{9,10},{10,9},{11,... | collective-permute-start | bytes 983048 | tf_op jit(solution)/shard_map/ppermute | solution.py:388
  19.7 7.9 %collective-permute-start.5 = (bf16[400,256]{1,0:T(8,128)(2,1)S(1)}, bf16[400,256]{1,0:T(8,128)(2,1)S(1)}, u32[]{:S(2)}, u32[]{:S(2)}) collective-permute-start(bf16[400,256]{1,0:T(8,128)(2,1)S(1)} %get-tuple-element.26), channel_id=1, source_target_pairs={{1,2},{2,1},{3,4},{4,3},{5,6},{6,5},{7,8},{8,7},{9,10},{10,9},{11,... | collective-permute-start | bytes 614408 | tf_op jit(solution)/shard_map/ppermute | solution.py:388
  20.4 18.6 %collective-permute-start.6 = (bf16[400,256]{1,0:T(8,128)(2,1)S(1)}, bf16[400,256]{1,0:T(8,128)(2,1)S(1)}, u32[]{:S(2)}, u32[]{:S(2)}) collective-permute-start(bf16[400,256]{1,0:T(8,128)(2,1)S(1)} %get-tuple-element.27), channel_id=1, source_target_pairs={{1,2},{2,1},{3,4},{4,3},{5,6},{6,5},{7,8},{8,7},{9,10},{10,9},{11,... | collective-permute-start | bytes 614408 | tf_op jit(solution)/shard_map/ppermute | solution.py:388
  29.8 12.5 %collective-permute-start.8 = (bf16[800,256]{1,0:T(8,128)(2,1)S(1)}, bf16[800,256]{1,0:T(8,128)(2,1)S(1)}, u32[]{:S(2)}, u32[]{:S(2)}) collective-permute-start(bf16[800,256]{1,0:T(8,128)(2,1)S(1)} %get-tuple-element.39), channel_id=1, source_target_pairs={{0,1},{1,0},{2,3},{3,2},{4,5},{5,4},{6,7},{7,6},{8,9},{9,8},{10,11... | collective-permute-start | bytes 1228808 | tf_op jit(solution)/shard_map/ppermute | solution.py:449
  42.3 1.7 %collective-permute-start.9 = (bf16[640,256]{1,0:T(8,128)(2,1)S(1)}, bf16[640,256]{1,0:T(8,128)(2,1)S(1)}, u32[]{:S(2)}, u32[]{:S(2)}) collective-permute-start(bf16[640,256]{1,0:T(8,128)(2,1)S(1)} %get-tuple-element.40), channel_id=1, source_target_pairs={{0,1},{1,0},{2,3},{3,2},{4,5},{5,4},{6,7},{7,6},{8,9},{9,8},{10,11... | collective-permute-start | bytes 983048 | tf_op jit(solution)/shard_map/ppermute | solution.py:451

commit v6 on v5

--- a/solution.py
+++ b/solution.py
@@ -131,16 +131,24 @@
     wait_all(weight_copies)
 
 
-def halo_mix(first, places, block_width, halves, spans, edge_filter, conv_local, mix, window, conv):
+def by_count(rows, filters, block_width, body):
+    depth = filters.shape[1]
+    row = rows // lax.axis_size("lat") * lax.axis_index("lat") + lax.axis_index("chan")
+    few = 3 * (rows - row) * (rows - row) < 2 * rows * rows
+    short = min(depth, -(-(depth - block_width) // 128) * 128)
+    pl.when(few)(lambda: body(short))
+    pl.when(jnp.logical_not(few))(lambda: body(depth))
+
+
+def halo_mix(depth, first, places, block_width, halves, spans, edge_filter, conv_local, mix, window, conv):
     at = 0
     for half, (low, high) in zip(halves, spans):
         window[at : at + high - low, :] = half[low:high, :]
         at += high - low
-    depth = edge_filter.shape[1]
     width = window.shape[1]
     for slot in range(places):
         result = conv_local[first + slot] + jnp.dot(
-            edge_filter[...], window[slot * block_width : slot * block_width + depth, :],
+            edge_filter[:, :depth], window[slot * block_width : slot * block_width + depth, :],
             preferred_element_type=jnp.float32,
         )
         rounded = result.astype(jnp.bfloat16)
@@ -151,41 +159,49 @@
     return jnp.dot(conv[...], mix[...], preferred_element_type=jnp.float32)
 
 
-def first_half_kernel(*refs, plan, ordered, block_width):
+def first_half_kernel(*refs, plan, ordered, block_width, rows):
     halves, refs = refs[: len(plan["spans"])], refs[len(plan["spans"]) + ordered :]
     edge_filter, conv_local, mix, residual, result, window, conv = refs
     first, places = plan["first"], plan["places"]
-    mixed = halo_mix(
-        first, places, block_width, halves, plan["spans"], edge_filter, conv_local, mix, window, conv
-    )
-    result[...] = residual[first * block_width : (first + places) * block_width, :] + mixed
+
+    def body(depth):
+        mixed = halo_mix(
+            depth, first, places, block_width, halves, plan["spans"], edge_filter, conv_local, mix, window, conv
+        )
+        result[...] = residual[first * block_width : (first + places) * block_width, :] + mixed
+
+    by_count(rows, edge_filter, block_width, body)
 
 
 def gelu(x):
     return 0.5 * x * (1.0 + lax.erf(x * 0.7071067811865476))
 
 
-def tail_kernel(*refs, plan, ordered, block_width, state_spans):
+def tail_kernel(*refs, plan, ordered, block_width, state_spans, rows):
     count = plan["all"]
     halves, refs = [refs[piece] for piece in plan["pieces"]], refs[count + ordered :]
     partials, refs = refs[: len(state_spans)], refs[len(state_spans) :]
     edge_filter, conv_local, mix, up, down, keep, send, window, conv = refs
-    mixed = halo_mix(
-        plan["first"], plan["places"], block_width, halves, plan["spans"], edge_filter, conv_local, mix,
-        window, conv,
-    )
-    before = [partial[low:high, :] for partial, (low, high) in zip(partials, state_spans)]
-    state = mixed + (before[0] if len(before) == 1 else jnp.concatenate(before, axis=0))
-    width = send.shape[1]
-    hidden = gelu(
-        jnp.dot(state.astype(jnp.bfloat16), up[...], preferred_element_type=jnp.float32)
-    ).astype(jnp.bfloat16)
-    total = state + jnp.dot(hidden, down[...], preferred_element_type=jnp.float32)
-    total = total.astype(jnp.bfloat16)
-    first = plan["first"] * block_width
-    keep[first : first + total.shape[0], :] = total[:, :width]
-    first -= plan["sent_from"] * block_width
-    send[first : first + total.shape[0], :] = total[:, width:]
+
+    def body(depth):
+        mixed = halo_mix(
+            depth, plan["first"], plan["places"], block_width, halves, plan["spans"], edge_filter, conv_local, mix,
+            window, conv,
+        )
+        before = [partial[low:high, :] for partial, (low, high) in zip(partials, state_spans)]
+        state = mixed + (before[0] if len(before) == 1 else jnp.concatenate(before, axis=0))
+        width = send.shape[1]
+        hidden = gelu(
+            jnp.dot(state.astype(jnp.bfloat16), up[...], preferred_element_type=jnp.float32)
+        ).astype(jnp.bfloat16)
+        total = state + jnp.dot(hidden, down[...], preferred_element_type=jnp.float32)
+        total = total.astype(jnp.bfloat16)
+        first = plan["first"] * block_width
+        keep[first : first + total.shape[0], :] = total[:, :width]
+        first -= plan["sent_from"] * block_width
+        send[first : first + total.shape[0], :] = total[:, width:]
+
+    by_count(rows, edge_filter, block_width, body)
 
 
 def begin_place(source, result, row, home, sem, lon_blocks, block_width):
@@ -398,7 +414,9 @@
     for plan in first_plans:
         done = partials[-1:]
         partials.append(pl.pallas_call(
-            functools.partial(first_half_kernel, plan=plan, ordered=len(done), block_width=block_width),
+            functools.partial(
+                first_half_kernel, plan=plan, ordered=len(done), block_width=block_width, rows=local_rows * bands
+            ),
             out_shape=jax.ShapeDtypeStruct((plan["places"] * block_width, channels), jnp.float32),
             in_specs=vmem(len(plan["pieces"])) + anywhere(len(done)) + vmem(4),
             out_specs=vmem(1)[0],
@@ -429,7 +447,8 @@
         used = [vmem(1) if piece in plan["pieces"] else anywhere(1) for piece in range(plan["all"])]
         keep, send = pl.pallas_call(
             functools.partial(
-                tail_kernel, plan=plan, ordered=len(done), block_width=block_width, state_spans=state_spans
+                tail_kernel, plan=plan, ordered=len(done), block_width=block_width, state_spans=state_spans,
+                rows=local_rows * bands,
             ),
             out_shape=[jax.ShapeDtypeStruct((size, width), narrow) for size in (cells, sent * block_width)],
             in_specs=sum(used, []) + anywhere(len(done)) + vmem(len(states) + 5),

time: 45.3 us -> 45.1 us (level)
  transfers between devices with their start and end apart: 10 -> 10, of which waited for: 3 -> 3; matrix products, arithmetic and copies ran while one was open for 0% -> 0% of each run, Pallas kernels for 53% -> 54%
where the time goes in v6:
time: 45.1 us; the launch traced here: 44.9 us
  Pallas kernels  25 us (55%)
  starting transfers between devices  16.9 us (37%)
  waiting for transfers between devices  2.65 us (6%)
    pallas_call x1, Pallas kernels, per_device(): pl.pallas_call(functools.partial(local_kernel, block_most=block_most, **s...  9.81 us
    ppermute x1, starting transfers between devices, per_device(): early = lax.ppermute(sends[0], 'chan', swap)  9.07 us
    pallas_call x3, Pallas kernels, per_device(): pl.pallas_call(functools.partial(tail_kernel, plan=plan, ordered=len(done...  7.87 us
    ppermute x1, starting transfers between devices, per_device(): up_other = lax.ppermute(up_weight, 'chan', swap)  4.32 us
    pallas_call x1, Pallas kernels, per_device(): pl.pallas_call(functools.partial(first_half_kernel, plan=plan, ordered=le...  4.16 us
    ppermute x3, starting transfers between devices, per_device(): halo_own = [lax.ppermute(piece, ('lat', 'chan'), pairs) for piece in relay]  2.03 us
    ppermute x1, waiting for transfers between devices, per_device(): up_other = lax.ppermute(up_weight, 'chan', swap)  1.45 us
    pallas_call x1, Pallas kernels, per_device(): pl.pallas_call(functools.partial(place_kernel, firsts=firsts[:-1], **size...  1.15 us
  transfers between devices with their start and end apart: 10, of which 3 were waited for; matrix products, arithmetic and copies ran while one was open for 0% of the time, Pallas kernels for 54%

profile of v6, /device:TPU:0, one launch (start us, length us, event | category | flops | bytes accessed | tf_op | source)
XLA Modules:
  0.0 44.9 jit_solution(10657787340274581988)
XLA Ops:
  0.0 0.5 %collective-permute-start = (bf16[2,1440,256]{2,1,0:T(8,128)(2,1)}, bf16[2,1440,256]{2,1,0:T(8,128)(2,1)S(1)}, u32[]{:S(2)}, u32[]{:S(2)}) collective-permute-start(bf16[2,1440,256]{2,1,0:T(8,128)(2,1)} %rows.1), channel_id=1, source_target_pairs={{0,1},{1,0},{2,3},{3,2},{4,5},{5,4},{6,7},{7,6},{8,9},{9,8},{10,11... | collective-permute-start | bytes 4423688 | tf_op jit(solution)/shard_map/ppermute | solution.py:359
  0.5 0.1 collective-permute-start.1
  0.6 1.1 %edge_row.1 = bf16[1440,256]{1,0:T(8,128)(2,1)S(1)} custom-call(bf16[2,1440,256]{2,1,0:T(8,128)(2,1)} %rows.1), custom_call_target="tpu_custom_call" | custom-call | flops 1000 | bytes 1000 | tf_op jit(solution)/shard_map/edge_row/pallas_call | solution.py:348
  1.8 0.7 %collective-permute-start.7 = (bf16[1440,256]{1,0:T(8,128)(2,1)S(1)}, bf16[1440,256]{1,0:T(8,128)(2,1)S(1)}, u32[]{:S(2)}, u32[]{:S(2)}) collective-permute-start(bf16[1440,256]{1,0:T(8,128)(2,1)S(1)} %edge_row.1), channel_id=1, source_target_pairs={{1,2},{2,1},{3,4},{4,3},{5,6},{6,5},{7,8},{8,7},{9,10},{10,9},{11,... | collective-permute-start | bytes 2211848 | tf_op jit(solution)/shard_map/ppermute | solution.py:358
  2.5 4.3 %collective-permute-start.2 = (bf16[512,512]{1,0:T(8,128)(2,1)S(1)}, bf16[512,512]{1,0:T(8,128)(2,1)S(1)}, u32[]{:S(2)}, u32[]{:S(2)}) collective-permute-start(bf16[512,512]{1,0:T(8,128)(2,1)S(1)} %copy-done.2), channel_id=1, source_target_pairs={{0,1},{1,0},{2,3},{3,2},{4,5},{5,4},{6,7},{7,6},{8,9},{9,8},{10,11... | collective-permute-start | bytes 1572872 | tf_op jit(solution)/shard_map/ppermute | solution.py:361
  6.8 0.1 collective-permute-start.3
  6.9 1.4 %collective-permute-done.2.refs_3_ = bf16[512,512]{1,0:T(8,128)(2,1)S(1)} collective-permute-done((bf16[512,512]{1,0:T(8,128)(2,1)S(1)}, bf16[512,512]{1,0:T(8,128)(2,1)S(1)}, u32[]{:S(2)}, u32[]{:S(2)}) %collective-permute-start.2) | collective-permute-done | bytes 524320 | tf_op jit(solution)/shard_map/ppermute | solution.py:361
  8.3 0.7 %collective-permute-done.3.refs_5_ = bf16[512,512]{1,0:T(8,128)(2,1)S(1)} collective-permute-done((bf16[512,512]{1,0:T(8,128)(2,1)S(1)}, bf16[512,512]{1,0:T(8,128)(2,1)S(1)}, u32[]{:S(2)}, u32[]{:S(2)}) %collective-permute-start.3) | collective-permute-done | bytes 524320 | tf_op jit(solution)/shard_map/ppermute | solution.py:362
  9.1 0.0 collective-permute-done.1
  9.1 0.0 collective-permute-done.other
  9.1 9.8 %local_taps.1 = (f32[18,400,256]{2,1,0:T(8,128)S(1)}, f32[18,400,256]{2,1,0:T(8,128)S(1)}, f32[1440,512]{1,0:T(8,128)S(1)}, bf16[400,320]{1,0:T(8,128)(2,1)S(1)}...) custom-call(s32[2,3]{1,0:T(2,128)S(1)} %copy-done, ...), custom_call_target="tpu_custom_call" | custom-call | flops 1000 | bytes 1000 | tf_op jit(solution)/shard_map/local_taps/pallas_call | solution.py:373
  18.9 0.1 relay_rows.1
  19.0 0.7 %collective-permute-start.4 = (bf16[640,256]{1,0:T(8,128)(2,1)S(1)}, bf16[640,256]{1,0:T(8,128)(2,1)S(1)}, u32[]{:S(2)}, u32[]{:S(2)}) collective-permute-start(bf16[640,256]{1,0:T(8,128)(2,1)S(1)} %get-tuple-element.25), channel_id=1, source_target_pairs={{1,2},{2,1},{3,4},{4,3},{5,6},{6,5},{7,8},{8,7},{9,10},{10,9},{11,... | collective-permute-start | bytes 983048 | tf_op jit(solution)/shard_map/ppermute | solution.py:404
  19.7 0.7 %collective-permute-start.5 = (bf16[400,256]{1,0:T(8,128)(2,1)S(1)}, bf16[400,256]{1,0:T(8,128)(2,1)S(1)}, u32[]{:S(2)}, u32[]{:S(2)}) collective-permute-start(bf16[400,256]{1,0:T(8,128)(2,1)S(1)} %get-tuple-element.26), channel_id=1, source_target_pairs={{1,2},{2,1},{3,4},{4,3},{5,6},{6,5},{7,8},{8,7},{9,10},{10,9},{11,... | collective-permute-start | bytes 614408 | tf_op jit(solution)/shard_map/ppermute | solution.py:404
  20.4 0.7 %collective-permute-start.6 = (bf16[400,256]{1,0:T(8,128)(2,1)S(1)}, bf16[400,256]{1,0:T(8,128)(2,1)S(1)}, u32[]{:S(2)}, u32[]{:S(2)}) collective-permute-start(bf16[400,256]{1,0:T(8,128)(2,1)S(1)} %get-tuple-element.27), channel_id=1, source_target_pairs={{1,2},{2,1},{3,4},{4,3},{5,6},{6,5},{7,8},{8,7},{9,10},{10,9},{11,... | collective-permute-start | bytes 614408 | tf_op jit(solution)/shard_map/ppermute | solution.py:404
  21.1 4.2 %edge_tap_first_half.1.refs_1_.refs_2_.refs_4_ = f32[1440,512]{1,0:T(8,128)S(1)} custom-call(bf16[1440,256]{1,0:T(8,128)(2,1)S(1)} %collective-permute-done.7.refs_0_.refs_1_, bf16[1440,256]{1,0:T(8,128)(2,1)S(1)} %collective-permute-done.7.refs_0_.refs_1_, bf16[400,320]{1,0:T(8,128)(2,1)S(1)} %get-tuple-element.24.ordered.refs_2_.refs_3_.refs_5_, ...), custom_call_target="tpu_custom_call" | custom-call | flops 60000002048 | bytes 1000 | tf_op jit(solution)/shard_map/edge_tap_first_half/pallas_call | solution.py:416
  25.2 2.4 %edge_tap_and_feed.3 = (bf16[1440,256]{1,0:T(8,128)(2,1)S(1)}, bf16[800,256]{1,0:T(8,128)(2,1)S(1)}) custom-call(bf16[640,256]{1,0:T(8,128)(2,1)S(1)} %collective-permute-done.4.refs_0_, f32[1440,512]{1,0:T(8,128)S(1)} %edge_tap_first_half.1.refs_1_.refs_2_.refs_4_, f32[1440,512]{1,0:T(8,128)S(1)} %edge_tap_first_half.1.refs_1_.refs_2_.refs_4_, ...), custom_call_target="tpu_custom_call" | custom-call | flops 1000 | bytes 1000 | tf_op jit(solution)/shard_map/edge_tap_and_feed/pallas_call | solution.py:448
  27.6 2.2 %edge_tap_and_feed.4 = (bf16[1440,256]{1,0:T(8,128)(2,1)S(1)}, bf16[800,256]{1,0:T(8,128)(2,1)S(1)}) custom-call(bf16[640,256]{1,0:T(8,128)(2,1)S(1)} %collective-permute-done.4.refs_0_, bf16[400,256]{1,0:T(8,128)(2,1)S(1)} %collective-permute-done.5.refs_1_, ...), custom_call_target="tpu_custom_call", output_to_operand_aliasing={{0}: (2, {}), {1}: (3, {})} | custom-call | flops 1000 | bytes 1000 | tf_op jit(solution)/shard_map/edge_tap_and_feed/pallas_call | solution.py:448
  29.8 9.1 %collective-permute-start.8 = (bf16[800,256]{1,0:T(8,128)(2,1)S(1)}, bf16[800,256]{1,0:T(8,128)(2,1)S(1)}, u32[]{:S(2)}, u32[]{:S(2)}) collective-permute-start(bf16[800,256]{1,0:T(8,128)(2,1)S(1)} %get-tuple-element.39), channel_id=1, source_target_pairs={{0,1},{1,0},{2,3},{3,2},{4,5},{5,4},{6,7},{7,6},{8,9},{9,8},{10,11... | collective-permute-start | bytes 1228808 | tf_op jit(solution)/shard_map/ppermute | solution.py:468
  38.9 3.3 %edge_tap_and_feed.5 = (bf16[1440,256]{1,0:T(8,128)(2,1)S(1)}, bf16[640,256]{1,0:T(8,128)(2,1)S(1)}) custom-call(bf16[640,256]{1,0:T(8,128)(2,1)S(1)} %collective-permute-done.4.refs_0_, bf16[400,256]{1,0:T(8,128)(2,1)S(1)} %collective-permute-done.5.refs_1_, bf16[400,256]{1,0:T(8,128)(2,1)S(1)} %collective-permute-done.6.refs_2_, ...), custom_call_target="tpu_custom_call", output_to_operand_aliasing={{0}: (3, {})} | custom-call | flops 10000000000 | bytes 1000 | tf_op jit(solution)/shard_map/edge_tap_and_feed/pallas_call | solution.py:448
  42.2 0.1 collective-permute-start.9
  42.3 1.1 %place_rows.1.before = bf16[2,1440,256]{2,1,0:T(8,128)(2,1)} custom-call(s32[2,3]{1,0:T(2,128)S(1)} %copy-done, bf16[1440,256]{1,0:T(8,128)(2,1)S(1)} %get-tuple-element.41.keep, bf16[800,256]{1,0:T(8,128)(2,1)S(1)} %collective-permute-done.8.refs_0_), custom_call_target="tpu_custom_call" | custom-call | flops 1000 | bytes 1000 | tf_op jit(solution)/shard_map/place_rows/pallas_call | solution.py:472
  43.5 0.4 collective-permute-done.9.source
  43.9 0.9 %place_last_rows.1 = bf16[2,1440,256]{2,1,0:T(8,128)(2,1)} custom-call(s32[2,3]{1,0:T(2,128)S(1)} %copy-done, bf16[640,256]{1,0:T(8,128)(2,1)S(1)} %collective-permute-done.9.source, bf16[2,1440,256]{2,1,0:T(8,128)(2,1)} %place_rows.1.before), custom_call_target="tpu_custom_call", output_to_operand_aliasing={{}: (2, {})} | custom-call | flops 1000 | bytes 1000 | tf_op jit(solution)/shard_map/place_last_rows/pallas_call | solution.py:483
  (13 shorter events, 0.0 us)
Async XLA Ops:
  0.0 2.5 %copy-start.2 = (bf16[512,512]{1,0:T(8,128)(2,1)S(1)}, bf16[512,512]{1,0:T(8,128)(2,1)}, u32[]{:S(2)}) copy-start(bf16[512,512]{1,0:T(8,128)(2,1)} %refs_2_.1) | copy-start | bytes 1572868
  0.0 6.8 %copy-start.3 = (bf16[512,512]{1,0:T(8,128)(2,1)S(1)}, bf16[512,512]{1,0:T(8,128)(2,1)}, u32[]{:S(2)}) copy-start(bf16[512,512]{1,0:T(8,128)(2,1)} %refs_4_.1) | copy-start | bytes 1572868
  0.0 9.1 %copy-start = (s32[2,3]{1,0:T(2,128)S(1)}, s32[2,3]{1,0:T(2,128)}, u32[]{:S(2)}) copy-start(s32[2,3]{1,0:T(2,128)} %block_start.5) | copy-start | bytes 76
  0.0 9.1 %copy-start.1 = (s32[2,3]{1,0:T(2,128)S(1)}, s32[2,3]{1,0:T(2,128)}, u32[]{:S(2)}) copy-start(s32[2,3]{1,0:T(2,128)} %block_count.1) | copy-start | bytes 76
  0.0 9.1 %collective-permute-start = (bf16[2,1440,256]{2,1,0:T(8,128)(2,1)}, bf16[2,1440,256]{2,1,0:T(8,128)(2,1)S(1)}, u32[]{:S(2)}, u32[]{:S(2)}) collective-permute-start(bf16[2,1440,256]{2,1,0:T(8,128)(2,1)} %rows.1), channel_id=1, source_target_pairs={{0,1},{1,0},{2,3},{3,2},{4,5},{5,4},{6,7},{7,6},{8,9},{9,8},{10,11... | collective-permute-start | bytes 4423688 | tf_op jit(solution)/shard_map/ppermute | solution.py:359
  0.5 8.6 %collective-permute-start.1 = (bf16[5,256,512]{2,1,0:T(8,128)(2,1)}, bf16[5,256,512]{2,1,0:T(8,128)(2,1)S(1)}, u32[]{:S(2)}, u32[]{:S(2)}) collective-permute-start(bf16[5,256,512]{2,1,0:T(8,128)(2,1)} %param.11), channel_id=1, source_target_pairs={{0,1},{1,0},{2,3},{3,2},{4,5},{5,4},{6,7},{7,6},{8,9},{9,8},{10,11... | collective-permute-start | bytes 3932168 | tf_op jit(solution)/shard_map/ppermute | solution.py:360
  1.8 19.3 %collective-permute-start.7 = (bf16[1440,256]{1,0:T(8,128)(2,1)S(1)}, bf16[1440,256]{1,0:T(8,128)(2,1)S(1)}, u32[]{:S(2)}, u32[]{:S(2)}) collective-permute-start(bf16[1440,256]{1,0:T(8,128)(2,1)S(1)} %edge_row.1), channel_id=1, source_target_pairs={{1,2},{2,1},{3,4},{4,3},{5,6},{6,5},{7,8},{8,7},{9,10},{10,9},{11,... | collective-permute-start | bytes 2211848 | tf_op jit(solution)/shard_map/ppermute | solution.py:358
  2.5 5.9 %collective-permute-start.2 = (bf16[512,512]{1,0:T(8,128)(2,1)S(1)}, bf16[512,512]{1,0:T(8,128)(2,1)S(1)}, u32[]{:S(2)}, u32[]{:S(2)}) collective-permute-start(bf16[512,512]{1,0:T(8,128)(2,1)S(1)} %copy-done.2), channel_id=1, source_target_pairs={{0,1},{1,0},{2,3},{3,2},{4,5},{5,4},{6,7},{7,6},{8,9},{9,8},{10,11... | collective-permute-start | bytes 1572872 | tf_op jit(solution)/shard_map/ppermute | solution.py:361
  6.8 2.3 %collective-permute-start.3 = (bf16[512,512]{1,0:T(8,128)(2,1)S(1)}, bf16[512,512]{1,0:T(8,128)(2,1)S(1)}, u32[]{:S(2)}, u32[]{:S(2)}) collective-permute-start(bf16[512,512]{1,0:T(8,128)(2,1)S(1)} %copy-done.3), channel_id=1, source_target_pairs={{0,1},{1,0},{2,3},{3,2},{4,5},{5,4},{6,7},{7,6},{8,9},{9,8},{10,11... | collective-permute-start | bytes 1572872 | tf_op jit(solution)/shard_map/ppermute | solution.py:362
  19.0 6.2 %collective-permute-start.4 = (bf16[640,256]{1,0:T(8,128)(2,1)S(1)}, bf16[640,256]{1,0:T(8,128)(2,1)S(1)}, u32[]{:S(2)}, u32[]{:S(2)}) collective-permute-start(bf16[640,256]{1,0:T(8,128)(2,1)S(1)} %get-tuple-element.25), channel_id=1, source_target_pairs={{1,2},{2,1},{3,4},{4,3},{5,6},{6,5},{7,8},{8,7},{9,10},{10,9},{11,... | collective-permute-start | bytes 983048 | tf_op jit(solution)/shard_map/ppermute | solution.py:404
  19.7 7.9 %collective-permute-start.5 = (bf16[400,256]{1,0:T(8,128)(2,1)S(1)}, bf16[400,256]{1,0:T(8,128)(2,1)S(1)}, u32[]{:S(2)}, u32[]{:S(2)}) collective-permute-start(bf16[400,256]{1,0:T(8,128)(2,1)S(1)} %get-tuple-element.26), channel_id=1, source_target_pairs={{1,2},{2,1},{3,4},{4,3},{5,6},{6,5},{7,8},{8,7},{9,10},{10,9},{11,... | collective-permute-start | bytes 614408 | tf_op jit(solution)/shard_map/ppermute | solution.py:404
  20.4 18.5 %collective-permute-start.6 = (bf16[400,256]{1,0:T(8,128)(2,1)S(1)}, bf16[400,256]{1,0:T(8,128)(2,1)S(1)}, u32[]{:S(2)}, u32[]{:S(2)}) collective-permute-start(bf16[400,256]{1,0:T(8,128)(2,1)S(1)} %get-tuple-element.27), channel_id=1, source_target_pairs={{1,2},{2,1},{3,4},{4,3},{5,6},{6,5},{7,8},{8,7},{9,10},{10,9},{11,... | collective-permute-start | bytes 614408 | tf_op jit(solution)/shard_map/ppermute | solution.py:404
  29.8 12.4 %collective-permute-start.8 = (bf16[800,256]{1,0:T(8,128)(2,1)S(1)}, bf16[800,256]{1,0:T(8,128)(2,1)S(1)}, u32[]{:S(2)}, u32[]{:S(2)}) collective-permute-start(bf16[800,256]{1,0:T(8,128)(2,1)S(1)} %get-tuple-element.39), channel_id=1, source_target_pairs={{0,1},{1,0},{2,3},{3,2},{4,5},{5,4},{6,7},{7,6},{8,9},{9,8},{10,11... | collective-permute-start | bytes 1228808 | tf_op jit(solution)/shard_map/ppermute | solution.py:468
  42.2 1.7 %collective-permute-start.9 = (bf16[640,256]{1,0:T(8,128)(2,1)S(1)}, bf16[640,256]{1,0:T(8,128)(2,1)S(1)}, u32[]{:S(2)}, u32[]{:S(2)}) collective-permute-start(bf16[640,256]{1,0:T(8,128)(2,1)S(1)} %get-tuple-element.40), channel_id=1, source_target_pairs={{0,1},{1,0},{2,3},{3,2},{4,5},{5,4},{6,7},{7,6},{8,9},{9,8},{10,11... | collective-permute-start | bytes 983048 | tf_op jit(solution)/shard_map/ppermute | solution.py:470

commit v7 on v6

--- a/solution.py
+++ b/solution.py
@@ -159,14 +159,20 @@
     return jnp.dot(conv[...], mix[...], preferred_element_type=jnp.float32)
 
 
-def first_half_kernel(*refs, plan, ordered, block_width, rows):
-    halves, refs = refs[: len(plan["spans"])], refs[len(plan["spans"]) + ordered :]
-    edge_filter, conv_local, mix, residual, result, window, conv = refs
+def window_kernel(half, window):
+    cells = half.shape[0]
+    window[:cells, :] = half[...]
+    window[cells:, :] = half[: window.shape[0] - cells, :]
+
+
+def first_half_kernel(
+    window, edge_filter, conv_local, mix, residual, result, conv, *, plan, block_width, rows
+):
     first, places = plan["first"], plan["places"]
 
     def body(depth):
         mixed = halo_mix(
-            depth, first, places, block_width, halves, plan["spans"], edge_filter, conv_local, mix, window, conv
+            depth, first, places, block_width, (), (), edge_filter, conv_local, mix, window, conv
         )
         result[...] = residual[first * block_width : (first + places) * block_width, :] + mixed
 
@@ -411,20 +417,28 @@
 
     partials = []
     first_plans = plans_of(FIRST_CUTS, lon_blocks, block_width, block_most)
-    for plan in first_plans:
-        done = partials[-1:]
-        partials.append(pl.pallas_call(
-            functools.partial(
-                first_half_kernel, plan=plan, ordered=len(done), block_width=block_width, rows=local_rows * bands
-            ),
-            out_shape=jax.ShapeDtypeStruct((plan["places"] * block_width, channels), jnp.float32),
-            in_specs=vmem(len(plan["pieces"])) + anywhere(len(done)) + vmem(4),
-            out_specs=vmem(1)[0],
-            scratch_shapes=halo_scratch(plan),
-            compiler_params=limit(10),
-            cost_estimate=cost(6 * 10**10),
-            name="edge_tap_first_half",
-        )(*[halo_other[piece] for piece in plan["pieces"]], *done, edge_filter, conv_other, mix_other, residual))
+    window, conv = halo_scratch(first_plans[0])
+    halo_window = pl.pallas_call(
+        window_kernel,
+        out_shape=jax.ShapeDtypeStruct(window.shape, narrow),
+        in_specs=vmem(1),
+        out_specs=vmem(1)[0],
+        compiler_params=limit(4),
+        cost_estimate=cost(6 * 10**10),
+        name="halo_window",
+    )(halo_other[0])
+    partials.append(pl.pallas_call(
+        functools.partial(
+            first_half_kernel, plan=first_plans[0], block_width=block_width, rows=local_rows * bands
+        ),
+        out_shape=jax.ShapeDtypeStruct((cells, channels), jnp.float32),
+        in_specs=vmem(5),
+        out_specs=vmem(1)[0],
+        scratch_shapes=[conv],
+        compiler_params=limit(10),
+        cost_estimate=cost(),
+        name="edge_tap_first_half",
+    )(halo_window, edge_filter, conv_other, mix_other, residual))
 
     sends, done = {}, partials[-1:]
     last_plans = plans_of(LAST_CUTS, lon_blocks, block_width, block_most)

time: 45.1 us -> 45.1 us (level)
    pallas_call x1 -> x2, Pallas kernels: 4.16 us -> 4.22 us  [the longest x1 4.16 us: per_device(): pl.pallas_call(functools.partial(first_half_kernel, plan=first_plans[0],...]
where the time goes in v7:
time: 45.1 us; the launch traced here: 45 us
  Pallas kernels  25.1 us (56%)
  starting transfers between devices  16.9 us (37%)
  waiting for transfers between devices  2.64 us (6%)
    pallas_call x1, Pallas kernels, per_device(): pl.pallas_call(functools.partial(local_kernel, block_most=block_most, **s...  9.81 us
    ppermute x1, starting transfers between devices, per_device(): early = lax.ppermute(sends[0], 'chan', swap)  9 us
    pallas_call x3, Pallas kernels, per_device(): pl.pallas_call(functools.partial(tail_kernel, plan=plan, ordered=len(done...  7.88 us
    ppermute x1, starting transfers between devices, per_device(): up_other = lax.ppermute(up_weight, 'chan', swap)  4.32 us
    pallas_call x1, Pallas kernels, per_device(): pl.pallas_call(functools.partial(first_half_kernel, plan=first_plans[0],...  4.16 us
    ppermute x3, starting transfers between devices, per_device(): halo_own = [lax.ppermute(piece, ('lat', 'chan'), pairs) for piece in relay]  2.03 us
    ppermute x1, waiting for transfers between devices, per_device(): up_other = lax.ppermute(up_weight, 'chan', swap)  1.45 us
    pallas_call x1, Pallas kernels, per_device(): pl.pallas_call(functools.partial(place_kernel, firsts=firsts[:-1], **size...  1.16 us
  transfers between devices with their start and end apart: 10, of which 3 were waited for; matrix products, arithmetic and copies ran while one was open for 0% of the time, Pallas kernels for 54%

profile of v7, /device:TPU:0, one launch (start us, length us, event | category | flops | bytes accessed | tf_op | source)
XLA Modules:
  0.0 45.0 jit_solution(5074134623686933528)
XLA Ops:
  0.0 0.5 %collective-permute-start = (bf16[2,1440,256]{2,1,0:T(8,128)(2,1)}, bf16[2,1440,256]{2,1,0:T(8,128)(2,1)S(1)}, u32[]{:S(2)}, u32[]{:S(2)}) collective-permute-start(bf16[2,1440,256]{2,1,0:T(8,128)(2,1)} %rows.1), channel_id=1, source_target_pairs={{0,1},{1,0},{2,3},{3,2},{4,5},{5,4},{6,7},{7,6},{8,9},{9,8},{10,11... | collective-permute-start | bytes 4423688 | tf_op jit(solution)/shard_map/ppermute | solution.py:365
  0.5 0.1 collective-permute-start.1
  0.6 1.1 %edge_row.1 = bf16[1440,256]{1,0:T(8,128)(2,1)S(1)} custom-call(bf16[2,1440,256]{2,1,0:T(8,128)(2,1)} %rows.1), custom_call_target="tpu_custom_call" | custom-call | flops 1000 | bytes 1000 | tf_op jit(solution)/shard_map/edge_row/pallas_call | solution.py:354
  1.8 0.7 %collective-permute-start.7 = (bf16[1440,256]{1,0:T(8,128)(2,1)S(1)}, bf16[1440,256]{1,0:T(8,128)(2,1)S(1)}, u32[]{:S(2)}, u32[]{:S(2)}) collective-permute-start(bf16[1440,256]{1,0:T(8,128)(2,1)S(1)} %edge_row.1), channel_id=1, source_target_pairs={{1,2},{2,1},{3,4},{4,3},{5,6},{6,5},{7,8},{8,7},{9,10},{10,9},{11,... | collective-permute-start | bytes 2211848 | tf_op jit(solution)/shard_map/ppermute | solution.py:364
  2.5 4.3 %collective-permute-start.2 = (bf16[512,512]{1,0:T(8,128)(2,1)S(1)}, bf16[512,512]{1,0:T(8,128)(2,1)S(1)}, u32[]{:S(2)}, u32[]{:S(2)}) collective-permute-start(bf16[512,512]{1,0:T(8,128)(2,1)S(1)} %copy-done.2), channel_id=1, source_target_pairs={{0,1},{1,0},{2,3},{3,2},{4,5},{5,4},{6,7},{7,6},{8,9},{9,8},{10,11... | collective-permute-start | bytes 1572872 | tf_op jit(solution)/shard_map/ppermute | solution.py:367
  6.8 0.1 collective-permute-start.3
  6.9 1.4 %collective-permute-done.2.refs_3_ = bf16[512,512]{1,0:T(8,128)(2,1)S(1)} collective-permute-done((bf16[512,512]{1,0:T(8,128)(2,1)S(1)}, bf16[512,512]{1,0:T(8,128)(2,1)S(1)}, u32[]{:S(2)}, u32[]{:S(2)}) %collective-permute-start.2) | collective-permute-done | bytes 524320 | tf_op jit(solution)/shard_map/ppermute | solution.py:367
  8.3 0.7 %collective-permute-done.3.refs_5_ = bf16[512,512]{1,0:T(8,128)(2,1)S(1)} collective-permute-done((bf16[512,512]{1,0:T(8,128)(2,1)S(1)}, bf16[512,512]{1,0:T(8,128)(2,1)S(1)}, u32[]{:S(2)}, u32[]{:S(2)}) %collective-permute-start.3) | collective-permute-done | bytes 524320 | tf_op jit(solution)/shard_map/ppermute | solution.py:368
  9.1 0.0 collective-permute-done.other
  9.1 9.8 %local_taps.1 = (f32[18,400,256]{2,1,0:T(8,128)S(1)}, f32[18,400,256]{2,1,0:T(8,128)S(1)}, f32[1440,512]{1,0:T(8,128)S(1)}, bf16[400,320]{1,0:T(8,128)(2,1)S(1)}...) custom-call(s32[2,3]{1,0:T(2,128)S(1)} %copy-done, ...), custom_call_target="tpu_custom_call" | custom-call | flops 1000 | bytes 1000 | tf_op jit(solution)/shard_map/local_taps/pallas_call | solution.py:379
  18.9 0.1 relay_rows.1
  19.0 0.7 %collective-permute-start.4 = (bf16[640,256]{1,0:T(8,128)(2,1)S(1)}, bf16[640,256]{1,0:T(8,128)(2,1)S(1)}, u32[]{:S(2)}, u32[]{:S(2)}) collective-permute-start(bf16[640,256]{1,0:T(8,128)(2,1)S(1)} %get-tuple-element.25), channel_id=1, source_target_pairs={{1,2},{2,1},{3,4},{4,3},{5,6},{6,5},{7,8},{8,7},{9,10},{10,9},{11,... | collective-permute-start | bytes 983048 | tf_op jit(solution)/shard_map/ppermute | solution.py:410
  19.7 0.7 %collective-permute-start.5 = (bf16[400,256]{1,0:T(8,128)(2,1)S(1)}, bf16[400,256]{1,0:T(8,128)(2,1)S(1)}, u32[]{:S(2)}, u32[]{:S(2)}) collective-permute-start(bf16[400,256]{1,0:T(8,128)(2,1)S(1)} %get-tuple-element.26), channel_id=1, source_target_pairs={{1,2},{2,1},{3,4},{4,3},{5,6},{6,5},{7,8},{8,7},{9,10},{10,9},{11,... | collective-permute-start | bytes 614408 | tf_op jit(solution)/shard_map/ppermute | solution.py:410
  20.4 0.7 %collective-permute-start.6 = (bf16[400,256]{1,0:T(8,128)(2,1)S(1)}, bf16[400,256]{1,0:T(8,128)(2,1)S(1)}, u32[]{:S(2)}, u32[]{:S(2)}) collective-permute-start(bf16[400,256]{1,0:T(8,128)(2,1)S(1)} %get-tuple-element.27), channel_id=1, source_target_pairs={{1,2},{2,1},{3,4},{4,3},{5,6},{6,5},{7,8},{8,7},{9,10},{10,9},{11,... | collective-permute-start | bytes 614408 | tf_op jit(solution)/shard_map/ppermute | solution.py:410
  21.1 0.1 halo_window.1.window
  21.1 4.2 %edge_tap_first_half.1.refs_1_.refs_2_.refs_4_ = f32[1440,512]{1,0:T(8,128)S(1)} custom-call(bf16[1680,256]{1,0:T(8,128)(2,1)S(1)} %halo_window.1.window, bf16[400,320]{1,0:T(8,128)(2,1)S(1)} %get-tuple-element.24.ordered.edge_filter.refs_3_.refs_5_, f32[18,400,256]{2,1,0:T(8,128)S(1)} %get-tuple-element.28.conv_local, ...), custom_call_target="tpu_custom_call" | custom-call | flops 1000 | bytes 1000 | tf_op jit(solution)/shard_map/edge_tap_first_half/pallas_call | solution.py:430
  25.3 2.4 %edge_tap_and_feed.3 = (bf16[1440,256]{1,0:T(8,128)(2,1)S(1)}, bf16[800,256]{1,0:T(8,128)(2,1)S(1)}) custom-call(bf16[640,256]{1,0:T(8,128)(2,1)S(1)} %collective-permute-done.4.refs_0_, f32[1440,512]{1,0:T(8,128)S(1)} %edge_tap_first_half.1.refs_1_.refs_2_.refs_4_, f32[1440,512]{1,0:T(8,128)S(1)} %edge_tap_first_half.1.refs_1_.refs_2_.refs_4_, ...), custom_call_target="tpu_custom_call" | custom-call | flops 1000 | bytes 1000 | tf_op jit(solution)/shard_map/edge_tap_and_feed/pallas_call | solution.py:462
  27.7 2.2 %edge_tap_and_feed.4 = (bf16[1440,256]{1,0:T(8,128)(2,1)S(1)}, bf16[800,256]{1,0:T(8,128)(2,1)S(1)}) custom-call(bf16[640,256]{1,0:T(8,128)(2,1)S(1)} %collective-permute-done.4.refs_0_, bf16[400,256]{1,0:T(8,128)(2,1)S(1)} %collective-permute-done.5.refs_1_, ...), custom_call_target="tpu_custom_call", output_to_operand_aliasing={{0}: (2, {}), {1}: (3, {})} | custom-call | flops 1000 | bytes 1000 | tf_op jit(solution)/shard_map/edge_tap_and_feed/pallas_call | solution.py:462
  29.9 9.0 %collective-permute-start.8 = (bf16[800,256]{1,0:T(8,128)(2,1)S(1)}, bf16[800,256]{1,0:T(8,128)(2,1)S(1)}, u32[]{:S(2)}, u32[]{:S(2)}) collective-permute-start(bf16[800,256]{1,0:T(8,128)(2,1)S(1)} %get-tuple-element.39), channel_id=1, source_target_pairs={{0,1},{1,0},{2,3},{3,2},{4,5},{5,4},{6,7},{7,6},{8,9},{9,8},{10,11... | collective-permute-start | bytes 1228808 | tf_op jit(solution)/shard_map/ppermute | solution.py:482
  38.9 3.3 %edge_tap_and_feed.5 = (bf16[1440,256]{1,0:T(8,128)(2,1)S(1)}, bf16[640,256]{1,0:T(8,128)(2,1)S(1)}) custom-call(bf16[640,256]{1,0:T(8,128)(2,1)S(1)} %collective-permute-done.4.refs_0_, bf16[400,256]{1,0:T(8,128)(2,1)S(1)} %collective-permute-done.5.refs_1_, bf16[400,256]{1,0:T(8,128)(2,1)S(1)} %collective-permute-done.6.refs_2_, ...), custom_call_target="tpu_custom_call", output_to_operand_aliasing={{0}: (3, {})} | custom-call | flops 10000000000 | bytes 1000 | tf_op jit(solution)/shard_map/edge_tap_and_feed/pallas_call | solution.py:462
  42.2 0.1 collective-permute-start.9
  42.3 1.2 %place_rows.1.before = bf16[2,1440,256]{2,1,0:T(8,128)(2,1)} custom-call(s32[2,3]{1,0:T(2,128)S(1)} %copy-done, bf16[1440,256]{1,0:T(8,128)(2,1)S(1)} %get-tuple-element.41.keep, bf16[800,256]{1,0:T(8,128)(2,1)S(1)} %collective-permute-done.8.refs_0_), custom_call_target="tpu_custom_call" | custom-call | flops 1000 | bytes 1000 | tf_op jit(solution)/shard_map/place_rows/pallas_call | solution.py:486
  43.5 0.4 collective-permute-done.9.source
  43.9 0.9 %place_last_rows.1 = bf16[2,1440,256]{2,1,0:T(8,128)(2,1)} custom-call(s32[2,3]{1,0:T(2,128)S(1)} %copy-done, bf16[640,256]{1,0:T(8,128)(2,1)S(1)} %collective-permute-done.9.source, bf16[2,1440,256]{2,1,0:T(8,128)(2,1)} %place_rows.1.before), custom_call_target="tpu_custom_call", output_to_operand_aliasing={{}: (2, {})} | custom-call | flops 1000 | bytes 1000 | tf_op jit(solution)/shard_map/place_last_rows/pallas_call | solution.py:497
  (14 shorter events, 0.0 us)
Async XLA Ops:
  0.0 2.5 %copy-start.2 = (bf16[512,512]{1,0:T(8,128)(2,1)S(1)}, bf16[512,512]{1,0:T(8,128)(2,1)}, u32[]{:S(2)}) copy-start(bf16[512,512]{1,0:T(8,128)(2,1)} %refs_2_.1) | copy-start | bytes 1572868
  0.0 6.8 %copy-start.3 = (bf16[512,512]{1,0:T(8,128)(2,1)S(1)}, bf16[512,512]{1,0:T(8,128)(2,1)}, u32[]{:S(2)}) copy-start(bf16[512,512]{1,0:T(8,128)(2,1)} %refs_4_.1) | copy-start | bytes 1572868
  0.0 9.1 %copy-start = (s32[2,3]{1,0:T(2,128)S(1)}, s32[2,3]{1,0:T(2,128)}, u32[]{:S(2)}) copy-start(s32[2,3]{1,0:T(2,128)} %block_start.5) | copy-start | bytes 76
  0.0 9.1 %copy-start.1 = (s32[2,3]{1,0:T(2,128)S(1)}, s32[2,3]{1,0:T(2,128)}, u32[]{:S(2)}) copy-start(s32[2,3]{1,0:T(2,128)} %block_count.1) | copy-start | bytes 76
  0.0 9.1 %collective-permute-start = (bf16[2,1440,256]{2,1,0:T(8,128)(2,1)}, bf16[2,1440,256]{2,1,0:T(8,128)(2,1)S(1)}, u32[]{:S(2)}, u32[]{:S(2)}) collective-permute-start(bf16[2,1440,256]{2,1,0:T(8,128)(2,1)} %rows.1), channel_id=1, source_target_pairs={{0,1},{1,0},{2,3},{3,2},{4,5},{5,4},{6,7},{7,6},{8,9},{9,8},{10,11... | collective-permute-start | bytes 4423688 | tf_op jit(solution)/shard_map/ppermute | solution.py:365
  0.5 8.6 %collective-permute-start.1 = (bf16[5,256,512]{2,1,0:T(8,128)(2,1)}, bf16[5,256,512]{2,1,0:T(8,128)(2,1)S(1)}, u32[]{:S(2)}, u32[]{:S(2)}) collective-permute-start(bf16[5,256,512]{2,1,0:T(8,128)(2,1)} %param.11), channel_id=1, source_target_pairs={{0,1},{1,0},{2,3},{3,2},{4,5},{5,4},{6,7},{7,6},{8,9},{9,8},{10,11... | collective-permute-start | bytes 3932168 | tf_op jit(solution)/shard_map/ppermute | solution.py:366
  1.8 19.3 %collective-permute-start.7 = (bf16[1440,256]{1,0:T(8,128)(2,1)S(1)}, bf16[1440,256]{1,0:T(8,128)(2,1)S(1)}, u32[]{:S(2)}, u32[]{:S(2)}) collective-permute-start(bf16[1440,256]{1,0:T(8,128)(2,1)S(1)} %edge_row.1), channel_id=1, source_target_pairs={{1,2},{2,1},{3,4},{4,3},{5,6},{6,5},{7,8},{8,7},{9,10},{10,9},{11,... | collective-permute-start | bytes 2211848 | tf_op jit(solution)/shard_map/ppermute | solution.py:364
  2.5 5.9 %collective-permute-start.2 = (bf16[512,512]{1,0:T(8,128)(2,1)S(1)}, bf16[512,512]{1,0:T(8,128)(2,1)S(1)}, u32[]{:S(2)}, u32[]{:S(2)}) collective-permute-start(bf16[512,512]{1,0:T(8,128)(2,1)S(1)} %copy-done.2), channel_id=1, source_target_pairs={{0,1},{1,0},{2,3},{3,2},{4,5},{5,4},{6,7},{7,6},{8,9},{9,8},{10,11... | collective-permute-start | bytes 1572872 | tf_op jit(solution)/shard_map/ppermute | solution.py:367
  6.8 2.3 %collective-permute-start.3 = (bf16[512,512]{1,0:T(8,128)(2,1)S(1)}, bf16[512,512]{1,0:T(8,128)(2,1)S(1)}, u32[]{:S(2)}, u32[]{:S(2)}) collective-permute-start(bf16[512,512]{1,0:T(8,128)(2,1)S(1)} %copy-done.3), channel_id=1, source_target_pairs={{0,1},{1,0},{2,3},{3,2},{4,5},{5,4},{6,7},{7,6},{8,9},{9,8},{10,11... | collective-permute-start | bytes 1572872 | tf_op jit(solution)/shard_map/ppermute | solution.py:368
  19.0 6.3 %collective-permute-start.4 = (bf16[640,256]{1,0:T(8,128)(2,1)S(1)}, bf16[640,256]{1,0:T(8,128)(2,1)S(1)}, u32[]{:S(2)}, u32[]{:S(2)}) collective-permute-start(bf16[640,256]{1,0:T(8,128)(2,1)S(1)} %get-tuple-element.25), channel_id=1, source_target_pairs={{1,2},{2,1},{3,4},{4,3},{5,6},{6,5},{7,8},{8,7},{9,10},{10,9},{11,... | collective-permute-start | bytes 983048 | tf_op jit(solution)/shard_map/ppermute | solution.py:410
  19.7 8.0 %collective-permute-start.5 = (bf16[400,256]{1,0:T(8,128)(2,1)S(1)}, bf16[400,256]{1,0:T(8,128)(2,1)S(1)}, u32[]{:S(2)}, u32[]{:S(2)}) collective-permute-start(bf16[400,256]{1,0:T(8,128)(2,1)S(1)} %get-tuple-element.26), channel_id=1, source_target_pairs={{1,2},{2,1},{3,4},{4,3},{5,6},{6,5},{7,8},{8,7},{9,10},{10,9},{11,... | collective-permute-start | bytes 614408 | tf_op jit(solution)/shard_map/ppermute | solution.py:410
  20.4 18.5 %collective-permute-start.6 = (bf16[400,256]{1,0:T(8,128)(2,1)S(1)}, bf16[400,256]{1,0:T(8,128)(2,1)S(1)}, u32[]{:S(2)}, u32[]{:S(2)}) collective-permute-start(bf16[400,256]{1,0:T(8,128)(2,1)S(1)} %get-tuple-element.27), channel_id=1, source_target_pairs={{1,2},{2,1},{3,4},{4,3},{5,6},{6,5},{7,8},{8,7},{9,10},{10,9},{11,... | collective-permute-start | bytes 614408 | tf_op jit(solution)/shard_map/ppermute | solution.py:410
  29.9 12.3 %collective-permute-start.8 = (bf16[800,256]{1,0:T(8,128)(2,1)S(1)}, bf16[800,256]{1,0:T(8,128)(2,1)S(1)}, u32[]{:S(2)}, u32[]{:S(2)}) collective-permute-start(bf16[800,256]{1,0:T(8,128)(2,1)S(1)} %get-tuple-element.39), channel_id=1, source_target_pairs={{0,1},{1,0},{2,3},{3,2},{4,5},{5,4},{6,7},{7,6},{8,9},{9,8},{10,11... | collective-permute-start | bytes 1228808 | tf_op jit(solution)/shard_map/ppermute | solution.py:482
  42.2 1.7 %collective-permute-start.9 = (bf16[640,256]{1,0:T(8,128)(2,1)S(1)}, bf16[640,256]{1,0:T(8,128)(2,1)S(1)}, u32[]{:S(2)}, u32[]{:S(2)}) collective-permute-start(bf16[640,256]{1,0:T(8,128)(2,1)S(1)} %get-tuple-element.40), channel_id=1, source_target_pairs={{0,1},{1,0},{2,3},{3,2},{4,5},{5,4},{6,7},{7,6},{8,9},{9,8},{10,11... | collective-permute-start | bytes 983048 | tf_op jit(solution)/shard_map/ppermute | solution.py:484
